TPU v7x, 32 devices: a whole 2x2x4 slice. The times are simulated.
32 devices in a mesh: dp: 4 (over y, core), ctx: 8 (over z, x).
Axes of the slice: x: 2, y: 2, z: 4, core: 2. Of those that a mesh axis runs over, the one named last changes fastest.
Arguments:
- query_act: bfloat16 [4096, 4096], P(('dp', 'ctx')), may hold values from -6 to 6
- key_act: bfloat16 [4096, 4096], P(('dp', 'ctx')), may hold values from -6 to 6
- value_act: bfloat16 [4096, 4096], P(('dp', 'ctx')), may hold values from -6 to 6
- out_grad: bfloat16 [4096, 4096], P(('dp', 'ctx')), may hold values from -6 to 6
- filter_taps: float32 [4096, 128], P('ctx'), may hold values from -0.5 to 0.5
- doc_ids: int32 [4096], replicated, may hold values from 0 to 7, as said below
Outputs:
- query_grad: bfloat16 [4096, 4096], P(('dp', 'ctx'))
- key_grad: bfloat16 [4096, 4096], P(('dp', 'ctx'))
- value_grad: bfloat16 [4096, 4096], P(('dp', 'ctx'))
- filter_grad: float32 [4096, 128], P('ctx')
Inputs may be any that keep to these rules, and one draw needn't show every extreme that they name: `doc_ids`: the document numbers start at 0, never fall, and rise by one at each boundary; the window holds 8 documents, each of at least 256 positions.
All inputs are finite; a program needn't handle non-finite values.
Results may differ from a plain program's by a relative error of at most 0.0064.
Values may be sent and summed in bfloat16 or wider, within the bound.
No kernel may reach another device: no remote copies, remote signals or barrier semaphores. Data moves between devices by JAX's collectives and lax.ppermute only.
A program may use at most 320 MiB of HBM per device.

v0:
```python
import math

import jax
import jax.numpy as jnp
from jax import lax
from jax.sharding import PartitionSpec as P


def from_behind(value, axis, steps):
    count = lax.axis_size(axis)
    leading, last = (max(0, -steps), min(count, count - steps))
    return lax.ppermute(value, axis, [(source, source + steps) for source in range(leading, last)])


def build_toeplitz(tap_rows):
    chan_count, tap_count = tap_rows.shape
    zero_col = jnp.zeros((chan_count, 1), tap_rows.dtype)
    tail_cols = jnp.zeros((chan_count, tap_count), tap_rows.dtype)
    pattern = jnp.concatenate([zero_col, tap_rows[:, ::-1], tail_cols], axis=1)
    tiled = jnp.tile(pattern, (1, tap_count))[:, : tap_count * 2 * tap_count]
    return tiled.reshape(chan_count, tap_count, 2 * tap_count)


def lag_sums(block):
    chan_count, tap_count, span = block.shape
    flat = block.reshape(chan_count, tap_count * span)
    flat = jnp.pad(flat, ((0, 0), (0, tap_count)))
    skewed = flat.reshape(chan_count, tap_count, span + 1)
    summed = jnp.sum(skewed[:, :, 1 : tap_count + 1], axis=1)
    return summed[:, ::-1]


def mix_block(kv_ext, g_ext, seg_ext, tap_rows):
    chan_count, tap_count = tap_rows.shape
    block_count = kv_ext.shape[1] // tap_count - 1
    kv_blocks = kv_ext.reshape(chan_count, block_count + 1, tap_count)
    windows = jnp.concatenate([kv_blocks[:, :-1], kv_blocks[:, 1:]], axis=2)
    seg_blocks = seg_ext.reshape(block_count + 2, tap_count)
    seg_win = jnp.concatenate([seg_blocks[:-1], seg_blocks[1:]], axis=1)
    same = (seg_win == seg_win[:, -1:]).astype(jnp.bfloat16)
    other = (seg_win != seg_win[:, -1:]).astype(jnp.bfloat16)
    rows_same = same[:, tap_count:]
    rows_other = other[:, tap_count:]
    toeplitz = build_toeplitz(tap_rows)
    kv_same = same[:block_count] * windows
    kv_other = other[:block_count] * windows
    z_same = jnp.einsum("cij,cbj->cbi", toeplitz, kv_same, preferred_element_type=jnp.float32)
    z_other = jnp.einsum("cij,cbj->cbi", toeplitz, kv_other, preferred_element_type=jnp.float32)
    mixed = rows_same[:block_count] * z_same + rows_other[:block_count] * z_other
    g_blocks = g_ext.reshape(chan_count, block_count + 1, tap_count)
    g_same = rows_same * g_blocks
    g_other = rows_other * g_blocks
    d_same = jnp.einsum("cij,cbi->cbj", toeplitz, g_same, preferred_element_type=jnp.float32)
    d_other = jnp.einsum("cij,cbi->cbj", toeplitz, g_other, preferred_element_type=jnp.float32)
    d_win = same * d_same + other * d_other
    back = d_win[:, :block_count, tap_count:] + d_win[:, 1:, :tap_count]
    outer = jnp.einsum(
        "cbi,cbj->cij", g_same[:, :block_count], kv_same, preferred_element_type=jnp.float32
    )
    outer = outer + jnp.einsum(
        "cbi,cbj->cij", g_other[:, :block_count], kv_other, preferred_element_type=jnp.float32
    )
    row_count = block_count * tap_count
    return (
        mixed.reshape(chan_count, row_count),
        back.reshape(chan_count, row_count),
        lag_sums(outer),
    )


def shards(query_act, key_act, value_act, out_grad, filter_taps, doc_ids):
    tap_count = filter_taps.shape[1]
    product = (key_act.astype(jnp.float32) * value_act.astype(jnp.float32)).astype(jnp.bfloat16)
    gated = (query_act.astype(jnp.float32) * out_grad.astype(jnp.float32)).astype(jnp.bfloat16)
    taps_local = filter_taps.astype(jnp.bfloat16)
    scale = 1.0 / math.sqrt(doc_ids.shape[0])
    seg_pad = jnp.pad(doc_ids, (tap_count, tap_count))
    kv_chan, g_chan = (
        lax.all_to_all(product, "ctx", split_axis=1, concat_axis=0, tiled=True),
        lax.all_to_all(gated, "ctx", split_axis=1, concat_axis=0, tiled=True),
    )
    group_rows = kv_chan.shape[0]
    kv_major = kv_chan.T
    g_major = g_chan.T
    prior = from_behind(kv_major[:, group_rows - tap_count :], "dp", 1)
    after = from_behind(g_major[:, :tap_count], "dp", -1)
    kv_ext = jnp.concatenate([prior, kv_major], 1)
    g_ext = jnp.concatenate([g_major, after], 1)
    start = lax.axis_index("dp") * group_rows
    seg_ext = lax.dynamic_slice_in_dim(seg_pad, start, group_rows + 2 * tap_count)
    mixed, back, partial_value = mix_block(kv_ext, g_ext, seg_ext, taps_local)
    mixed_tok, back_tok = (
        lax.all_to_all(
            mixed.T.astype(jnp.bfloat16), "ctx", split_axis=0, concat_axis=1, tiled=True
        ),
        lax.all_to_all(back.T.astype(jnp.bfloat16), "ctx", split_axis=0, concat_axis=1, tiled=True),
    )
    filter_total = lax.psum(partial_value, "dp")
    mixed_f = mixed_tok.astype(jnp.float32)
    back_f = back_tok.astype(jnp.float32)
    query_grad = (out_grad.astype(jnp.float32) * mixed_f).astype(jnp.bfloat16)
    key_grad = (back_f * value_act.astype(jnp.float32)).astype(jnp.bfloat16)
    value_grad = (back_f * key_act.astype(jnp.float32)).astype(jnp.bfloat16)
    return (query_grad, key_grad, value_grad, filter_total * scale)


def solution(mesh):
    in_specs = (
        P(("dp", "ctx"), None),
        P(("dp", "ctx"), None),
        P(("dp", "ctx"), None),
        P(("dp", "ctx"), None),
        P("ctx", None),
        P(),
    )
    out_specs = (
        P(("dp", "ctx"), None),
        P(("dp", "ctx"), None),
        P(("dp", "ctx"), None),
        P("ctx", None),
    )
    return jax.shard_map(shards, mesh=mesh, in_specs=in_specs, out_specs=out_specs, check_vma=False)
```

profile of v0, /device:TPU:0, one launch (start us, length us, event | category | flops | bytes accessed | tf_op | source)
XLA Modules:
  0.0 633.7 jit_solution(10825425501990091766)
XLA Ops:
  10.8 7.3 %all-to-all-start.2 = ((bf16[128,8,512]{0,2,1:T(8,128)(2,1)}), bf16[128,8,512]{0,2,1:T(8,128)(2,1)S(1)}, u32[]{:S(2)}, u32[]{:S(2)}) async-start(bf16[128,8,512]{0,2,1:T(8,128)(2,1)} %bitcast.12), calls=%async_computation.2 | async-start | bytes 2097152 | tf_op jit(solution)/shard_map/all_to_all | solution.py:80
  19.0 24.9 %all-to-all-done.2 = bf16[128,8,512]{0,2,1:T(8,128)(2,1)S(1)} async-done(((bf16[128,8,512]{0,2,1:T(8,128)(2,1)}), bf16[128,8,512]{0,2,1:T(8,128)(2,1)S(1)}, u32[]{:S(2)}, u32[]{:S(2)}) %all-to-all-start.2) | async-done | bytes 1048608 | tf_op jit(solution)/shard_map/all_to_all | solution.py:80
  46.0 11.5 %tile.4 = bf16[512,128,257]{0,2,1:T(8,128)(2,1)} broadcast(bf16[512,257]{0,1:T(8,128)(2,1)S(1)} %copy.72), dimensions={0,2} | broadcast | bytes 33948672 | tf_op jit(solution)/shard_map/tile | solution.py:20
  57.6 30.6 %tile.10 = bf16[512,32896]{0,1:T(8,128)(2,1)} reshape(bf16[512,128,257]{0,2,1:T(8,128)(2,1)} %tile.4) | data formatting | bytes 67371008 | tf_op jit(solution)/shard_map/tile | solution.py:20
  88.1 22.9 %slice.109 = bf16[512,32768]{0,1:T(8,128)(2,1)} slice(bf16[512,32896]{0,1:T(8,128)(2,1)} %tile.10), slice={[0:512], [0:32768]} | slice | bytes 67108864 | tf_op jit(solution)/shard_map/slice | solution.py:20
  111.0 45.6 %copy.90 = bf16[512,128,256]{2,1,0:T(8,128)(2,1)} copy(bf16[512,128,256]{0,2,1:T(8,128)(2,1)} %bitcast.61) | data formatting | bytes 67108864 | tf_op jit(solution)/shard_map/reshape | solution.py:21
  161.6 17.9 %fusion.17 = f32[512,9,256]{2,1,0:T(8,128)} fusion(bf16[512,9,128]{2,1,0:T(8,128)(2,1)S(1)} %get-tuple-element.21, bf16[512,128,256]{2,1,0:T(8,128)(2,1)} %copy.90), kind=kOutput, calls=%fused_computation.45 | convolution fusion | flops 301989888 | bytes 39452672 | tf_op jit(solution)/shard_map/cij,cbi->cbj/dot_general | solution.py:53
  179.5 18.8 %multiply_add_fusion = f32[512,9,256]{2,1,0:T(8,128)} fusion(f32[512,9,256]{2,1,0:T(8,128)} %fusion.17, f32[9,256]{1,0:T(8,128)S(1)} %get-tuple-element.18, f32[9,256]{1,0:T(8,128)S(1)} %get-tuple-element.29, bf16[512,9,128]{2,1,0:T(8,128)(2,1)S(1)} %get-tuple-element.20, bf16[512,128,256]{2,1,0:T(8,128)(2,1)} %copy.90), kind=kOutput, calls=%fused_computation.2 | convolution fusion | flops 305528832 | bytes 44189696 | tf_op jit(solution)/shard_map/cij,cbi->cbj/dot_general | solution.py:54
  202.5 3.6 all-to-all-start.3
  208.4 25.3 %all-to-all-done.3 = bf16[8,128,512]{1,2,0:T(8,128)(2,1)S(1)} async-done(((bf16[8,128,512]{1,2,0:T(8,128)(2,1)}), bf16[8,128,512]{1,2,0:T(8,128)(2,1)S(1)}, u32[]{:S(2)}, u32[]{:S(2)}) %all-to-all-start.3) | async-done | bytes 1048608 | tf_op jit(solution)/shard_map/all_to_all | solution.py:96
  236.0 3.6 all-to-all-start
  239.6 26.2 %all-to-all-done = bf16[128,8,512]{0,2,1:T(8,128)(2,1)S(1)} async-done(((bf16[128,8,512]{0,2,1:T(8,128)(2,1)}), bf16[128,8,512]{0,2,1:T(8,128)(2,1)S(1)}, u32[]{:S(2)}, u32[]{:S(2)}) %all-to-all-start) | async-done | bytes 1048608 | tf_op jit(solution)/shard_map/all_to_all | solution.py:79
  271.4 3.3 copy.74
  274.7 16.0 %fusion.16 = f32[512,8,128]{2,1,0:T(8,128)} fusion(bf16[512,8,256]{2,1,0:T(8,128)(2,1)S(1)} %copy.74, bf16[512,128,256]{2,1,0:T(8,128)(2,1)} %copy.90), kind=kOutput, calls=%fused_computation.44 | convolution fusion | flops 268435456 | bytes 37748736 | tf_op jit(solution)/shard_map/cij,cbj->cbi/dot_general | solution.py:47
  290.7 23.9 %fusion.9 = f32[512,128,256]{2,1,0:T(8,128)} fusion(bf16[512,8,256]{2,1,0:T(8,128)(2,1)S(1)} %copy.74, bf16[512,9,128]{2,1,0:T(8,128)(2,1)S(1)} %copy-done.2), kind=kOutput, calls=%fused_computation.25 | convolution fusion | flops 268435456 | bytes 70254592 | tf_op jit(solution)/shard_map/cbi,cbj->cij/dot_general | solution.py:57
  314.6 3.3 copy.75
  318.0 14.7 %add_convert_fusion = bf16[512,8,128]{2,1,0:T(8,128)(2,1)S(1)} fusion(f32[512,8,128]{2,1,0:T(8,128)} %fusion.16, bf16[512,8,256]{2,1,0:T(8,128)(2,1)S(1)} %copy.75, bf16[512,128,256]{2,1,0:T(8,128)(2,1)} %copy.90, f32[8,128]{1,0:T(8,128)S(1)} %get-tuple-element.33, f32[8,128]{1,0:T(8,128)S(1)} %get-tuple-element.34), kind=kOutput, calls=%fused_computation.16 | convolution fusion | flops 270532608 | bytes 38805504 | tf_op jit(solution)/shard_map/cij,cbj->cbi/dot_general | solution.py:48
  334.3 4.3 all-to-all-start.1
  338.8 42.7 %convolution_add_fusion = f32[512,128,256]{2,1,0:T(8,128)} fusion(f32[512,128,256]{2,1,0:T(8,128)} %fusion.9, bf16[512,8,256]{2,1,0:T(8,128)(2,1)S(1)} %copy.75, bf16[512,9,128]{2,1,0:T(8,128)(2,1)} %copy-done), kind=kOutput, calls=%fused_computation.1 | convolution fusion | flops 285212672 | bytes 137363456 | tf_op jit(solution)/shard_map/cbi,cbj->cij/dot_general | solution.py:60
  381.6 69.3 %copy.91 = f32[512,128,256]{0,2,1:T(8,128)} copy(f32[512,128,256]{2,1,0:T(8,128)} %convolution_add_fusion) | data formatting | bytes 134217728 | tf_op jit(solution)/shard_map/reshape | solution.py:26
  450.9 43.6 %pad.9 = f32[512,32896]{0,1:T(8,128)} pad(f32[512,32768]{0,1:T(8,128)} %bitcast.22, f32[]{:T(128)} %constant.6.clone.1), padding=0_0x0_128 | pad | bytes 134479872 | tf_op jit(solution)/shard_map/jit(_pad)/pad | solution.py:27
  494.4 76.0 %reshape.140 = f32[512,128,257]{0,2,1:T(8,128)} reshape(f32[512,32896]{0,1:T(8,128)} %pad.9) | data formatting | bytes 134742016 | tf_op jit(solution)/shard_map/reshape | solution.py:28
  570.4 13.3 %slice_reduce_fusion = f32[512,128]{0,1:T(8,128)S(1)} fusion(f32[512,128,257]{0,2,1:T(8,128)} %reshape.140), kind=kLoop, calls=%fused_computation | loop fusion | flops 8323072 | bytes 33816576 | tf_op jit(solution)/shard_map/reduce_sum | solution.py:29
  587.7 34.1 %all-reduce.4.cloned.1.call-done = f32[512,128]{0,1:T(8,128)} async-done(((f32[512,128]{0,1:T(8,128)}), f32[512,128]{0,1:T(8,128)}) %all-reduce.4.cloned.1.call-update) | async-done | bytes 262160 | tf_op jit(solution)/shard_map/psum | solution.py:98
  (72 shorter events, 36.8 us)
Async XLA Ops:
  7.2 1.7 copy-start.7
  8.9 2.0 copy-start.3
  9.6 8.6 %copy-start.10 = (s32[4096]{0:T(1024)S(1)}, s32[4096]{0:T(1024)}, u32[]{:S(2)}) copy-start(s32[4096]{0:T(1024)} %param.11) | copy-start | bytes 49156
  9.6 9.0 %copy-start.9 = (f32[512,128]{1,0:T(8,128)S(1)}, f32[512,128]{1,0:T(8,128)}, u32[]{:S(2)}) copy-start(f32[512,128]{1,0:T(8,128)} %param.10) | copy-start | bytes 786436
  10.8 33.0 %all-to-all-start.2 = ((bf16[128,8,512]{0,2,1:T(8,128)(2,1)}), bf16[128,8,512]{0,2,1:T(8,128)(2,1)S(1)}, u32[]{:S(2)}, u32[]{:S(2)}) async-start(bf16[128,8,512]{0,2,1:T(8,128)(2,1)} %bitcast.12), calls=%async_computation.2 | async-start | bytes 2097152 | tf_op jit(solution)/shard_map/all_to_all | solution.py:80
  44.4 112.2 %collective-permute-start.1 = (bf16[512,128]{0,1:T(8,128)(2,1)S(1)}, bf16[512,128]{0,1:T(8,128)(2,1)S(1)}, u32[]{:S(2)}, u32[]{:S(2)}) collective-permute-start(bf16[512,128]{0,1:T(8,128)(2,1)S(1)} %slice.113), channel_id=1, source_target_pairs={{8,0},{16,8},{24,16},{9,1},{17,9},{25,17},{10,2},{18,10},{26,18},{... | collective-permute-start | bytes 393224 | tf_op jit(solution)/shard_map/ppermute | solution.py:12
  161.5 17.9 %copy-start.1 = (bf16[512,9,128]{2,1,0:T(8,128)(2,1)}, bf16[512,9,128]{2,1,0:T(8,128)(2,1)S(1)}, u32[]{:S(2)}) copy-start(bf16[512,9,128]{2,1,0:T(8,128)(2,1)S(1)} %get-tuple-element.21) | copy-start | bytes 3538948
  161.5 17.9 %copy-start = (bf16[512,9,128]{2,1,0:T(8,128)(2,1)}, bf16[512,9,128]{2,1,0:T(8,128)(2,1)S(1)}, u32[]{:S(2)}) copy-start(bf16[512,9,128]{2,1,0:T(8,128)(2,1)S(1)} %get-tuple-element.20) | copy-start | bytes 3538948
  201.4 4.7 copy-start.8
  202.5 31.2 %all-to-all-start.3 = ((bf16[8,128,512]{1,2,0:T(8,128)(2,1)}), bf16[8,128,512]{1,2,0:T(8,128)(2,1)S(1)}, u32[]{:S(2)}, u32[]{:S(2)}) async-start(bf16[8,128,512]{1,2,0:T(8,128)(2,1)} %copy_bitcast_fusion), calls=%async_computation.3 | async-start | bytes 2097152 | tf_op jit(solution)/shard_map/all_to_all | solution.py:96
  236.0 29.8 %all-to-all-start = ((bf16[128,8,512]{0,2,1:T(8,128)(2,1)}), bf16[128,8,512]{0,2,1:T(8,128)(2,1)S(1)}, u32[]{:S(2)}, u32[]{:S(2)}) async-start(bf16[128,8,512]{0,2,1:T(8,128)(2,1)} %bitcast.2), calls=%async_computation | async-start | bytes 2097152 | tf_op jit(solution)/shard_map/all_to_all | solution.py:79
  266.4 2.3 collective-permute-start
  274.7 16.0 %copy-start.2 = (bf16[512,9,128]{2,1,0:T(8,128)(2,1)S(1)}, bf16[512,9,128]{2,1,0:T(8,128)(2,1)}, u32[]{:S(2)}) copy-start(bf16[512,9,128]{2,1,0:T(8,128)(2,1)} %copy-done.1) | copy-start | bytes 3538948
  334.3 289.3 %all-to-all-start.1 = ((bf16[8,128,512]{2,1,0:T(8,128)(2,1)}), bf16[8,128,512]{2,1,0:T(8,128)(2,1)}, u32[]{:S(2)}, u32[]{:S(2)}) async-start(bf16[8,128,512]{2,1,0:T(8,128)(2,1)} %bitcast.9), calls=%async_computation.1 | async-start | bytes 2097152 | tf_op jit(solution)/shard_map/all_to_all | solution.py:93
  338.6 283.2 %all-reduce.4.cloned.1.call-start = ((), (), s32[]{:S(2)}) async-start(), calls=%async_computation.4 | async-start | bytes 524288 | tf_op jit(solution)/shard_map/psum | solution.py:98
  570.4 14.7 %copy-start.6 = (bf16[128,4096]{0,1:T(8,128)(2,1)S(1)}, bf16[128,4096]{0,1:T(8,128)(2,1)}, u32[]{:S(2)}) copy-start(bf16[128,4096]{0,1:T(8,128)(2,1)} %get-tuple-element.26) | copy-start | bytes 3145732
  583.7 2.7 copy-start.5
  586.4 38.8 %copy-start.4 = (bf16[128,4096]{0,1:T(8,128)(2,1)S(1)}, bf16[128,4096]{0,1:T(8,128)(2,1)}, u32[]{:S(2)}) copy-start(bf16[128,4096]{0,1:T(8,128)(2,1)} %copy-done.3) | copy-start | bytes 3145732
Sparse Core Ops, SparseCore 0:
  585.2 36.5 all-reduce.3
where the time goes:
time: 637 us; the launch traced here: 634 us
  local copies, waits for them, and re-layouts  326 us (51%)
  matrix products  134 us (21%)
  waiting for transfers between devices  111 us (17%)
  other arithmetic  25.9 us (4%)
  starting transfers between devices  21.7 us (3%)
  between operations  14.4 us (2%)
    reshape x1, local copies, waits for them, and re-layouts, lag_sums(): skewed = flat.reshape(chan_count, tap_count, span + 1)  76 us
    reshape x1, local copies, waits for them, and re-layouts, lag_sums(): flat = block.reshape(chan_count, tap_count * span)  69.3 us
    reshape x1, local copies, waits for them, and re-layouts, build_toeplitz(): return tiled.reshape(chan_count, tap_count, 2 * tap_count)  45.6 us
    pad x1, local copies, waits for them, and re-layouts, lag_sums(): flat = jnp.pad(flat, ((0, 0), (0, tap_count)))  43.6 us
    dot_general x1, matrix products, mix_block(): jnp.einsum('cbi,cbj->cij', g_other[:, :block_count], kv_other, preferred_...  42.7 us
    another operation x2, local copies, waits for them, and re-layouts, build_toeplitz(): tiled = jnp.tile(pattern, (1, tap_count))[:, :tap_count * 2 * tap_count]  42.1 us
    psum x1, waiting for transfers between devices, shards(): filter_total = lax.psum(partial_value, 'dp')  34.1 us
    all_to_all x1, waiting for transfers between devices, shards(): lax.all_to_all(product, 'ctx', split_axis=1, concat_axis=0, tiled=True)  26.2 us
  transfers between devices with their start and end apart: 7, of which 5 were waited for; matrix products, arithmetic and copies ran while one was open for 58% of the time, Pallas kernels for 0%

commit v1 on v0

v1 whole, which is shorter than its diff:
```python
import functools
import math

import jax
import jax.numpy as jnp
import ml_dtypes
import numpy as np
from jax import lax
from jax.experimental import pallas as pl
from jax.experimental.pallas import tpu as pltpu
from jax.sharding import PartitionSpec as P

BOTH = ("dp", "ctx")
F32 = jnp.float32
BF16 = jnp.bfloat16


def split_bf16(matrix):
    high = matrix.astype(ml_dtypes.bfloat16)
    low = (matrix - high.astype(np.float64)).astype(ml_dtypes.bfloat16)
    return high, low


def transforms(count):
    freq = np.arange(count) + 0.5
    place = np.arange(count)

    def forward(offset):
        angle = np.pi / count * np.outer(freq, place + offset)
        high, low = split_bf16(np.concatenate([np.cos(angle), -np.sin(angle)], 0))
        return np.concatenate([high, low], 1)

    angle = np.pi / count * np.outer(place, freq)
    inverse = np.concatenate([np.cos(angle), -np.sin(angle)], 1) / count
    return forward(0), forward(-count), forward(count), split_bf16(inverse)


def dot(a, b):
    return jnp.dot(a, b, preferred_element_type=F32)


def doubled(block):
    return jnp.concatenate([block, block], 0)


def tap_spectrum(fwd, taps):
    both = jnp.concatenate([taps, taps], 1)
    return lax.dot_general(fwd, both, (((1,), (1,)), ((), ())), preferred_element_type=F32)


def halves(spectrum):
    count = spectrum.shape[0] // 2
    return spectrum[:count], spectrum[count:]


def times(a, b):
    ar, ai = halves(a)
    br, bi = halves(b)
    return jnp.concatenate([ar * br - ai * bi, ar * bi + ai * br], 0)


def times_conj(a, b):
    ar, ai = halves(a)
    br, bi = halves(b)
    return jnp.concatenate([ar * br + ai * bi, ai * br - ar * bi], 0)


def invert(inv, spectrum):
    out = dot(inv, spectrum.astype(BF16))
    count = out.shape[0] // 2
    return out[:count] + out[count:]


def masked(block, mask):
    return block * mask.astype(BF16)


def tiles(width, chans):
    tile = max(chans, min(width, 1024))
    return [(start, start + tile, range(start // chans, (start + tile) // chans)) for start in range(0, width, tile)]


def own_lags_kernel(x_ref, g_ref, masks_ref, fwd_ref, inv_ref, out_ref, sent_ref):
    first, rest = masks_ref[:, 0:1], masks_ref[:, 1:2]
    sent_ref[...] = g_ref[...]
    fwd = fwd_ref[...]
    chans = out_ref.shape[2]
    for start, stop, groups in tiles(x_ref.shape[1], chans):
        x, g = x_ref[:, start:stop], g_ref[:, start:stop]
        corr = times_conj(dot(fwd, doubled(masked(g, first))), dot(fwd, doubled(masked(x, first))))
        corr += times_conj(dot(fwd, doubled(masked(g, rest))), dot(fwd, doubled(masked(x, rest))))
        lags = invert(inv_ref[...], corr)
        for j, group in enumerate(groups):
            out_ref[group] = lags[:, j * chans : (j + 1) * chans]


def own_back_kernel(place_ref, g_ref, mine_ref, other_ref, masks_ref, fwd_ref, inv_ref, out_ref, taps_ref):
    first, rest = masks_ref[:, 0:1], masks_ref[:, 1:2]
    fwd, inv = fwd_ref[...], inv_ref[...]
    me, core = place_ref[0], place_ref[1]
    chans = 2 * mine_ref.shape[1]
    for start, stop, groups in tiles(g_ref.shape[1], chans):
        parts = []
        for group in groups:
            mine, other = mine_ref[group ^ me], other_ref[group ^ me]
            parts += [jnp.where(core == 0, mine, other), jnp.where(core == 0, other, mine)]
        taps = tap_spectrum(fwd, jnp.concatenate(parts, 0))
        taps_ref[:, start:stop] = taps
        g = g_ref[:, start:stop]
        head = invert(inv, times_conj(dot(fwd, doubled(masked(g, first))), taps))
        tail = invert(inv, times_conj(dot(fwd, doubled(masked(g, rest))), taps))
        out_ref[:, start:stop] = head * first + tail * rest


def lags_kernel(place_ref, g_ref, prior_ref, own_ref, masks_ref, fwd_ref, prior_fwd_ref, inv_ref, keep_ref, send_ref):
    first, before = masks_ref[:, 0:1], masks_ref[:, 2:3]
    chans = own_ref.shape[2]
    half = own_ref.shape[1] // 2
    me = place_ref[0]
    for start, stop, groups in tiles(g_ref.shape[1], chans):
        g = dot(fwd_ref[...], doubled(masked(g_ref[:, start:stop], first)))
        prior = dot(prior_fwd_ref[...], doubled(masked(prior_ref[:, start:stop], before)))
        lags = invert(inv_ref[...], times_conj(g, prior))
        for j, group in enumerate(groups):
            total = own_ref[group] + lags[:, j * chans : (j + 1) * chans]
            keep_ref[group ^ me] = total[:half]
            send_ref[group ^ me] = total[half:].astype(send_ref.dtype)


def query_kernel(x_ref, prior_ref, o_ref, taps_ref, masks_ref, fwd_ref, prior_fwd_ref, inv_ref, out_ref):
    first, rest, before = masks_ref[:, 0:1], masks_ref[:, 1:2], masks_ref[:, 2:3]
    fwd, inv = fwd_ref[...], inv_ref[...]
    for start, stop, _ in tiles(x_ref.shape[1], 1):
        x = x_ref[:, start:stop]
        taps = taps_ref[:, start:stop]
        prior = dot(prior_fwd_ref[...], doubled(masked(prior_ref[:, start:stop], before)))
        head = invert(inv, times(dot(fwd, doubled(masked(x, first))) + prior, taps))
        tail = invert(inv, times(dot(fwd, doubled(masked(x, rest))), taps))
        mixed = head * first + tail * rest
        out_ref[:, start:stop] = (o_ref[:, start:stop].astype(F32) * mixed).astype(out_ref.dtype)


def back_kernel(next_ref, own_ref, k_ref, v_ref, taps_ref, masks_ref, next_fwd_ref, inv_ref, k_out, v_out):
    after, last = masks_ref[:, 3:4], masks_ref[:, 4:5]
    for start, stop, _ in tiles(k_ref.shape[1], 1):
        later = dot(next_fwd_ref[...], doubled(masked(next_ref[:, start:stop], after)))
        later = invert(inv_ref[...], times_conj(later, taps_ref[:, start:stop]))
        back = own_ref[:, start:stop] + last * later
        k_out[:, start:stop] = (back * v_ref[:, start:stop].astype(F32)).astype(k_out.dtype)
        v_out[:, start:stop] = (back * k_ref[:, start:stop].astype(F32)).astype(v_out.dtype)


def first_sum_kernel(keep_ref, swapped_ref, own_ref, *send_refs):
    own_ref[...] = keep_ref[:2] + swapped_ref[:2].astype(F32)
    for j, send_ref in enumerate(send_refs):
        at = slice(2 * j + 2, 2 * j + 4)
        send_ref[...] = (keep_ref[at] + swapped_ref[at].astype(F32)).astype(send_ref.dtype)


def second_sum_kernel(count, *refs):
    total = refs[0][...]
    for ref in refs[1:count]:
        total = total + ref[...].astype(F32)
    own_ref, low_ref, high_ref = refs[count:]
    own_ref[...] = total[0]
    low_ref[...] = total[0].astype(low_ref.dtype)
    high_ref[...] = total[1].astype(high_ref.dtype)


def third_sum_kernel(count, *refs):
    total = refs[0][...]
    for ref in refs[1:count]:
        total = total + ref[...].astype(F32)
    for ref in refs[count:]:
        ref[...] = total


def finish_kernel(scale, place_ref, mine_ref, other_ref, out_ref):
    mine, other = mine_ref[...], other_ref[...]
    core = place_ref[1]
    low = jnp.where(core == 0, mine, other)
    high = jnp.where(core == 0, other, mine)
    out_ref[...] = jnp.concatenate([low, high], 0).T * scale


def swap(value, axis, bit):
    count = lax.axis_size(axis)
    return lax.ppermute(value, axis, [(i, i ^ bit) for i in range(count)])


def cross(value, dp_bits, ctx_bits):
    dp, ctx = lax.axis_size("dp"), lax.axis_size("ctx")
    pairs = [(d * ctx + c, (d ^ dp_bits) * ctx + (c ^ ctx_bits)) for d in range(dp) for c in range(ctx)]
    return lax.ppermute(value, BOTH, pairs)


def bits_of(count):
    assert count & (count - 1) == 0
    return [1 << b for b in range(count.bit_length() - 1)]


def gather_taps(taps):
    dp, ctx = lax.axis_size("dp"), lax.axis_size("ctx")
    core = lax.axis_index("dp") % 2
    chans = taps.shape[0]
    half = lax.dynamic_slice_in_dim(taps, core * (chans // 2), chans // 2, 0).astype(BF16)[None]
    steps = []
    for bit in bits_of(ctx):
        half = jnp.concatenate([half, swap(half, "ctx", bit)], 0)
        steps.append(half)
    return half, swap(half, "dp", 1), steps


def document_masks(doc_ids, rows):
    index = lax.axis_index(BOTH)
    padded = jnp.pad(doc_ids, (rows, rows), constant_values=-1)
    window = lax.dynamic_slice_in_dim(padded, index * rows, 3 * rows).reshape(3, rows)
    own = window[1]
    first = own == own[0]
    last = own == own[-1]
    before = window[0] == own[0]
    after = window[2] == own[-1]
    columns = [first, ~first, before, after, last, last, last, last]
    return jnp.stack(columns, 1).astype(F32)


def shards(query_act, key_act, value_act, out_grad, filter_taps, doc_ids):
    rows, width = query_act.shape
    chans, tap_count = filter_taps.shape
    dp, ctx = lax.axis_size("dp"), lax.axis_size("ctx")
    assert rows == tap_count and chans * ctx == width
    scale = 1.0 / math.sqrt(doc_ids.shape[0])
    count = dp * ctx
    fwd, prior_fwd, next_fwd, (inv_high, inv_low) = transforms(tap_count)
    inv = np.concatenate([inv_high, inv_low], 0)
    rolled = [np.concatenate([np.roll(m, -c * rows // 2, 0) for m in (inv_high, inv_low)], 0) for c in (0, 1)]
    core = lax.axis_index("dp") % 2
    inv_lags = lax.dynamic_index_in_dim(jnp.asarray(np.stack(rolled)), core, 0, keepdims=False)
    fwd, prior_fwd, next_fwd, inv = map(jnp.asarray, (fwd, prior_fwd, next_fwd, inv))

    place = jnp.stack([lax.axis_index("ctx"), core]).astype(jnp.int32)
    x = (key_act.astype(F32) * value_act.astype(F32)).astype(BF16)
    prior = lax.ppermute(x, BOTH, [(i, i + 1) for i in range(count - 1)])
    g = (query_act.astype(F32) * out_grad.astype(F32)).astype(BF16)
    taps_mine, taps_other, steps = gather_taps(filter_taps)
    masks = document_masks(doc_ids, rows)

    vmem = pl.BlockSpec(memory_space=pltpu.VMEM)
    smem = pl.BlockSpec(memory_space=pltpu.SMEM)
    anywhere = pl.BlockSpec(memory_space=pl.ANY)
    streamed = pl.BlockSpec()

    def call(kernel, outs, *args, scalars=0, after=(), out_specs=None):
        read = len(args)
        return pl.pallas_call(
            lambda *refs: kernel(*refs[:read], *refs[read + len(after) :]),
            out_shape=outs,
            in_specs=[smem] * scalars + [vmem] * (read - scalars) + [anywhere] * len(after),
            out_specs=jax.tree.map(lambda _: vmem, outs) if out_specs is None else out_specs,
            compiler_params=pltpu.CompilerParams(vmem_limit_bytes=40 * 1024 * 1024),
            cost_estimate=pl.CostEstimate(flops=1, bytes_accessed=1, transcendentals=0),
        )(*args, *after)

    sds = jax.ShapeDtypeStruct
    act = sds((rows, width), BF16)
    own_lags, g_sent = call(
        own_lags_kernel, (sds((ctx, rows, chans), F32), act), x, g, masks, fwd, inv_lags, after=(steps[1],),
        out_specs=(vmem, streamed),
    )
    later = lax.ppermute(g_sent, BOTH, [(i + 1, i) for i in range(count - 1)])
    keep, send = call(
        lags_kernel,
        (sds((ctx, rows // 2, chans), F32), sds((ctx, rows // 2, chans), BF16)),
        place, g, prior, own_lags, masks, fwd, prior_fwd, inv_lags,
        scalars=1, after=(steps[-1],), out_specs=(vmem, streamed),
    )
    own_back, spectrum = call(
        own_back_kernel,
        (sds((rows, width), F32), sds((2 * rows, width), F32)),
        place, g, taps_mine, taps_other, masks, fwd, inv,
        scalars=1, after=(send,),
    )
    query_grad = call(query_kernel, act, x, prior, out_grad, spectrum, masks, fwd, prior_fwd, inv)
    key_grad, value_grad = call(
        back_kernel, (act, act), later, own_back, key_act, value_act, spectrum, masks, next_fwd, inv
    )

    near = [j for j in range(2, ctx, 2)]
    pair = (2, rows // 2, chans)
    own, *sends = call(
        first_sum_kernel,
        (sds(pair, F32),) + (sds(pair, BF16),) * len(near),
        keep, swap(send, "dp", 1),
        out_specs=(vmem,) + (streamed,) * len(near),
    )
    got = [swap(value, "ctx", j) for value, j in zip(sends, near)]
    single = pair[1:]
    own, low, high = call(
        functools.partial(second_sum_kernel, 1 + len(got)),
        (sds(single, F32), sds(single, BF16), sds(single, BF16)),
        own, *got,
        out_specs=(vmem, streamed, streamed),
    )
    got = [
        cross(high if j else low, d, j) for d in range(0, dp, 2) for j in (0, 1) if d or j
    ]
    total, total_sent = call(
        functools.partial(third_sum_kernel, 1 + len(got)),
        (sds(single, F32), sds(single, F32)),
        own, *got,
        out_specs=(vmem, streamed),
    )
    filter_grad = call(
        functools.partial(finish_kernel, scale), sds((chans, tap_count), F32), place, total, swap(total_sent, "dp", 1),
        scalars=1,
    )
    return (query_grad, key_grad, value_grad, filter_grad)


def solution(mesh):
    in_specs = (
        P(BOTH, None),
        P(BOTH, None),
        P(BOTH, None),
        P(BOTH, None),
        P("ctx", None),
        P(),
    )
    out_specs = (
        P(BOTH, None),
        P(BOTH, None),
        P(BOTH, None),
        P("ctx", None),
    )
    return jax.shard_map(shards, mesh=mesh, in_specs=in_specs, out_specs=out_specs, check_vma=False)
```

time: 637 us -> 111 us (0.17)
  local copies, waits for them, and re-layouts: 326 us -> 6.22 us
  matrix products: 134 us -> 0 us
  waiting for transfers between devices: 111 us -> 29.3 us
  Pallas kernels: 0 us -> 24.6 us
  starting transfers between devices: 21.7 us -> 43.3 us
  other arithmetic: 25.9 us -> 5.73 us
  between operations: 14.4 us -> 0.91 us
    reshape x4 -> x0, local copies, waits for them, and re-layouts: 194 us -> none  [the longest x1 76 us: lag_sums(): skewed = flat.reshape(chan_count, tap_count, span + 1)]
    dot_general x6 -> x0, matrix products: 134 us -> none  [the longest x1 42.7 us: mix_block(): jnp.einsum('cbi,cbj->cij', g_other[:, :block_count], kv_other, preferred_...]
    all_to_all x4 -> x0, waiting for transfers between devices: 76.4 us -> none  [the longest x1 26.2 us: shards(): lax.all_to_all(product, 'ctx', split_axis=1, concat_axis=0, tiled=True)]
    pad x1 -> x0, local copies, waits for them, and re-layouts: 43.6 us -> none  [lag_sums(): flat = jnp.pad(flat, ((0, 0), (0, tap_count)))]
    ppermute x2 -> x14, starting transfers between devices: 2.77 us -> 43.3 us  [the longest x9 35.3 us: swap(): return lax.ppermute(value, axis, [(i, i ^ bit) for i in range(count)])]
    another operation x2, local copies, waits for them, and re-layouts: 42.1 us -> 2.05 us  [document_masks(): return jnp.stack(columns, 1).astype(F32)]
    psum x1 -> x0, waiting for transfers between devices: 34.1 us -> none  [shards(): filter_total = lax.psum(partial_value, 'dp')]
    ppermute x2 -> x14, waiting for transfers between devices: 0.77 us -> 29.3 us  [the longest x9 26.2 us: swap(): return lax.ppermute(value, axis, [(i, i ^ bit) for i in range(count)])]
  transfers between devices with their start and end apart: 7 -> 14, of which waited for: 5 -> 7; matrix products, arithmetic and copies ran while one was open for 58% -> 9% of each run, Pallas kernels for 0% -> 21%
where the time goes in v1:
time: 111 us; the launch traced here: 110 us
  starting transfers between devices  43.3 us (39%)
  waiting for transfers between devices  29.3 us (26%)
  Pallas kernels  24.6 us (22%)
  local copies, waits for them, and re-layouts  6.22 us (6%)
  other arithmetic  5.73 us (5%)
    ppermute x9, starting transfers between devices, swap(): return lax.ppermute(value, axis, [(i, i ^ bit) for i in range(count)])  35.3 us
    ppermute x9, waiting for transfers between devices, swap(): return lax.ppermute(value, axis, [(i, i ^ bit) for i in range(count)])  26.2 us
    pallas_call x9, Pallas kernels, call(): pl.pallas_call(lambda *refs: kernel(*refs[:read], *refs[read + len(after)...  24.6 us
    ppermute x3, starting transfers between devices, cross(): return lax.ppermute(value, BOTH, pairs)  3.55 us
    ppermute x3, waiting for transfers between devices, cross(): return lax.ppermute(value, BOTH, pairs)  3.07 us
    ppermute x1, starting transfers between devices, shards(): prior = lax.ppermute(x, BOTH, [(i, i + 1) for i in range(count - 1)])  2.97 us
    unnamed x30, local copies, waits for them, and re-layouts  2.55 us
  transfers between devices with their start and end apart: 14, of which 7 were waited for; matrix products, arithmetic and copies ran while one was open for 9% of the time, Pallas kernels for 21%

profile of v1, /device:TPU:0, one launch (start us, length us, event | category | flops | bytes accessed | tf_op | source)
XLA Modules:
  0.0 110.1 jit_solution(11224007092701370271)
XLA Ops:
  1.6 3.0 %collective-permute-start.1 = (bf16[1,256,128]{2,1,0:T(8,128)(2,1)S(1)}, bf16[1,256,128]{2,1,0:T(8,128)(2,1)S(1)}, u32[]{:S(2)}, u32[]{:S(2)}) collective-permute-start(bf16[1,256,128]{2,1,0:T(8,128)(2,1)S(1)} %fusion), channel_id=1, source_target_pairs={{0,1},{1,0},{2,3},{3,2},{4,5},{5,4},{6,7},{7,6},{8,9},{9,8},{10,11... | collective-permute-start | bytes 196616 | tf_op jit(solution)/shard_map/ppermute | solution.py:188
  4.6 1.8 %multiply_convert_fusion.1.refs_0_ = bf16[128,4096]{1,0:T(8,128)(2,1)S(1)} fusion(bf16[128,4096]{1,0:T(8,128)(2,1)} %refs_3_.2, bf16[128,4096]{1,0:T(8,128)(2,1)} %refs_2_.3), kind=kLoop, calls=%fused_computation.1 | loop fusion | flops 2097152 | bytes 3145728 | tf_op jit(solution)/shard_map/convert_element_type | solution.py:242
  6.4 3.0 %collective-permute-start = (bf16[128,4096]{1,0:T(8,128)(2,1)S(1)}, bf16[128,4096]{1,0:T(8,128)(2,1)}, u32[]{:S(2)}, u32[]{:S(2)}) collective-permute-start(bf16[128,4096]{1,0:T(8,128)(2,1)S(1)} %multiply_convert_fusion.1.refs_0_), channel_id=1, source_target_pairs={{0,1},{1,2},{2,3},{3,4},{4,5},{5,6},{6,7},{7,8},{8,9},{9,10},{10,1... | collective-permute-start | bytes 3145736 | tf_op jit(solution)/shard_map/ppermute | solution.py:243
  9.7 1.1 %collective-permute-start.2 = (bf16[2,256,128]{2,1,0:T(8,128)(2,1)S(1)}, bf16[2,256,128]{2,1,0:T(8,128)(2,1)S(1)}, u32[]{:S(2)}, u32[]{:S(2)}) collective-permute-start(bf16[2,256,128]{2,1,0:T(8,128)(2,1)S(1)} %pad_maximum_fusion.2), channel_id=1, source_target_pairs={{0,2},{1,3},{2,0},{3,1},{4,6},{5,7},{6,4},{7,5},{8,10},{9,11},{10,... | collective-permute-start | bytes 393224 | tf_op jit(solution)/shard_map/ppermute | solution.py:188
  11.5 3.2 %collective-permute-done.2 = bf16[2,256,128]{2,1,0:T(8,128)(2,1)S(1)} collective-permute-done((bf16[2,256,128]{2,1,0:T(8,128)(2,1)S(1)}, bf16[2,256,128]{2,1,0:T(8,128)(2,1)S(1)}, u32[]{:S(2)}, u32[]{:S(2)}) %collective-permute-start.2) | collective-permute-done | bytes 131104 | tf_op jit(solution)/shard_map/ppermute | solution.py:188
  16.1 2.1 %collective-permute-start.3 = (bf16[4,256,128]{2,1,0:T(8,128)(2,1)}, bf16[4,256,128]{2,1,0:T(8,128)(2,1)}, u32[]{:S(2)}, u32[]{:S(2)}) collective-permute-start(bf16[4,256,128]{2,1,0:T(8,128)(2,1)} %pad_maximum_fusion.1.refs_5_), channel_id=1, source_target_pairs={{0,4},{1,5},{2,6},{3,7},{4,0},{5,1},{6,2},{7,3},{8,12},{9,13},{10,... | collective-permute-start | bytes 786440 | tf_op jit(solution)/shard_map/ppermute | solution.py:188
  18.2 1.9 %compare_bitcast_fusion = (pred[128,1]{0,1:T(4,128)(4,1)S(1)}, pred[128,1]{0,1:T(4,128)(4,1)S(1)}, pred[128,1]{0,1:T(4,128)(4,1)S(1)}, pred[128,1]{0,1:T(4,128)(4,1)S(1)}, pred[128,1]{0,1:T(4,128)(4,1)}) fusion(s32[]{:T(128)} %bitcast.7, s32[384]{0:T(512)S(1)} %pad_dynamic-slice_fusion, s32[]{:T(128)} %bitcast.3), kind=kLoop, calls=%fused_computation.9 | loop fusion | flops 640 | bytes 2184 | tf_op jit(solution)/shard_map/stack | solution.py:224
  20.1 1.2 %stack.32 = pred[128,8]{0,1:T(8,128)(4,1)} concatenate(pred[128,1]{0,1:T(4,128)(4,1)S(1)} %get-tuple-element.41, pred[128,1]{0,1:T(4,128)(4,1)S(1)} %get-tuple-element.39, pred[128,1]{0,1:T(4,128)(4,1)S(1)} %get-tuple-element.40, pred[128,1]{0,1:T(4,128)(4,1)} %get-tuple-element.42, pred[128,1]{0,1:T(4,128)(4,1)S(1)} %get-tuple-element.38, pred[128,1]{0,1:T(4,128)(4,1)S(1)} %get-tuple-element.38, ...), dimensions={1} | concatenate | bytes 2048 | tf_op jit(solution)/shard_map/stack | solution.py:224
  24.0 4.1 %shard_map.138 = (f32[8,128,512]{2,1,0:T(8,128)S(1)}, bf16[128,4096]{1,0:T(8,128)(2,1)S(1)}) custom-call(bf16[128,4096]{1,0:T(8,128)(2,1)S(1)} %multiply_convert_fusion.1.refs_0_, bf16[128,4096]{1,0:T(8,128)(2,1)S(1)} %multiply_convert_fusion.refs_1_, f32[128,8]{1,0:T(8,128)S(1)} %convert_element_type.31.refs_2_.refs_4_.refs_5_, ...), custom_call_target="tpu_custom_call" | custom-call | flops 1 | bytes 1 | tf_op jit(solution)/shard_map/pallas_call | solution.py:255
  28.1 1.5 %collective-permute-start.5 = (bf16[128,4096]{1,0:T(8,128)(2,1)S(1)}, bf16[128,4096]{1,0:T(8,128)(2,1)S(1)}, u32[]{:S(2)}, u32[]{:S(2)}) collective-permute-start(bf16[128,4096]{1,0:T(8,128)(2,1)S(1)} %get-tuple-element.24), channel_id=1, source_target_pairs={{1,0},{2,1},{3,2},{4,3},{5,4},{6,5},{7,6},{8,7},{9,8},{10,9},{11,1... | collective-permute-start | bytes 3145736 | tf_op jit(solution)/shard_map/ppermute | solution.py:270
  30.8 3.6 %shard_map.139 = (f32[8,64,512]{2,1,0:T(8,128)S(1)}, bf16[8,64,512]{2,1,0:T(8,128)(2,1)S(1)}) custom-call(s32[2]{0:T(128)S(1)} %pad_add_fusion.refs_0_, bf16[128,4096]{1,0:T(8,128)(2,1)S(1)} %multiply_convert_fusion.refs_1_, bf16[128,4096]{1,0:T(8,128)(2,1)} %collective-permute-done.refs_2_.refs_1_, f32[8,128,512]{2,1,0:T(8,128)S(1)} %get-tuple-element.21.refs_3_, ...), custom_call_target="tpu_custom_call" | custom-call | flops 1 | bytes 1 | tf_op jit(solution)/shard_map/pallas_call | solution.py:255
  34.5 24.5 %collective-permute-start.6 = (bf16[8,64,512]{2,1,0:T(8,128)(2,1)S(1)}, bf16[8,64,512]{2,1,0:T(8,128)(2,1)S(1)}, u32[]{:S(2)}, u32[]{:S(2)}) collective-permute-start(bf16[8,64,512]{2,1,0:T(8,128)(2,1)S(1)} %get-tuple-element.22.refs_7_), channel_id=1, source_target_pairs={{0,8},{8,0},{16,24},{24,16},{1,9},{9,1},{17,25},{25,17},{2,10},{10... | collective-permute-start | bytes 1572872 | tf_op jit(solution)/shard_map/ppermute | solution.py:188
  59.0 1.5 %collective-permute-done.6.refs_1_ = bf16[8,64,512]{2,1,0:T(8,128)(2,1)S(1)} collective-permute-done((bf16[8,64,512]{2,1,0:T(8,128)(2,1)S(1)}, bf16[8,64,512]{2,1,0:T(8,128)(2,1)S(1)}, u32[]{:S(2)}, u32[]{:S(2)}) %collective-permute-start.6) | collective-permute-done | bytes 524320 | tf_op jit(solution)/shard_map/ppermute | solution.py:188
  60.8 2.8 %collective-permute-start.8 = (bf16[2,64,512]{2,1,0:T(8,128)(2,1)S(1)}, bf16[2,64,512]{2,1,0:T(8,128)(2,1)S(1)}, u32[]{:S(2)}, u32[]{:S(2)}) collective-permute-start(bf16[2,64,512]{2,1,0:T(8,128)(2,1)S(1)} %get-tuple-element.31), channel_id=1, source_target_pairs={{0,4},{1,5},{2,6},{3,7},{4,0},{5,1},{6,2},{7,3},{8,12},{9,13},{10,... | collective-permute-start | bytes 393224 | tf_op jit(solution)/shard_map/ppermute | solution.py:188
  63.6 1.4 %collective-permute-start.9 = (bf16[2,64,512]{2,1,0:T(8,128)(2,1)S(1)}, bf16[2,64,512]{2,1,0:T(8,128)(2,1)S(1)}, u32[]{:S(2)}, u32[]{:S(2)}) collective-permute-start(bf16[2,64,512]{2,1,0:T(8,128)(2,1)S(1)} %get-tuple-element.32), channel_id=1, source_target_pairs={{0,6},{1,7},{2,4},{3,5},{4,2},{5,3},{6,0},{7,1},{8,14},{9,15},{10,... | collective-permute-start | bytes 393224 | tf_op jit(solution)/shard_map/ppermute | solution.py:188
  65.1 19.1 %collective-permute-done.7.refs_1_ = bf16[2,64,512]{2,1,0:T(8,128)(2,1)S(1)} collective-permute-done((bf16[2,64,512]{2,1,0:T(8,128)(2,1)S(1)}, bf16[2,64,512]{2,1,0:T(8,128)(2,1)S(1)}, u32[]{:S(2)}, u32[]{:S(2)}) %collective-permute-start.7) | collective-permute-done | bytes 131104 | tf_op jit(solution)/shard_map/ppermute | solution.py:188
  84.2 2.4 %collective-permute-done.8.refs_2_ = bf16[2,64,512]{2,1,0:T(8,128)(2,1)S(1)} collective-permute-done((bf16[2,64,512]{2,1,0:T(8,128)(2,1)S(1)}, bf16[2,64,512]{2,1,0:T(8,128)(2,1)S(1)}, u32[]{:S(2)}, u32[]{:S(2)}) %collective-permute-start.8) | collective-permute-done | bytes 131104 | tf_op jit(solution)/shard_map/ppermute | solution.py:188
  86.6 1.5 %collective-permute-start.11 = (bf16[64,512]{1,0:T(8,128)(2,1)S(1)}, bf16[64,512]{1,0:T(8,128)(2,1)S(1)}, u32[]{:S(2)}, u32[]{:S(2)}) collective-permute-start(bf16[64,512]{1,0:T(8,128)(2,1)S(1)} %get-tuple-element.35), channel_id=1, source_target_pairs={{0,16},{1,17},{2,18},{3,19},{4,20},{5,21},{6,22},{7,23},{8,24},{9,... | collective-permute-start | bytes 196616 | tf_op jit(solution)/shard_map/ppermute | solution.py:194
  88.1 2.1 %collective-permute-start.10 = (bf16[64,512]{1,0:T(8,128)(2,1)S(1)}, bf16[64,512]{1,0:T(8,128)(2,1)S(1)}, u32[]{:S(2)}, u32[]{:S(2)}) collective-permute-start(bf16[64,512]{1,0:T(8,128)(2,1)S(1)} %get-tuple-element.34), channel_id=1, source_target_pairs={{0,1},{1,0},{2,3},{3,2},{4,5},{5,4},{6,7},{7,6},{8,9},{9,8},{10,11... | collective-permute-start | bytes 196616 | tf_op jit(solution)/shard_map/ppermute | solution.py:194
  90.9 2.3 %collective-permute-done.12.refs_3_ = bf16[64,512]{1,0:T(8,128)(2,1)S(1)} collective-permute-done((bf16[64,512]{1,0:T(8,128)(2,1)S(1)}, bf16[64,512]{1,0:T(8,128)(2,1)S(1)}, u32[]{:S(2)}, u32[]{:S(2)}) %collective-permute-start.12) | collective-permute-done | bytes 65568 | tf_op jit(solution)/shard_map/ppermute | solution.py:194
  93.4 5.0 %shard_map.140 = (f32[128,4096]{1,0:T(8,128)S(1)}, f32[256,4096]{1,0:T(8,128)S(1)}) custom-call(s32[2]{0:T(128)S(1)} %pad_add_fusion.refs_0_, bf16[128,4096]{1,0:T(8,128)(2,1)S(1)} %multiply_convert_fusion.refs_1_, bf16[8,256,128]{2,1,0:T(8,128)(2,1)S(1)} %pad_maximum_fusion.refs_8_.refs_2_, bf16[8,256,128]{2,1,0:T(8,128)(2,1)S(1)} %collective-permute-done.4.refs_3_, ...), custom_call_target="tpu_custom_call" | custom-call | flops 1 | bytes 1 | tf_op jit(solution)/shard_map/pallas_call | solution.py:255
  98.4 6.8 %shard_map.141 = bf16[128,4096]{1,0:T(8,128)(2,1)} custom-call(bf16[128,4096]{1,0:T(8,128)(2,1)S(1)} %multiply_convert_fusion.1.refs_0_, bf16[128,4096]{1,0:T(8,128)(2,1)} %collective-permute-done.refs_2_.refs_1_, bf16[128,4096]{1,0:T(8,128)(2,1)S(1)} %copy-done.1, f32[256,4096]{1,0:T(8,128)S(1)} %get-tuple-element.23.refs_3_.refs_4_, ...), custom_call_target="tpu_custom_call" | custom-call | flops 1 | bytes 1 | tf_op jit(solution)/shard_map/pallas_call | solution.py:255
  105.2 3.5 %shard_map.142 = (bf16[128,4096]{1,0:T(8,128)(2,1)}, bf16[128,4096]{1,0:T(8,128)(2,1)}) custom-call(bf16[128,4096]{1,0:T(8,128)(2,1)S(1)} %collective-permute-done.5.refs_0_, f32[128,4096]{1,0:T(8,128)S(1)} %get-tuple-element.25.refs_1_, bf16[128,4096]{1,0:T(8,128)(2,1)S(1)} %copy-done.3, bf16[128,4096]{1,0:T(8,128)(2,1)S(1)} %copy-done.2, ...), custom_call_target="tpu_custom_call" | custom-call | flops 1 | bytes 1 | tf_op jit(solution)/shard_map/pallas_call | solution.py:255
  108.7 1.4 %shard_map.146 = f32[512,128]{1,0:T(8,128)} custom-call(s32[2]{0:T(128)S(1)} %pad_add_fusion.refs_0_, f32[64,512]{1,0:T(8,128)S(1)} %get-tuple-element.36.refs_1_, f32[64,512]{1,0:T(8,128)S(1)} %collective-permute-done.13.refs_2_), custom_call_target="tpu_custom_call" | custom-call | flops 1 | bytes 1 | tf_op jit(solution)/shard_map/pallas_call | solution.py:255
  (57 shorter events, 8.5 us)
Async XLA Ops:
  0.6 8.7 %copy-start.1 = (bf16[128,4096]{1,0:T(8,128)(2,1)S(1)}, bf16[128,4096]{1,0:T(8,128)(2,1)}, u32[]{:S(2)}) copy-start(bf16[128,4096]{1,0:T(8,128)(2,1)} %refs_2_.2) | copy-start | bytes 3145732
  1.6 7.8 %copy-start.9 = (bf16[128,4096]{1,0:T(8,128)(2,1)S(1)}, bf16[128,4096]{1,0:T(8,128)(2,1)}, u32[]{:S(2)}) copy-start(bf16[128,4096]{1,0:T(8,128)(2,1)} %param.11) | copy-start | bytes 3145732
  1.6 8.1 %collective-permute-start.1 = (bf16[1,256,128]{2,1,0:T(8,128)(2,1)S(1)}, bf16[1,256,128]{2,1,0:T(8,128)(2,1)S(1)}, u32[]{:S(2)}, u32[]{:S(2)}) collective-permute-start(bf16[1,256,128]{2,1,0:T(8,128)(2,1)S(1)} %fusion), channel_id=1, source_target_pairs={{0,1},{1,0},{2,3},{3,2},{4,5},{5,4},{6,7},{7,6},{8,9},{9,8},{10,11... | collective-permute-start | bytes 196616 | tf_op jit(solution)/shard_map/ppermute | solution.py:188
  6.4 24.4 %collective-permute-start = (bf16[128,4096]{1,0:T(8,128)(2,1)S(1)}, bf16[128,4096]{1,0:T(8,128)(2,1)}, u32[]{:S(2)}, u32[]{:S(2)}) collective-permute-start(bf16[128,4096]{1,0:T(8,128)(2,1)S(1)} %multiply_convert_fusion.1.refs_0_), channel_id=1, source_target_pairs={{0,1},{1,2},{2,3},{3,4},{4,5},{5,6},{6,7},{7,8},{8,9},{9,10},{10,1... | collective-permute-start | bytes 3145736 | tf_op jit(solution)/shard_map/ppermute | solution.py:243
  9.7 11.7 %copy-start.10 = (bf16[1,256,128]{2,1,0:T(8,128)(2,1)}, bf16[1,256,128]{2,1,0:T(8,128)(2,1)S(1)}, u32[]{:S(2)}) copy-start(bf16[1,256,128]{2,1,0:T(8,128)(2,1)S(1)} %collective-permute-done.1) | copy-start | bytes 196612
  9.7 5.0 %collective-permute-start.2 = (bf16[2,256,128]{2,1,0:T(8,128)(2,1)S(1)}, bf16[2,256,128]{2,1,0:T(8,128)(2,1)S(1)}, u32[]{:S(2)}, u32[]{:S(2)}) collective-permute-start(bf16[2,256,128]{2,1,0:T(8,128)(2,1)S(1)} %pad_maximum_fusion.2), channel_id=1, source_target_pairs={{0,2},{1,3},{2,0},{3,1},{4,6},{5,7},{6,4},{7,5},{8,10},{9,11},{10,... | collective-permute-start | bytes 393224 | tf_op jit(solution)/shard_map/ppermute | solution.py:188
  16.1 13.6 %collective-permute-start.3 = (bf16[4,256,128]{2,1,0:T(8,128)(2,1)}, bf16[4,256,128]{2,1,0:T(8,128)(2,1)}, u32[]{:S(2)}, u32[]{:S(2)}) collective-permute-start(bf16[4,256,128]{2,1,0:T(8,128)(2,1)} %pad_maximum_fusion.1.refs_5_), channel_id=1, source_target_pairs={{0,4},{1,5},{2,6},{3,7},{4,0},{5,1},{6,2},{7,3},{8,12},{9,13},{10,... | collective-permute-start | bytes 786440 | tf_op jit(solution)/shard_map/ppermute | solution.py:188
  22.1 7.6 %copy-start.11 = (bf16[1,256,128]{2,1,0:T(8,128)(2,1)S(1)}, bf16[1,256,128]{2,1,0:T(8,128)(2,1)}, u32[]{:S(2)}) copy-start(bf16[1,256,128]{2,1,0:T(8,128)(2,1)} %copy-done.10) | copy-start | bytes 196612
  22.1 8.7 %copy-start.7 = (bf16[256,256]{1,0:T(8,128)(2,1)S(1)}, bf16[256,256]{1,0:T(8,128)(2,1)}, u32[]{:S(2)}) copy-start(bf16[256,256]{1,0:T(8,128)(2,1)} %constant.52.clone.refs_6_) | copy-start | bytes 393220
  28.1 77.0 %collective-permute-start.5 = (bf16[128,4096]{1,0:T(8,128)(2,1)S(1)}, bf16[128,4096]{1,0:T(8,128)(2,1)S(1)}, u32[]{:S(2)}, u32[]{:S(2)}) collective-permute-start(bf16[128,4096]{1,0:T(8,128)(2,1)S(1)} %get-tuple-element.24), channel_id=1, source_target_pairs={{1,0},{2,1},{3,2},{4,3},{5,4},{6,5},{7,6},{8,7},{9,8},{10,9},{11,1... | collective-permute-start | bytes 3145736 | tf_op jit(solution)/shard_map/ppermute | solution.py:270
  34.5 58.9 %copy-start.5 = (bf16[256,256]{1,0:T(8,128)(2,1)S(1)}, bf16[256,256]{1,0:T(8,128)(2,1)}, u32[]{:S(2)}) copy-start(bf16[256,256]{1,0:T(8,128)(2,1)} %constant.51.clone.refs_3_.refs_5_) | copy-start | bytes 393220
  34.5 58.9 %copy-start.6 = (bf16[256,256]{1,0:T(8,128)(2,1)S(1)}, bf16[256,256]{1,0:T(8,128)(2,1)}, u32[]{:S(2)}) copy-start(bf16[256,256]{1,0:T(8,128)(2,1)} %constant.54.clone.refs_6_.refs_7_) | copy-start | bytes 393220
  34.5 26.0 %collective-permute-start.6 = (bf16[8,64,512]{2,1,0:T(8,128)(2,1)S(1)}, bf16[8,64,512]{2,1,0:T(8,128)(2,1)S(1)}, u32[]{:S(2)}, u32[]{:S(2)}) collective-permute-start(bf16[8,64,512]{2,1,0:T(8,128)(2,1)S(1)} %get-tuple-element.22.refs_7_), channel_id=1, source_target_pairs={{0,8},{8,0},{16,24},{24,16},{1,9},{9,1},{17,25},{25,17},{2,10},{10... | collective-permute-start | bytes 1572872 | tf_op jit(solution)/shard_map/ppermute | solution.py:188
  59.0 34.4 %collective-permute-start.4 = (bf16[8,256,128]{2,1,0:T(8,128)(2,1)S(1)}, bf16[8,256,128]{2,1,0:T(8,128)(2,1)S(1)}, u32[]{:S(2)}, u32[]{:S(2)}) collective-permute-start(bf16[8,256,128]{2,1,0:T(8,128)(2,1)S(1)} %pad_maximum_fusion.refs_8_.refs_2_), channel_id=1, source_target_pairs={{0,8},{8,0},{16,24},{24,16},{1,9},{9,1},{17,25},{25,17},{2,10},{10... | collective-permute-start | bytes 1572872 | tf_op jit(solution)/shard_map/ppermute | solution.py:188
  60.6 23.6 %collective-permute-start.7 = (bf16[2,64,512]{2,1,0:T(8,128)(2,1)S(1)}, bf16[2,64,512]{2,1,0:T(8,128)(2,1)S(1)}, u32[]{:S(2)}, u32[]{:S(2)}) collective-permute-start(bf16[2,64,512]{2,1,0:T(8,128)(2,1)S(1)} %get-tuple-element.30), channel_id=1, source_target_pairs={{0,2},{1,3},{2,0},{3,1},{4,6},{5,7},{6,4},{7,5},{8,10},{9,11},{10,... | collective-permute-start | bytes 393224 | tf_op jit(solution)/shard_map/ppermute | solution.py:188
  60.8 25.7 %collective-permute-start.8 = (bf16[2,64,512]{2,1,0:T(8,128)(2,1)S(1)}, bf16[2,64,512]{2,1,0:T(8,128)(2,1)S(1)}, u32[]{:S(2)}, u32[]{:S(2)}) collective-permute-start(bf16[2,64,512]{2,1,0:T(8,128)(2,1)S(1)} %get-tuple-element.31), channel_id=1, source_target_pairs={{0,4},{1,5},{2,6},{3,7},{4,0},{5,1},{6,2},{7,3},{8,12},{9,13},{10,... | collective-permute-start | bytes 393224 | tf_op jit(solution)/shard_map/ppermute | solution.py:188
  63.6 22.9 %collective-permute-start.9 = (bf16[2,64,512]{2,1,0:T(8,128)(2,1)S(1)}, bf16[2,64,512]{2,1,0:T(8,128)(2,1)S(1)}, u32[]{:S(2)}, u32[]{:S(2)}) collective-permute-start(bf16[2,64,512]{2,1,0:T(8,128)(2,1)S(1)} %get-tuple-element.32), channel_id=1, source_target_pairs={{0,6},{1,7},{2,4},{3,5},{4,2},{5,3},{6,0},{7,1},{8,14},{9,15},{10,... | collective-permute-start | bytes 393224 | tf_op jit(solution)/shard_map/ppermute | solution.py:188
  86.6 4.3 %collective-permute-start.11 = (bf16[64,512]{1,0:T(8,128)(2,1)S(1)}, bf16[64,512]{1,0:T(8,128)(2,1)S(1)}, u32[]{:S(2)}, u32[]{:S(2)}) collective-permute-start(bf16[64,512]{1,0:T(8,128)(2,1)S(1)} %get-tuple-element.35), channel_id=1, source_target_pairs={{0,16},{1,17},{2,18},{3,19},{4,20},{5,21},{6,22},{7,23},{8,24},{9,... | collective-permute-start | bytes 196616 | tf_op jit(solution)/shard_map/ppermute | solution.py:194
  88.1 5.2 %collective-permute-start.12 = (bf16[64,512]{1,0:T(8,128)(2,1)S(1)}, bf16[64,512]{1,0:T(8,128)(2,1)S(1)}, u32[]{:S(2)}, u32[]{:S(2)}) collective-permute-start(bf16[64,512]{1,0:T(8,128)(2,1)S(1)} %get-tuple-element.34), channel_id=1, source_target_pairs={{0,17},{1,16},{2,19},{3,18},{4,21},{5,20},{6,23},{7,22},{8,25},{9,... | collective-permute-start | bytes 196616 | tf_op jit(solution)/shard_map/ppermute | solution.py:194
  88.1 5.2 %collective-permute-start.10 = (bf16[64,512]{1,0:T(8,128)(2,1)S(1)}, bf16[64,512]{1,0:T(8,128)(2,1)S(1)}, u32[]{:S(2)}, u32[]{:S(2)}) collective-permute-start(bf16[64,512]{1,0:T(8,128)(2,1)S(1)} %get-tuple-element.34), channel_id=1, source_target_pairs={{0,1},{1,0},{2,3},{3,2},{4,5},{5,4},{6,7},{7,6},{8,9},{9,8},{10,11... | collective-permute-start | bytes 196616 | tf_op jit(solution)/shard_map/ppermute | solution.py:194
  93.3 15.5 %collective-permute-start.13 = (f32[64,512]{1,0:T(8,128)S(1)}, f32[64,512]{1,0:T(8,128)S(1)}, u32[]{:S(2)}, u32[]{:S(2)}) collective-permute-start(f32[64,512]{1,0:T(8,128)S(1)} %get-tuple-element.37), channel_id=1, source_target_pairs={{0,8},{8,0},{16,24},{24,16},{1,9},{9,1},{17,25},{25,17},{2,10},{10... | collective-permute-start | bytes 393224 | tf_op jit(solution)/shard_map/ppermute | solution.py:188
  98.3 6.8 %copy-start.2 = (bf16[128,4096]{1,0:T(8,128)(2,1)S(1)}, bf16[128,4096]{1,0:T(8,128)(2,1)}, u32[]{:S(2)}) copy-start(bf16[128,4096]{1,0:T(8,128)(2,1)} %refs_3_.2) | copy-start | bytes 3145732
  98.3 6.8 %copy-start.3 = (bf16[128,4096]{1,0:T(8,128)(2,1)S(1)}, bf16[128,4096]{1,0:T(8,128)(2,1)}, u32[]{:S(2)}) copy-start(bf16[128,4096]{1,0:T(8,128)(2,1)} %refs_2_.3) | copy-start | bytes 3145732
  98.3 6.8 %copy-start.8 = (bf16[256,256]{1,0:T(8,128)(2,1)S(1)}, bf16[256,256]{1,0:T(8,128)(2,1)}, u32[]{:S(2)}) copy-start(bf16[256,256]{1,0:T(8,128)(2,1)} %constant.53.clone.refs_6_) | copy-start | bytes 393220
  (5 other events, 12.6 us)

commit v2 on v1

v2 whole, which is shorter than its diff:
```python
import functools
import math

import jax
import jax.numpy as jnp
import ml_dtypes
import numpy as np
from jax import lax
from jax.experimental import pallas as pl
from jax.experimental.pallas import tpu as pltpu
from jax.sharding import PartitionSpec as P

BOTH = ("dp", "ctx")
F32 = jnp.float32
BF16 = jnp.bfloat16


def split_bf16(matrix):
    high = matrix.astype(ml_dtypes.bfloat16)
    low = (matrix - high.astype(np.float64)).astype(ml_dtypes.bfloat16)
    return high, low


def transforms(count):
    freq = np.arange(count) + 0.5
    place = np.arange(count)

    def forward(offset):
        angle = np.pi / count * np.outer(freq, place + offset)
        high, low = split_bf16(np.concatenate([np.cos(angle), -np.sin(angle)], 0))
        return np.concatenate([high, low], 1)

    angle = np.pi / count * np.outer(place, freq)
    inverse = np.concatenate([np.cos(angle), -np.sin(angle)], 1) / count
    return forward(0), forward(-count), forward(count), split_bf16(inverse)


def dot(a, b):
    return jnp.dot(a, b, preferred_element_type=F32)


def doubled(block):
    return jnp.concatenate([block, block], 0)


def tap_spectrum(fwd, taps):
    both = jnp.concatenate([taps, taps], 1)
    return lax.dot_general(fwd, both, (((1,), (1,)), ((), ())), preferred_element_type=F32)


def halves(spectrum):
    count = spectrum.shape[0] // 2
    return spectrum[:count], spectrum[count:]


def times(a, b):
    ar, ai = halves(a)
    br, bi = halves(b)
    return jnp.concatenate([ar * br - ai * bi, ar * bi + ai * br], 0)


def times_conj(a, b):
    ar, ai = halves(a)
    br, bi = halves(b)
    return jnp.concatenate([ar * br + ai * bi, ai * br - ar * bi], 0)


def invert(inv, *spectra):
    out = dot(inv, jnp.concatenate([spectrum.astype(BF16) for spectrum in spectra], 0))
    count = out.shape[0] // 2
    return out[:count] + out[count:]


def masked(block, mask):
    return block * mask.astype(BF16)


def masked_inverse(inv, *masks):
    return jnp.concatenate([masked(inv, doubled(mask)) for mask in masks], 1)


def tiles(width, chans):
    tile = max(chans, 1024)
    spans = [(start, min(start + tile, width)) for start in range(0, width, tile)]
    return [(start, stop, range(start // chans, stop // chans)) for start, stop in spans]


def pick(flag, one, other):
    return jnp.where(flag != 0, one, other)


def product(a, b):
    return (a.astype(F32) * b.astype(F32)).astype(BF16)


def my_ctx():
    return lax.axis_index("ctx")


def my_quarter():
    return lax.axis_index("dp") % 4


def my_core():
    return lax.axis_index("dp") % 2


def my_parity():
    return lax.axis_index("ctx") % 2


def start_copy(flag, one, other, target, sem):
    @pl.when(flag != 0)
    def _():
        pltpu.make_async_copy(one, target, sem).start()

    @pl.when(flag == 0)
    def _():
        pltpu.make_async_copy(other, target, sem).start()


def store_when(flag, value, one_ref, other_ref, at):
    @pl.when(flag != 0)
    def _():
        one_ref[:, at] = value

    @pl.when(flag == 0)
    def _():
        other_ref[:, at] = value


def prelude_kernel(
    q_ref, k_ref, v_ref, o_ref, taps_ref, pair_ref, cross_ref, quarter_ref, bufs, tap_buf, sems, tap_sem
):
    split = pair_ref.shape[1]
    share = tap_buf.shape[0]
    rows = pl.ds(pl.multiple_of(my_quarter() * share, share), share)
    tap_copy = pltpu.make_async_copy(taps_ref.at[rows, :], tap_buf, tap_sem)
    spans = tiles(split, 1)
    copies = []
    for i, (start, stop, _) in enumerate(spans):
        at, high = slice(start, stop), slice(split + start, split + stop)
        parts = (k_ref.at[:, at], v_ref.at[:, at], q_ref.at[:, high], o_ref.at[:, high])
        copies.append([pltpu.make_async_copy(part, bufs.at[j, :, at], sems.at[j, i]) for j, part in enumerate(parts)])
    tap_copy.start()
    for group in copies:
        for copy in group:
            copy.start()
    tap_copy.wait()
    quarter_ref[0] = tap_buf[...].astype(quarter_ref.dtype)
    for group, (start, stop, _) in zip(copies, spans):
        at = slice(start, stop)
        for copy in group:
            copy.wait()
        store_when(my_parity(), product(bufs[0, :, at], bufs[1, :, at]), cross_ref, pair_ref, at)
        store_when(my_parity(), product(bufs[2, :, at], bufs[3, :, at]), pair_ref, cross_ref, at)


def masks_kernel(held_ref, docs_ref, out_ref, sent_ref):
    sent_ref[...] = held_ref[...]
    count, rows = docs_ref.shape
    index = lax.axis_index(BOTH)
    own = docs_ref[pl.ds(index, 1), :]
    before = docs_ref[pl.ds(jnp.maximum(index - 1, 0), 1), :]
    after = docs_ref[pl.ds(jnp.minimum(index + 1, count - 1), 1), :]
    first = own == own[:, 0:1]
    last = own == own[:, rows - 1 : rows]
    before = (before == own[:, 0:1]) & (index > 0)
    after = (after == own[:, rows - 1 : rows]) & (index < count - 1)
    lines = [jnp.where(line, 1.0, 0.0) for line in (first, ~first, before, after, last, last, last, last)]
    out_ref[...] = jnp.concatenate(lines, 0).T


def spectra_kernel(
    q_ref, k_ref, v_ref, o_ref, masks_ref, fwd_ref, inv_ref, taps_in,
    lags_ref, xa_ref, xb_ref, ga_ref, gb_ref, pair_ref, cross_ref, taps_out,
):
    taps_out[...] = taps_in[...]
    first, rest = masks_ref[:, 0:1], masks_ref[:, 1:2]
    fwd = fwd_ref[...]
    odd, split = my_parity(), pair_ref.shape[1]
    for start, stop, _ in tiles(lags_ref.shape[1], 1):
        at = slice(start, stop)
        x, g = product(k_ref[:, at], v_ref[:, at]), product(q_ref[:, at], o_ref[:, at])
        if start < split:
            store_when(odd, g, pair_ref, cross_ref, at)
        else:
            store_when(odd, x, cross_ref, pair_ref, slice(start - split, stop - split))
        xa, ga = dot(fwd, doubled(masked(x, first))), dot(fwd, doubled(masked(g, first)))
        xb, gb = dot(fwd, doubled(masked(x, rest))), dot(fwd, doubled(masked(g, rest)))
        xa_ref[:, at], ga_ref[:, at] = xa, ga
        xb_ref[:, at], gb_ref[:, at] = xb, gb
        lags_ref[:, at] = invert(inv_ref[...], times_conj(ga, xa) + times_conj(gb, xb))


def fetch_halo(odd, spans, low_if_odd, low_if_even, halo_ref, sems):
    split = low_if_odd.shape[1]
    for i, (start, stop, _) in enumerate(spans):
        target, sem = halo_ref.at[:, start:stop], sems.at[i]
        if start < split:
            start_copy(odd, low_if_odd.at[:, start:stop], low_if_even.at[:, start:stop], target, sem)
        else:
            high = slice(start - split, stop - split)
            start_copy(odd, low_if_even.at[:, high], low_if_odd.at[:, high], target, sem)

    def wait(i):
        start, stop, _ = spans[i]
        pltpu.make_async_copy(low_if_odd.at[:, 0 : stop - start], halo_ref.at[:, start:stop], sems.at[i]).wait()

    return wait


def lags_kernel(
    pair_ref, cross_ref, held_ref, own_ref, xa_ref, xb_ref, ga_ref, masks_ref,
    prior_fwd_ref, next_fwd_ref, inv_ref, keep_ref, halo_ref, send_ref, sent_ref, sems,
):
    sent_ref[...] = held_ref[...]
    rows = masks_ref.shape[0]
    before, after = masks_ref[:, 2:3], masks_ref[:, 3:4]
    single = masks_ref[rows - 1 : rows, 0:1] > 0.0
    chans, half = keep_ref.shape[2], keep_ref.shape[1]
    me, core = my_ctx(), my_core()
    split = pair_ref.shape[1]
    spans = tiles(2 * split, chans)
    wait = fetch_halo(my_parity(), spans, pair_ref, cross_ref, halo_ref, sems)
    for i, (start, stop, groups) in enumerate(spans):
        at = slice(start, stop)
        wait(i)
        if start < split:
            prior = dot(prior_fwd_ref[...], doubled(masked(halo_ref[:, at], before)))
            spectrum = times_conj(ga_ref[:, at], prior)
        else:
            later = dot(next_fwd_ref[...], doubled(masked(halo_ref[:, at], after)))
            spectrum = times_conj(later, jnp.where(single, xa_ref[:, at], xb_ref[:, at]))
        lags = own_ref[:, at] + invert(inv_ref[...], spectrum)
        low, high = lags[:half], lags[half:]
        keep, send = pick(core, high, low), pick(core, low, high)
        for j, group in enumerate(groups):
            keep_ref[group ^ me] = keep[:, j * chans : (j + 1) * chans]
            send_ref[group ^ me] = send[:, j * chans : (j + 1) * chans].astype(send_ref.dtype)


def middle_kernel(
    halo_ref, k_ref, v_ref, o_ref, xa_ref, xb_ref, ga_ref, gb_ref, mine_ref, other_ref,
    masks_ref, fwd_ref, prior_fwd_ref, next_fwd_ref, inv_ref,
    taps_ref, mixed_ref, back_ref, q_out, k_out, v_out,
):
    first, rest, before, after, last = (masks_ref[:, i : i + 1] for i in range(5))
    inv_two = masked_inverse(inv_ref[...], first, rest)
    inv_three = masked_inverse(inv_ref[...], first, rest, last)
    me, quarter = my_ctx(), my_quarter()
    split = q_out.shape[1]
    chans = 4 * mine_ref.shape[2]
    for start, stop, groups in tiles(2 * split, chans):
        parts = []
        for group in groups:
            for r in range(4):
                place = (r ^ quarter) // 2, group ^ me
                parts.append(pick((r ^ quarter) % 2, other_ref[place], mine_ref[place]))
        at = slice(start, stop)
        taps = tap_spectrum(fwd_ref[...], jnp.concatenate(parts, 0))
        taps_ref[:, at] = taps
        halo = halo_ref[:, at]
        xa, xb, ga, gb = (ref[:, at] for ref in (xa_ref, xb_ref, ga_ref, gb_ref))
        if start < split:
            prior = dot(prior_fwd_ref[...], doubled(masked(halo, before)))
            mixed = invert(inv_two, times(xa + prior, taps), times(xb, taps))
            q_out[:, at] = (o_ref[:, at].astype(F32) * mixed).astype(q_out.dtype)
            back_ref[:, at] = invert(inv_two, times_conj(ga, taps), times_conj(gb, taps))
        else:
            mine = slice(start - split, stop - split)
            later = dot(next_fwd_ref[...], doubled(masked(halo, after)))
            mixed_ref[:, mine] = invert(inv_two, times(xa, taps), times(xb, taps))
            back = invert(inv_three, times_conj(ga, taps), times_conj(gb, taps), times_conj(later, taps))
            k_out[:, mine] = (back * v_ref[:, at].astype(F32)).astype(k_out.dtype)
            v_out[:, mine] = (back * k_ref[:, at].astype(F32)).astype(v_out.dtype)


def last_kernel(
    pair_ref, cross_ref, k_ref, v_ref, o_ref, taps_ref, mixed_ref, back_ref, q_half, k_half, v_half,
    masks_ref, prior_fwd_ref, next_fwd_ref, inv_ref, q_out, k_out, v_out, halo_ref, sems,
):
    first, before, after, last = (masks_ref[:, i : i + 1] for i in (0, 2, 3, 4))
    inv_first = masked_inverse(inv_ref[...], first)
    inv_last = masked_inverse(inv_ref[...], last)
    split = pair_ref.shape[1]
    spans = tiles(2 * split, 1)
    wait = fetch_halo(my_parity(), spans, cross_ref, pair_ref, halo_ref, sems)
    q_out[:, :split] = q_half[...]
    k_out[:, split:] = k_half[...]
    v_out[:, split:] = v_half[...]
    for i, (start, stop, _) in enumerate(spans):
        at = slice(start, stop)
        taps = taps_ref[:, at]
        wait(i)
        if start < split:
            later = dot(next_fwd_ref[...], doubled(masked(halo_ref[:, at], after)))
            back = back_ref[:, at] + invert(inv_last, times_conj(later, taps))
            k_out[:, at] = (back * v_ref[:, at].astype(F32)).astype(k_out.dtype)
            v_out[:, at] = (back * k_ref[:, at].astype(F32)).astype(v_out.dtype)
        else:
            prior = dot(prior_fwd_ref[...], doubled(masked(halo_ref[:, at], before)))
            mixed = mixed_ref[:, start - split : stop - split] + invert(inv_first, times(prior, taps))
            q_out[:, at] = (o_ref[:, at].astype(F32) * mixed).astype(q_out.dtype)


def first_sum_kernel(keep_ref, swapped_ref, own_ref, *send_refs):
    own_ref[...] = keep_ref[:2] + swapped_ref[:2].astype(F32)
    for j, send_ref in enumerate(send_refs):
        at = slice(2 * j + 2, 2 * j + 4)
        send_ref[...] = (keep_ref[at] + swapped_ref[at].astype(F32)).astype(send_ref.dtype)


def second_sum_kernel(count, *refs):
    total = refs[0][...]
    for ref in refs[1:count]:
        total = total + ref[...].astype(F32)
    own_ref, low_ref, high_ref = refs[count:]
    own_ref[...] = total[0]
    low_ref[...] = total[0].astype(low_ref.dtype)
    high_ref[...] = total[1].astype(high_ref.dtype)


def third_sum_kernel(count, *refs):
    total = refs[0][...]
    for ref in refs[1:count]:
        total = total + ref[...].astype(F32)
    for ref in refs[count:]:
        ref[...] = total


def finish_kernel(scale, mine_ref, other_ref, out_ref):
    mine, other = mine_ref[...], other_ref[...]
    core = my_core()
    low = jnp.where(core == 0, mine, other)
    high = jnp.where(core == 0, other, mine)
    out_ref[...] = jnp.concatenate([low, high], 0).T * scale


def swap(value, axis, bit):
    count = lax.axis_size(axis)
    return lax.ppermute(value, axis, [(i, i ^ bit) for i in range(count)])


def cross(value, dp_bits, ctx_bits):
    dp, ctx = lax.axis_size("dp"), lax.axis_size("ctx")
    pairs = [(d * ctx + c, (d ^ dp_bits) * ctx + (c ^ ctx_bits)) for d in range(dp) for c in range(ctx)]
    return lax.ppermute(value, BOTH, pairs)


def bits_of(count):
    assert count & (count - 1) == 0
    return [1 << b for b in range(count.bit_length() - 1)]


def gather_near_taps(mine):
    pair = jnp.concatenate([mine, swap(mine, "ctx", 1)], 0)
    return jnp.concatenate([pair] + [swap(pair, "ctx", j) for j in range(2, lax.axis_size("ctx"), 2)], 0)


def gather_far_taps(near):
    both = jnp.stack([near, swap(near, "dp", 2)])
    return both, swap(both, "dp", 1)


def shards(query_act, key_act, value_act, out_grad, filter_taps, doc_ids):
    rows, width = query_act.shape
    chans, tap_count = filter_taps.shape
    dp, ctx = lax.axis_size("dp"), lax.axis_size("ctx")
    assert rows == tap_count and chans * ctx == width
    scale = 1.0 / math.sqrt(doc_ids.shape[0])
    count = dp * ctx
    fwd, prior_fwd, next_fwd, (inv_high, inv_low) = transforms(tap_count)
    inv = np.concatenate([inv_high, inv_low], 0)
    fwd, prior_fwd, next_fwd, inv = map(jnp.asarray, (fwd, prior_fwd, next_fwd, inv))

    split = width // 2
    pairs = [(i, i ^ 1) for i in range(count)]
    crosses = [(i, i + 1 if i % 2 else i - 1) for i in range(1, count - 1)]
    vmem = pl.BlockSpec(memory_space=pltpu.VMEM)
    anywhere = pl.BlockSpec(memory_space=pl.ANY)
    hbm = pl.BlockSpec(memory_space=pltpu.HBM)
    streamed = pl.BlockSpec()

    def call(kernel, outs, *args, after=(), direct=0, out_specs=None, scratch=(), limit=8):
        read = len(args)
        return pl.pallas_call(
            lambda *refs: kernel(*refs[:read], *refs[read + len(after) :]),
            out_shape=outs,
            in_specs=[hbm] * direct + [vmem] * (read - direct) + [anywhere] * len(after),
            out_specs=jax.tree.map(lambda _: vmem, outs) if out_specs is None else out_specs,
            scratch_shapes=scratch,
            compiler_params=pltpu.CompilerParams(vmem_limit_bytes=limit * 1024 * 1024),
            cost_estimate=pl.CostEstimate(flops=1, bytes_accessed=1, transcendentals=0),
        )(*args, *after)

    sds = jax.ShapeDtypeStruct
    act = sds((rows, width), BF16)
    full = sds((2 * rows, width), F32)
    half_act = sds((rows, split), BF16)
    half_sum = sds((rows, split), F32)
    n_tiles = len(tiles(width, chans))
    buffer = pltpu.VMEM((rows, width), BF16)

    share = chans // 4
    acts = (query_act, key_act, value_act, out_grad)
    sent, held, taps_quarter = call(
        prelude_kernel,
        (half_act, half_act, sds((1, share, tap_count), BF16)),
        *acts, filter_taps,
        direct=5, out_specs=(streamed, vmem, streamed),
        scratch=[
            pltpu.VMEM((4, rows, split), BF16),
            pltpu.VMEM((share, tap_count), F32),
            pltpu.SemaphoreType.DMA((4, n_tiles)),
            pltpu.SemaphoreType.DMA,
        ],
        limit=60,
    )
    pair_early = lax.ppermute(sent, BOTH, pairs)
    taps_near = gather_near_taps(taps_quarter)
    masks, sent = call(
        masks_kernel,
        (sds((rows, 8), F32), half_act),
        held, doc_ids.reshape(-1, rows),
        after=(taps_near, pair_early), out_specs=(vmem, streamed),
    )
    cross_early = lax.ppermute(sent, BOTH, crosses)
    own_lags, xa, xb, ga, gb, held, sent, taps_near = call(
        spectra_kernel,
        (sds((rows, width), F32), full, full, full, full, half_act, half_act, sds(taps_near.shape, BF16)),
        *acts, masks, fwd, inv, taps_near,
        after=(pair_early,), out_specs=(vmem,) * 6 + (streamed,) * 2, limit=16,
    )
    cross_late = lax.ppermute(sent, BOTH, crosses)
    taps_mine, taps_other = gather_far_taps(taps_near)
    keep, halo, send, sent = call(
        lags_kernel,
        (sds((ctx, rows // 2, chans), F32), act, sds((ctx, rows // 2, chans), BF16), half_act),
        pair_early, cross_early, held, own_lags, xa, xb, ga, masks, prior_fwd, next_fwd, inv,
        direct=2, out_specs=(vmem, vmem, streamed, streamed),
        scratch=[pltpu.SemaphoreType.DMA((n_tiles,))], limit=12,
    )
    pair_late = lax.ppermute(sent, BOTH, pairs)
    spectrum, own_mixed, own_back, query_half, key_half, value_half = call(
        middle_kernel,
        (full, half_sum, half_sum, half_act, half_act, half_act),
        halo, key_act, value_act, out_grad, xa, xb, ga, gb, taps_mine, taps_other,
        masks, fwd, prior_fwd, next_fwd, inv,
        after=(send,), limit=16,
    )

    near = [j for j in range(2, ctx, 2)]
    pair = (2, rows // 2, chans)
    own, *sends = call(
        first_sum_kernel,
        (sds(pair, F32),) + (sds(pair, BF16),) * len(near),
        keep, swap(send, "dp", 1),
        after=(cross_late,), out_specs=(vmem,) + (streamed,) * len(near),
    )
    got = [swap(value, "ctx", j) for value, j in zip(sends, near)]
    query_grad, key_grad, value_grad = call(
        last_kernel,
        (act, act, act),
        pair_late, cross_late, key_act, value_act, out_grad, spectrum, own_mixed, own_back,
        query_half, key_half, value_half, masks, prior_fwd, next_fwd, inv,
        direct=2, scratch=[buffer, pltpu.SemaphoreType.DMA((n_tiles,))], limit=12,
    )
    piece = pair[1:]
    own, low, high = call(
        functools.partial(second_sum_kernel, 1 + len(got)),
        (sds(piece, F32), sds(piece, BF16), sds(piece, BF16)),
        own, *got,
        after=(query_half,), out_specs=(vmem, streamed, streamed),
    )
    got = [
        cross(high if j else low, d, j) for d in range(0, dp, 2) for j in (0, 1) if d or j
    ]
    total, total_sent = call(
        functools.partial(third_sum_kernel, 1 + len(got)),
        (sds(piece, F32), sds(piece, F32)),
        own, *got,
        out_specs=(vmem, streamed),
    )
    filter_grad = call(
        functools.partial(finish_kernel, scale), sds((chans, tap_count), F32), total, swap(total_sent, "dp", 1),
    )
    return (query_grad, key_grad, value_grad, filter_grad)


def solution(mesh):
    in_specs = (
        P(BOTH, None),
        P(BOTH, None),
        P(BOTH, None),
        P(BOTH, None),
        P("ctx", None),
        P(),
    )
    out_specs = (
        P(BOTH, None),
        P(BOTH, None),
        P(BOTH, None),
        P("ctx", None),
    )
    return jax.shard_map(shards, mesh=mesh, in_specs=in_specs, out_specs=out_specs, check_vma=False)
```

time: 111 us -> 77.8 us (0.70)
  starting transfers between devices: 43.3 us -> 29.3 us
  waiting for transfers between devices: 29.3 us -> 20.3 us
  other arithmetic: 5.73 us -> 0.05 us
  local copies, waits for them, and re-layouts: 6.22 us -> 3.13 us
    ppermute x9 -> x11, starting transfers between devices: 35.3 us -> 22.2 us  [swap(): return lax.ppermute(value, axis, [(i, i ^ bit) for i in range(count)])]
    ppermute x9 -> x11, waiting for transfers between devices: 26.2 us -> 14.8 us  [swap(): return lax.ppermute(value, axis, [(i, i ^ bit) for i in range(count)])]
    ppermute x2 -> x4, starting transfers between devices: 4.45 us -> 1.45 us  [the longest x1 0.69 us: shards(): cross_early = lax.ppermute(sent, BOTH, crosses)]
    ppermute x3, starting transfers between devices: 3.55 us -> 5.69 us  [cross(): return lax.ppermute(value, BOTH, pairs)]
    ppermute x3, waiting for transfers between devices: 3.07 us -> 5.16 us  [cross(): return lax.ppermute(value, BOTH, pairs)]
    another operation x2 -> x0, local copies, waits for them, and re-layouts: 2.05 us -> none  [document_masks(): return jnp.stack(columns, 1).astype(F32)]
    convert_element_type x3 -> x0, other arithmetic: 2.04 us -> none  [the longest x1 1.79 us: shards(): x = (key_act.astype(F32) * value_act.astype(F32)).astype(BF16)]
    another operation x2 -> x1, other arithmetic: 1.94 us -> 0.05 us  [gather_far_taps(): both = jnp.stack([near, swap(near, 'dp', 2)])]
  transfers between devices with their start and end apart: 14 -> 18, of which waited for: 7 -> 9; matrix products, arithmetic and copies ran while one was open for 9% -> 1% of each run, Pallas kernels for 21% -> 25%
where the time goes in v2:
time: 77.8 us; the launch traced here: 77.5 us
  starting transfers between devices  29.3 us (38%)
  Pallas kernels  23.7 us (30%)
  waiting for transfers between devices  20.3 us (26%)
  local copies, waits for them, and re-layouts  3.13 us (4%)
  between operations  0.9 us (1%)
    pallas_call x10, Pallas kernels, call(): pl.pallas_call(lambda *refs: kernel(*refs[:read], *refs[read + len(after)...  23.7 us
    ppermute x11, starting transfers between devices, swap(): return lax.ppermute(value, axis, [(i, i ^ bit) for i in range(count)])  22.2 us
    ppermute x11, waiting for transfers between devices, swap(): return lax.ppermute(value, axis, [(i, i ^ bit) for i in range(count)])  14.8 us
    ppermute x3, starting transfers between devices, cross(): return lax.ppermute(value, BOTH, pairs)  5.69 us
    ppermute x3, waiting for transfers between devices, cross(): return lax.ppermute(value, BOTH, pairs)  5.16 us
    unnamed x23, local copies, waits for them, and re-layouts  3.1 us
  transfers between devices with their start and end apart: 18, of which 9 were waited for; matrix products, arithmetic and copies ran while one was open for 1% of the time, Pallas kernels for 25%

profile of v2, /device:TPU:0, one launch (start us, length us, event | category | flops | bytes accessed | tf_op | source)
XLA Modules:
  0.0 77.5 jit_solution(9147628801214572241)
XLA Ops:
  0.7 3.2 %shard_map.129 = (bf16[128,2048]{1,0:T(8,128)(2,1)}, bf16[128,2048]{1,0:T(8,128)(2,1)}, bf16[1,128,128]{2,1,0:T(8,128)(2,1)}) custom-call(bf16[128,4096]{1,0:T(8,128)(2,1)} %refs_0_.3, bf16[128,4096]{1,0:T(8,128)(2,1)} %refs_2_.7, bf16[128,4096]{1,0:T(8,128)(2,1)} %refs_3_.7, bf16[128,4096]{1,0:T(8,128)(2,1)} %refs_4_.3, f32[512,128]{1,0:T(8,128)} %refs_4_.2), custom_call_target="tpu_custom_call" | custom-call | flops 1 | bytes 1 | tf_op jit(solution)/shard_map/pallas_call | solution.py:387
  4.0 3.0 %collective-permute-start.1 = (bf16[1,128,128]{2,1,0:T(8,128)(2,1)}, bf16[1,128,128]{2,1,0:T(8,128)(2,1)S(1)}, u32[]{:S(2)}, u32[]{:S(2)}) collective-permute-start(bf16[1,128,128]{2,1,0:T(8,128)(2,1)} %get-tuple-element.41), channel_id=1, source_target_pairs={{0,1},{1,0},{2,3},{3,2},{4,5},{5,4},{6,7},{7,6},{8,9},{9,8},{10,11... | collective-permute-start | bytes 98312 | tf_op jit(solution)/shard_map/ppermute | solution.py:342
  7.8 1.3 %collective-permute-done.1 = bf16[1,128,128]{2,1,0:T(8,128)(2,1)S(1)} collective-permute-done((bf16[1,128,128]{2,1,0:T(8,128)(2,1)}, bf16[1,128,128]{2,1,0:T(8,128)(2,1)S(1)}, u32[]{:S(2)}, u32[]{:S(2)}) %collective-permute-start.1) | collective-permute-done | bytes 32800 | tf_op jit(solution)/shard_map/ppermute | solution.py:342
  9.1 2.4 %collective-permute-start.2 = (bf16[2,128,128]{2,1,0:T(8,128)(2,1)S(1)}, bf16[2,128,128]{2,1,0:T(8,128)(2,1)S(1)}, u32[]{:S(2)}, u32[]{:S(2)}) collective-permute-start(bf16[2,128,128]{2,1,0:T(8,128)(2,1)S(1)} %get-tuple-element.74), channel_id=1, source_target_pairs={{0,2},{1,3},{2,0},{3,1},{4,6},{5,7},{6,4},{7,5},{8,10},{9,11},{10,... | collective-permute-start | bytes 196616 | tf_op jit(solution)/shard_map/ppermute | solution.py:342
  11.5 2.6 %collective-permute-start.3 = (bf16[2,128,128]{2,1,0:T(8,128)(2,1)S(1)}, bf16[2,128,128]{2,1,0:T(8,128)(2,1)S(1)}, u32[]{:S(2)}, u32[]{:S(2)}) collective-permute-start(bf16[2,128,128]{2,1,0:T(8,128)(2,1)S(1)} %get-tuple-element.74), channel_id=1, source_target_pairs={{0,4},{1,5},{2,6},{3,7},{4,0},{5,1},{6,2},{7,3},{8,12},{9,13},{10,... | collective-permute-start | bytes 196616 | tf_op jit(solution)/shard_map/ppermute | solution.py:342
  14.4 3.7 %collective-permute-done.3 = bf16[2,128,128]{2,1,0:T(8,128)(2,1)S(1)} collective-permute-done((bf16[2,128,128]{2,1,0:T(8,128)(2,1)S(1)}, bf16[2,128,128]{2,1,0:T(8,128)(2,1)S(1)}, u32[]{:S(2)}, u32[]{:S(2)}) %collective-permute-start.3) | collective-permute-done | bytes 65568 | tf_op jit(solution)/shard_map/ppermute | solution.py:342
  18.1 2.1 %collective-permute-done.4 = bf16[2,128,128]{2,1,0:T(8,128)(2,1)S(1)} collective-permute-done((bf16[2,128,128]{2,1,0:T(8,128)(2,1)S(1)}, bf16[2,128,128]{2,1,0:T(8,128)(2,1)S(1)}, u32[]{:S(2)}, u32[]{:S(2)}) %collective-permute-start.4) | collective-permute-done | bytes 65568 | tf_op jit(solution)/shard_map/ppermute | solution.py:342
  20.6 1.0 %copy-done.8 = bf16[128,2048]{1,0:T(8,128)(2,1)S(1)} copy-done((bf16[128,2048]{1,0:T(8,128)(2,1)S(1)}, bf16[128,2048]{1,0:T(8,128)(2,1)}, u32[]{:S(2)}) %copy-start.8) | copy-done | bytes 524312
  22.6 1.2 %copy-done.3 = bf16[128,4096]{1,0:T(8,128)(2,1)S(1)} copy-done((bf16[128,4096]{1,0:T(8,128)(2,1)S(1)}, bf16[128,4096]{1,0:T(8,128)(2,1)}, u32[]{:S(2)}) %copy-start.3) | copy-done | bytes 1048600
  23.8 6.0 %shard_map.131 = (f32[128,4096]{1,0:T(8,128)S(1)}, f32[256,4096]{1,0:T(8,128)S(1)}, f32[256,4096]{1,0:T(8,128)S(1)}, f32[256,4096]{1,0:T(8,128)S(1)}, f32[256,40...) custom-call(bf16[128,4096]{1,0:T(8,128)(2,1)S(1)} %copy-done.3, ...), custom_call_target="tpu_custom_call" | custom-call | flops 1 | bytes 1 | tf_op jit(solution)/shard_map/pallas_call | solution.py:387
  29.8 5.3 %collective-permute-start.8 = (bf16[8,128,128]{2,1,0:T(8,128)(2,1)S(1)}, bf16[8,128,128]{2,1,0:T(8,128)(2,1)S(1)}, u32[]{:S(2)}, u32[]{:S(2)}) collective-permute-start(bf16[8,128,128]{2,1,0:T(8,128)(2,1)S(1)} %get-tuple-element.53), channel_id=1, source_target_pairs={{0,16},{8,24},{16,0},{24,8},{1,17},{9,25},{17,1},{25,9},{2,18},{10... | collective-permute-start | bytes 786440 | tf_op jit(solution)/shard_map/ppermute | solution.py:342
  35.8 3.0 %shard_map.132 = (f32[8,64,512]{2,1,0:T(8,128)S(1)}, bf16[128,4096]{1,0:T(8,128)(2,1)S(1)}, bf16[8,64,512]{2,1,0:T(8,128)(2,1)S(1)}, bf16[128,2048]{1,0:T(8,128)(2,1)S(1)}) custom-call(bf16[128,2048]{1,0:T(8,128)(2,1)S(1)} %collective-permute-done.refs_3_.refs_8_.refs_0_, bf16[128,2048]{1,0:T(8,128)(2,1)S(1)} %collective-permute-done.5.refs_1_, ...), custom_call_target="tpu_custom_call" | custom-call | flops 1 | bytes 1 | tf_op jit(solution)/shard_map/pallas_call | solution.py:387
  38.8 3.2 %collective-permute-start.10 = (bf16[8,64,512]{2,1,0:T(8,128)(2,1)S(1)}, bf16[8,64,512]{2,1,0:T(8,128)(2,1)S(1)}, u32[]{:S(2)}, u32[]{:S(2)}) collective-permute-start(bf16[8,64,512]{2,1,0:T(8,128)(2,1)S(1)} %get-tuple-element.54.refs_15_), channel_id=1, source_target_pairs={{0,8},{8,0},{16,24},{24,16},{1,9},{9,1},{17,25},{25,17},{2,10},{10... | collective-permute-start | bytes 1572872 | tf_op jit(solution)/shard_map/ppermute | solution.py:342
  42.0 6.1 %collective-permute-done.8 = bf16[8,128,128]{2,1,0:T(8,128)(2,1)S(1)} collective-permute-done((bf16[8,128,128]{2,1,0:T(8,128)(2,1)S(1)}, bf16[8,128,128]{2,1,0:T(8,128)(2,1)S(1)}, u32[]{:S(2)}, u32[]{:S(2)}) %collective-permute-start.8) | collective-permute-done | bytes 262176 | tf_op jit(solution)/shard_map/ppermute | solution.py:342
  48.2 1.2 %collective-permute-start.9 = (bf16[2,8,128,128]{3,2,1,0:T(8,128)(2,1)S(1)}, bf16[2,8,128,128]{3,2,1,0:T(8,128)(2,1)S(1)}, u32[]{:S(2)}, u32[]{:S(2)}) collective-permute-start(bf16[2,8,128,128]{3,2,1,0:T(8,128)(2,1)S(1)} %pad_maximum_fusion.refs_8_), channel_id=1, source_target_pairs={{0,8},{8,0},{16,24},{24,16},{1,9},{9,1},{17,25},{25,17},{2,10},{10... | collective-permute-start | bytes 1572872 | tf_op jit(solution)/shard_map/ppermute | solution.py:342
  49.4 1.2 %collective-permute-start.11 = (bf16[2,64,512]{2,1,0:T(8,128)(2,1)S(1)}, bf16[2,64,512]{2,1,0:T(8,128)(2,1)S(1)}, u32[]{:S(2)}, u32[]{:S(2)}) collective-permute-start(bf16[2,64,512]{2,1,0:T(8,128)(2,1)S(1)} %get-tuple-element.66), channel_id=1, source_target_pairs={{0,2},{1,3},{2,0},{3,1},{4,6},{5,7},{6,4},{7,5},{8,10},{9,11},{10,... | collective-permute-start | bytes 393224 | tf_op jit(solution)/shard_map/ppermute | solution.py:342
  50.7 2.6 %collective-permute-start.12 = (bf16[2,64,512]{2,1,0:T(8,128)(2,1)S(1)}, bf16[2,64,512]{2,1,0:T(8,128)(2,1)S(1)}, u32[]{:S(2)}, u32[]{:S(2)}) collective-permute-start(bf16[2,64,512]{2,1,0:T(8,128)(2,1)S(1)} %get-tuple-element.67), channel_id=1, source_target_pairs={{0,4},{1,5},{2,6},{3,7},{4,0},{5,1},{6,2},{7,3},{8,12},{9,13},{10,... | collective-permute-start | bytes 393224 | tf_op jit(solution)/shard_map/ppermute | solution.py:342
  53.9 6.2 %shard_map.133 = (f32[256,4096]{1,0:T(8,128)S(1)}, f32[128,2048]{1,0:T(8,128)S(1)}, f32[128,2048]{1,0:T(8,128)S(1)}, bf16[128,2048]{1,0:T(8,128)(2,1)S(1)}, bf16...) custom-call(bf16[128,4096]{1,0:T(8,128)(2,1)S(1)} %get-tuple-element.51.refs_0_, bf16[128,4096]{1,0:T(8,128)(2,1)S(1)} %copy-done, ...), custom_call_target="tpu_custom_call" | custom-call | flops 1 | bytes 1 | tf_op jit(solution)/shard_map/pallas_call | solution.py:387
  60.1 1.3 %collective-permute-done.13.refs_3_ = bf16[2,64,512]{2,1,0:T(8,128)(2,1)S(1)} collective-permute-done((bf16[2,64,512]{2,1,0:T(8,128)(2,1)S(1)}, bf16[2,64,512]{2,1,0:T(8,128)(2,1)S(1)}, u32[]{:S(2)}, u32[]{:S(2)}) %collective-permute-start.13) | collective-permute-done | bytes 131104 | tf_op jit(solution)/shard_map/ppermute | solution.py:342
  61.6 3.1 %collective-permute-start.14 = (bf16[64,512]{1,0:T(8,128)(2,1)S(1)}, bf16[64,512]{1,0:T(8,128)(2,1)S(1)}, u32[]{:S(2)}, u32[]{:S(2)}) collective-permute-start(bf16[64,512]{1,0:T(8,128)(2,1)S(1)} %get-tuple-element.70), channel_id=1, source_target_pairs={{0,1},{1,0},{2,3},{3,2},{4,5},{5,4},{6,7},{7,6},{8,9},{9,8},{10,11... | collective-permute-start | bytes 196616 | tf_op jit(solution)/shard_map/ppermute | solution.py:348
  64.7 2.5 %collective-permute-start.15 = (bf16[64,512]{1,0:T(8,128)(2,1)S(1)}, bf16[64,512]{1,0:T(8,128)(2,1)S(1)}, u32[]{:S(2)}, u32[]{:S(2)}) collective-permute-start(bf16[64,512]{1,0:T(8,128)(2,1)S(1)} %get-tuple-element.71), channel_id=1, source_target_pairs={{0,16},{1,17},{2,18},{3,19},{4,20},{5,21},{6,22},{7,23},{8,24},{9,... | collective-permute-start | bytes 196616 | tf_op jit(solution)/shard_map/ppermute | solution.py:348
  67.2 3.2 %collective-permute-done.15.refs_2_ = bf16[64,512]{1,0:T(8,128)(2,1)S(1)} collective-permute-done((bf16[64,512]{1,0:T(8,128)(2,1)S(1)}, bf16[64,512]{1,0:T(8,128)(2,1)S(1)}, u32[]{:S(2)}, u32[]{:S(2)}) %collective-permute-start.15) | collective-permute-done | bytes 65568 | tf_op jit(solution)/shard_map/ppermute | solution.py:348
  70.5 1.9 %collective-permute-done.16.refs_3_ = bf16[64,512]{1,0:T(8,128)(2,1)S(1)} collective-permute-done((bf16[64,512]{1,0:T(8,128)(2,1)S(1)}, bf16[64,512]{1,0:T(8,128)(2,1)S(1)}, u32[]{:S(2)}, u32[]{:S(2)}) %collective-permute-start.16) | collective-permute-done | bytes 65568 | tf_op jit(solution)/shard_map/ppermute | solution.py:348
  72.5 4.0 %shard_map.134 = (bf16[128,4096]{1,0:T(8,128)(2,1)}, bf16[128,4096]{1,0:T(8,128)(2,1)}, bf16[128,4096]{1,0:T(8,128)(2,1)}) custom-call(bf16[128,2048]{1,0:T(8,128)(2,1)S(1)} %collective-permute-done.6.refs_0_, bf16[128,2048]{1,0:T(8,128)(2,1)S(1)} %collective-permute-done.7.refs_1_.refs_2_, bf16[128,4096]{1,0:T(8,128)(2,1)S(1)} %copy-done, ...), custom_call_target="tpu_custom_call" | custom-call | flops 1 | bytes 1 | tf_op jit(solution)/shard_map/pallas_call | solution.py:387
  (48 shorter events, 5.0 us)
Async XLA Ops:
  0.6 21.9 %copy-start.4 = (bf16[256,256]{1,0:T(8,128)(2,1)S(1)}, bf16[256,256]{1,0:T(8,128)(2,1)}, u32[]{:S(2)}) copy-start(bf16[256,256]{1,0:T(8,128)(2,1)} %constant.11.clone.refs_6_.refs_10_.refs_14_) | copy-start | bytes 393220
  0.6 21.9 %copy-start.7 = (bf16[256,256]{1,0:T(8,128)(2,1)S(1)}, bf16[256,256]{1,0:T(8,128)(2,1)}, u32[]{:S(2)}) copy-start(bf16[256,256]{1,0:T(8,128)(2,1)} %constant.8.clone.refs_5_.refs_11_) | copy-start | bytes 393220
  0.7 21.9 %copy-start = (bf16[128,4096]{1,0:T(8,128)(2,1)S(1)}, bf16[128,4096]{1,0:T(8,128)(2,1)}, u32[]{:S(2)}) copy-start(bf16[128,4096]{1,0:T(8,128)(2,1)} %refs_2_.7) | copy-start | bytes 3145732
  0.7 21.9 %copy-start.1 = (bf16[128,4096]{1,0:T(8,128)(2,1)S(1)}, bf16[128,4096]{1,0:T(8,128)(2,1)}, u32[]{:S(2)}) copy-start(bf16[128,4096]{1,0:T(8,128)(2,1)} %refs_3_.7) | copy-start | bytes 3145732
  3.9 31.9 %copy-start.5 = (bf16[256,256]{1,0:T(8,128)(2,1)S(1)}, bf16[256,256]{1,0:T(8,128)(2,1)}, u32[]{:S(2)}) copy-start(bf16[256,256]{1,0:T(8,128)(2,1)} %constant.10.clone.refs_9_.refs_13_) | copy-start | bytes 393220
  4.0 31.9 %copy-start.6 = (bf16[256,256]{1,0:T(8,128)(2,1)S(1)}, bf16[256,256]{1,0:T(8,128)(2,1)}, u32[]{:S(2)}) copy-start(bf16[256,256]{1,0:T(8,128)(2,1)} %constant.9.clone.refs_8_.refs_12_) | copy-start | bytes 393220
  4.0 5.1 %collective-permute-start.1 = (bf16[1,128,128]{2,1,0:T(8,128)(2,1)}, bf16[1,128,128]{2,1,0:T(8,128)(2,1)S(1)}, u32[]{:S(2)}, u32[]{:S(2)}) collective-permute-start(bf16[1,128,128]{2,1,0:T(8,128)(2,1)} %get-tuple-element.41), channel_id=1, source_target_pairs={{0,1},{1,0},{2,3},{3,2},{4,5},{5,4},{6,7},{7,6},{8,9},{9,8},{10,11... | collective-permute-start | bytes 98312 | tf_op jit(solution)/shard_map/ppermute | solution.py:342
  7.0 13.6 %collective-permute-start = (bf16[128,2048]{1,0:T(8,128)(2,1)}, bf16[128,2048]{1,0:T(8,128)(2,1)S(1)}, u32[]{:S(2)}, u32[]{:S(2)}) collective-permute-start(bf16[128,2048]{1,0:T(8,128)(2,1)} %get-tuple-element.39), channel_id=1, source_target_pairs={{0,1},{1,0},{2,3},{3,2},{4,5},{5,4},{6,7},{7,6},{8,9},{9,8},{10,11... | collective-permute-start | bytes 1572872 | tf_op jit(solution)/shard_map/ppermute | solution.py:420
  9.1 5.3 %collective-permute-start.2 = (bf16[2,128,128]{2,1,0:T(8,128)(2,1)S(1)}, bf16[2,128,128]{2,1,0:T(8,128)(2,1)S(1)}, u32[]{:S(2)}, u32[]{:S(2)}) collective-permute-start(bf16[2,128,128]{2,1,0:T(8,128)(2,1)S(1)} %get-tuple-element.74), channel_id=1, source_target_pairs={{0,2},{1,3},{2,0},{3,1},{4,6},{5,7},{6,4},{7,5},{8,10},{9,11},{10,... | collective-permute-start | bytes 196616 | tf_op jit(solution)/shard_map/ppermute | solution.py:342
  11.5 6.6 %collective-permute-start.3 = (bf16[2,128,128]{2,1,0:T(8,128)(2,1)S(1)}, bf16[2,128,128]{2,1,0:T(8,128)(2,1)S(1)}, u32[]{:S(2)}, u32[]{:S(2)}) collective-permute-start(bf16[2,128,128]{2,1,0:T(8,128)(2,1)S(1)} %get-tuple-element.74), channel_id=1, source_target_pairs={{0,4},{1,5},{2,6},{3,7},{4,0},{5,1},{6,2},{7,3},{8,12},{9,13},{10,... | collective-permute-start | bytes 196616 | tf_op jit(solution)/shard_map/ppermute | solution.py:342
  14.1 6.1 %collective-permute-start.4 = (bf16[2,128,128]{2,1,0:T(8,128)(2,1)S(1)}, bf16[2,128,128]{2,1,0:T(8,128)(2,1)S(1)}, u32[]{:S(2)}, u32[]{:S(2)}) collective-permute-start(bf16[2,128,128]{2,1,0:T(8,128)(2,1)S(1)} %get-tuple-element.74), channel_id=1, source_target_pairs={{0,6},{1,7},{2,4},{3,5},{4,2},{5,3},{6,0},{7,1},{8,14},{9,15},{10,... | collective-permute-start | bytes 196616 | tf_op jit(solution)/shard_map/ppermute | solution.py:342
  21.8 14.0 %collective-permute-start.5 = (bf16[128,2048]{1,0:T(8,128)(2,1)S(1)}, bf16[128,2048]{1,0:T(8,128)(2,1)S(1)}, u32[]{:S(2)}, u32[]{:S(2)}) collective-permute-start(bf16[128,2048]{1,0:T(8,128)(2,1)S(1)} %get-tuple-element.42), channel_id=1, source_target_pairs={{1,2},{2,1},{3,4},{4,3},{5,6},{6,5},{7,8},{8,7},{9,10},{10,9},{11,... | collective-permute-start | bytes 1572872 | tf_op jit(solution)/shard_map/ppermute | solution.py:428
  29.8 18.3 %collective-permute-start.8 = (bf16[8,128,128]{2,1,0:T(8,128)(2,1)S(1)}, bf16[8,128,128]{2,1,0:T(8,128)(2,1)S(1)}, u32[]{:S(2)}, u32[]{:S(2)}) collective-permute-start(bf16[8,128,128]{2,1,0:T(8,128)(2,1)S(1)} %get-tuple-element.53), channel_id=1, source_target_pairs={{0,16},{8,24},{16,0},{24,8},{1,17},{9,25},{17,1},{25,9},{2,18},{10... | collective-permute-start | bytes 786440 | tf_op jit(solution)/shard_map/ppermute | solution.py:342
  35.1 14.2 %collective-permute-start.7 = (bf16[128,2048]{1,0:T(8,128)(2,1)S(1)}, bf16[128,2048]{1,0:T(8,128)(2,1)S(1)}, u32[]{:S(2)}, u32[]{:S(2)}) collective-permute-start(bf16[128,2048]{1,0:T(8,128)(2,1)S(1)} %get-tuple-element.50), channel_id=1, source_target_pairs={{1,2},{2,1},{3,4},{4,3},{5,6},{6,5},{7,8},{8,7},{9,10},{10,9},{11,... | collective-permute-start | bytes 1572872 | tf_op jit(solution)/shard_map/ppermute | solution.py:435
  38.8 10.5 %collective-permute-start.10 = (bf16[8,64,512]{2,1,0:T(8,128)(2,1)S(1)}, bf16[8,64,512]{2,1,0:T(8,128)(2,1)S(1)}, u32[]{:S(2)}, u32[]{:S(2)}) collective-permute-start(bf16[8,64,512]{2,1,0:T(8,128)(2,1)S(1)} %get-tuple-element.54.refs_15_), channel_id=1, source_target_pairs={{0,8},{8,0},{16,24},{24,16},{1,9},{9,1},{17,25},{25,17},{2,10},{10... | collective-permute-start | bytes 1572872 | tf_op jit(solution)/shard_map/ppermute | solution.py:342
  48.2 5.7 %collective-permute-start.9 = (bf16[2,8,128,128]{3,2,1,0:T(8,128)(2,1)S(1)}, bf16[2,8,128,128]{3,2,1,0:T(8,128)(2,1)S(1)}, u32[]{:S(2)}, u32[]{:S(2)}) collective-permute-start(bf16[2,8,128,128]{3,2,1,0:T(8,128)(2,1)S(1)} %pad_maximum_fusion.refs_8_), channel_id=1, source_target_pairs={{0,8},{8,0},{16,24},{24,16},{1,9},{9,1},{17,25},{25,17},{2,10},{10... | collective-permute-start | bytes 1572872 | tf_op jit(solution)/shard_map/ppermute | solution.py:342
  49.3 23.2 %collective-permute-start.6 = (bf16[128,2048]{1,0:T(8,128)(2,1)S(1)}, bf16[128,2048]{1,0:T(8,128)(2,1)S(1)}, u32[]{:S(2)}, u32[]{:S(2)}) collective-permute-start(bf16[128,2048]{1,0:T(8,128)(2,1)S(1)} %get-tuple-element.49), channel_id=1, source_target_pairs={{0,1},{1,0},{2,3},{3,2},{4,5},{5,4},{6,7},{7,6},{8,9},{9,8},{10,11... | collective-permute-start | bytes 1572872 | tf_op jit(solution)/shard_map/ppermute | solution.py:444
  49.4 10.7 %collective-permute-start.11 = (bf16[2,64,512]{2,1,0:T(8,128)(2,1)S(1)}, bf16[2,64,512]{2,1,0:T(8,128)(2,1)S(1)}, u32[]{:S(2)}, u32[]{:S(2)}) collective-permute-start(bf16[2,64,512]{2,1,0:T(8,128)(2,1)S(1)} %get-tuple-element.66), channel_id=1, source_target_pairs={{0,2},{1,3},{2,0},{3,1},{4,6},{5,7},{6,4},{7,5},{8,10},{9,11},{10,... | collective-permute-start | bytes 393224 | tf_op jit(solution)/shard_map/ppermute | solution.py:342
  50.7 9.5 %collective-permute-start.12 = (bf16[2,64,512]{2,1,0:T(8,128)(2,1)S(1)}, bf16[2,64,512]{2,1,0:T(8,128)(2,1)S(1)}, u32[]{:S(2)}, u32[]{:S(2)}) collective-permute-start(bf16[2,64,512]{2,1,0:T(8,128)(2,1)S(1)} %get-tuple-element.67), channel_id=1, source_target_pairs={{0,4},{1,5},{2,6},{3,7},{4,0},{5,1},{6,2},{7,3},{8,12},{9,13},{10,... | collective-permute-start | bytes 393224 | tf_op jit(solution)/shard_map/ppermute | solution.py:342
  53.3 8.2 %collective-permute-start.13 = (bf16[2,64,512]{2,1,0:T(8,128)(2,1)S(1)}, bf16[2,64,512]{2,1,0:T(8,128)(2,1)S(1)}, u32[]{:S(2)}, u32[]{:S(2)}) collective-permute-start(bf16[2,64,512]{2,1,0:T(8,128)(2,1)S(1)} %get-tuple-element.68), channel_id=1, source_target_pairs={{0,6},{1,7},{2,4},{3,5},{4,2},{5,3},{6,0},{7,1},{8,14},{9,15},{10,... | collective-permute-start | bytes 393224 | tf_op jit(solution)/shard_map/ppermute | solution.py:342
  61.6 5.7 %collective-permute-start.14 = (bf16[64,512]{1,0:T(8,128)(2,1)S(1)}, bf16[64,512]{1,0:T(8,128)(2,1)S(1)}, u32[]{:S(2)}, u32[]{:S(2)}) collective-permute-start(bf16[64,512]{1,0:T(8,128)(2,1)S(1)} %get-tuple-element.70), channel_id=1, source_target_pairs={{0,1},{1,0},{2,3},{3,2},{4,5},{5,4},{6,7},{7,6},{8,9},{9,8},{10,11... | collective-permute-start | bytes 196616 | tf_op jit(solution)/shard_map/ppermute | solution.py:348
  64.7 5.8 %collective-permute-start.15 = (bf16[64,512]{1,0:T(8,128)(2,1)S(1)}, bf16[64,512]{1,0:T(8,128)(2,1)S(1)}, u32[]{:S(2)}, u32[]{:S(2)}) collective-permute-start(bf16[64,512]{1,0:T(8,128)(2,1)S(1)} %get-tuple-element.71), channel_id=1, source_target_pairs={{0,16},{1,17},{2,18},{3,19},{4,20},{5,21},{6,22},{7,23},{8,24},{9,... | collective-permute-start | bytes 196616 | tf_op jit(solution)/shard_map/ppermute | solution.py:348
  67.2 5.2 %collective-permute-start.16 = (bf16[64,512]{1,0:T(8,128)(2,1)S(1)}, bf16[64,512]{1,0:T(8,128)(2,1)S(1)}, u32[]{:S(2)}, u32[]{:S(2)}) collective-permute-start(bf16[64,512]{1,0:T(8,128)(2,1)S(1)} %get-tuple-element.70), channel_id=1, source_target_pairs={{0,17},{1,16},{2,19},{3,18},{4,21},{5,20},{6,23},{7,22},{8,25},{9,... | collective-permute-start | bytes 196616 | tf_op jit(solution)/shard_map/ppermute | solution.py:348
  72.4 4.1 %collective-permute-start.17 = (f32[64,512]{1,0:T(8,128)S(1)}, f32[64,512]{1,0:T(8,128)S(1)}, u32[]{:S(2)}, u32[]{:S(2)}) collective-permute-start(f32[64,512]{1,0:T(8,128)S(1)} %get-tuple-element.73), channel_id=1, source_target_pairs={{0,8},{8,0},{16,24},{24,16},{1,9},{9,1},{17,25},{25,17},{2,10},{10... | collective-permute-start | bytes 393224 | tf_op jit(solution)/shard_map/ppermute | solution.py:342
  (4 other events, 44.0 us)

commit v3 on v2

--- a/solution.py
+++ b/solution.py
@@ -119,45 +119,49 @@
         pltpu.make_async_copy(other, target, sem).start()
 
 
-def store_when(flag, value, one_ref, other_ref, at):
-    @pl.when(flag != 0)
-    def _():
-        one_ref[:, at] = value
-
-    @pl.when(flag == 0)
-    def _():
-        other_ref[:, at] = value
-
-
 def prelude_kernel(
-    q_ref, k_ref, v_ref, o_ref, taps_ref, pair_ref, cross_ref, quarter_ref, bufs, tap_buf, sems, tap_sem
+    q_ref, k_ref, v_ref, o_ref, taps_ref, pair_ref, quarter_ref, a_buf, b_buf, tap_buf, sems, tap_sem
 ):
     split = pair_ref.shape[1]
     share = tap_buf.shape[0]
     rows = pl.ds(pl.multiple_of(my_quarter() * share, share), share)
     tap_copy = pltpu.make_async_copy(taps_ref.at[rows, :], tap_buf, tap_sem)
     spans = tiles(split, 1)
-    copies = []
+    odd = my_parity()
     for i, (start, stop, _) in enumerate(spans):
         at, high = slice(start, stop), slice(split + start, split + stop)
-        parts = (k_ref.at[:, at], v_ref.at[:, at], q_ref.at[:, high], o_ref.at[:, high])
-        copies.append([pltpu.make_async_copy(part, bufs.at[j, :, at], sems.at[j, i]) for j, part in enumerate(parts)])
+        start_copy(odd, q_ref.at[:, high], k_ref.at[:, at], a_buf.at[:, at], sems.at[0, i])
+        start_copy(odd, o_ref.at[:, high], v_ref.at[:, at], b_buf.at[:, at], sems.at[1, i])
     tap_copy.start()
-    for group in copies:
-        for copy in group:
-            copy.start()
+    for i, (start, stop, _) in enumerate(spans):
+        at = slice(start, stop)
+        pltpu.make_async_copy(k_ref.at[:, at], a_buf.at[:, at], sems.at[0, i]).wait()
+        pltpu.make_async_copy(v_ref.at[:, at], b_buf.at[:, at], sems.at[1, i]).wait()
+        pair_ref[:, at] = product(a_buf[:, at], b_buf[:, at])
     tap_copy.wait()
     quarter_ref[0] = tap_buf[...].astype(quarter_ref.dtype)
-    for group, (start, stop, _) in zip(copies, spans):
-        at = slice(start, stop)
-        for copy in group:
-            copy.wait()
-        store_when(my_parity(), product(bufs[0, :, at], bufs[1, :, at]), cross_ref, pair_ref, at)
-        store_when(my_parity(), product(bufs[2, :, at], bufs[3, :, at]), pair_ref, cross_ref, at)
-
-
-def masks_kernel(held_ref, docs_ref, out_ref, sent_ref):
-    sent_ref[...] = held_ref[...]
+
+
+def cross_kernel(q_ref, k_ref, v_ref, o_ref, cross_ref):
+    split = cross_ref.shape[1]
+    for start, stop, _ in tiles(split, 1):
+        low, high = slice(start, stop), slice(split + start, split + stop)
+
+        @pl.when(my_parity() != 0)
+        def _():
+            cross_ref[:, low] = product(k_ref[:, low], v_ref[:, low])
+
+        @pl.when(my_parity() == 0)
+        def _():
+            cross_ref[:, low] = product(q_ref[:, high], o_ref[:, high])
+
+
+def late_kernel(q_ref, k_ref, v_ref, o_ref, docs_ref, masks_ref, pair_ref, cross_ref):
+    split = cross_ref.shape[1]
+    for start, stop, _ in tiles(split, 1):
+        low, high = slice(start, stop), slice(split + start, split + stop)
+        store_when(my_parity(), product(k_ref[:, high], v_ref[:, high]), cross_ref, pair_ref, low)
+        store_when(my_parity(), product(q_ref[:, low], o_ref[:, low]), pair_ref, cross_ref, low)
     count, rows = docs_ref.shape
     index = lax.axis_index(BOTH)
     own = docs_ref[pl.ds(index, 1), :]
@@ -168,24 +172,27 @@
     before = (before == own[:, 0:1]) & (index > 0)
     after = (after == own[:, rows - 1 : rows]) & (index < count - 1)
     lines = [jnp.where(line, 1.0, 0.0) for line in (first, ~first, before, after, last, last, last, last)]
-    out_ref[...] = jnp.concatenate(lines, 0).T
+    masks_ref[...] = jnp.concatenate(lines, 0).T
+
+
+def store_when(flag, value, one_ref, other_ref, at):
+    @pl.when(flag != 0)
+    def _():
+        one_ref[:, at] = value
+
+    @pl.when(flag == 0)
+    def _():
+        other_ref[:, at] = value
 
 
 def spectra_kernel(
-    q_ref, k_ref, v_ref, o_ref, masks_ref, fwd_ref, inv_ref, taps_in,
-    lags_ref, xa_ref, xb_ref, ga_ref, gb_ref, pair_ref, cross_ref, taps_out,
+    q_ref, k_ref, v_ref, o_ref, masks_ref, fwd_ref, inv_ref, lags_ref, xa_ref, xb_ref, ga_ref, gb_ref
 ):
-    taps_out[...] = taps_in[...]
     first, rest = masks_ref[:, 0:1], masks_ref[:, 1:2]
     fwd = fwd_ref[...]
-    odd, split = my_parity(), pair_ref.shape[1]
     for start, stop, _ in tiles(lags_ref.shape[1], 1):
         at = slice(start, stop)
         x, g = product(k_ref[:, at], v_ref[:, at]), product(q_ref[:, at], o_ref[:, at])
-        if start < split:
-            store_when(odd, g, pair_ref, cross_ref, at)
-        else:
-            store_when(odd, x, cross_ref, pair_ref, slice(start - split, stop - split))
         xa, ga = dot(fwd, doubled(masked(x, first))), dot(fwd, doubled(masked(g, first)))
         xb, gb = dot(fwd, doubled(masked(x, rest))), dot(fwd, doubled(masked(g, rest)))
         xa_ref[:, at], ga_ref[:, at] = xa, ga
@@ -211,10 +218,10 @@
 
 
 def lags_kernel(
-    pair_ref, cross_ref, held_ref, own_ref, xa_ref, xb_ref, ga_ref, masks_ref,
-    prior_fwd_ref, next_fwd_ref, inv_ref, keep_ref, halo_ref, send_ref, sent_ref, sems,
+    pair_ref, cross_ref, own_ref, xa_ref, xb_ref, ga_ref, masks_ref,
+    prior_fwd_ref, next_fwd_ref, inv_ref, keep_ref, halo_ref, *rest,
 ):
-    sent_ref[...] = held_ref[...]
+    *sends, sems = rest
     rows = masks_ref.shape[0]
     before, after = masks_ref[:, 2:3], masks_ref[:, 3:4]
     single = masks_ref[rows - 1 : rows, 0:1] > 0.0
@@ -237,11 +244,16 @@
         keep, send = pick(core, high, low), pick(core, low, high)
         for j, group in enumerate(groups):
             keep_ref[group ^ me] = keep[:, j * chans : (j + 1) * chans]
-            send_ref[group ^ me] = send[:, j * chans : (j + 1) * chans].astype(send_ref.dtype)
+            place, value = group ^ me, send[:, j * chans : (j + 1) * chans].astype(BF16)
+            for near, send_ref in enumerate(sends):
+
+                @pl.when(place // 2 == near)
+                def _(send_ref=send_ref):
+                    send_ref[place % 2] = value
 
 
 def middle_kernel(
-    halo_ref, k_ref, v_ref, o_ref, xa_ref, xb_ref, ga_ref, gb_ref, mine_ref, other_ref,
+    halo_ref, k_ref, v_ref, o_ref, xa_ref, xb_ref, ga_ref, gb_ref, near_ref, far_ref, other_near_ref, other_far_ref,
     masks_ref, fwd_ref, prior_fwd_ref, next_fwd_ref, inv_ref,
     taps_ref, mixed_ref, back_ref, q_out, k_out, v_out,
 ):
@@ -250,13 +262,15 @@
     inv_three = masked_inverse(inv_ref[...], first, rest, last)
     me, quarter = my_ctx(), my_quarter()
     split = q_out.shape[1]
-    chans = 4 * mine_ref.shape[2]
+    shares = (near_ref, far_ref), (other_near_ref, other_far_ref)
+    chans = 4 * near_ref.shape[1]
     for start, stop, groups in tiles(2 * split, chans):
         parts = []
         for group in groups:
             for r in range(4):
-                place = (r ^ quarter) // 2, group ^ me
-                parts.append(pick((r ^ quarter) % 2, other_ref[place], mine_ref[place]))
+                place = r ^ quarter
+                mine, other = (pick(place // 2, far[group ^ me], near[group ^ me]) for near, far in shares)
+                parts.append(pick(place % 2, other, mine))
         at = slice(start, stop)
         taps = tap_spectrum(fwd_ref[...], jnp.concatenate(parts, 0))
         taps_ref[:, at] = taps
@@ -278,17 +292,25 @@
 
 def last_kernel(
     pair_ref, cross_ref, k_ref, v_ref, o_ref, taps_ref, mixed_ref, back_ref, q_half, k_half, v_half,
-    masks_ref, prior_fwd_ref, next_fwd_ref, inv_ref, q_out, k_out, v_out, halo_ref, sems,
+    masks_ref, prior_fwd_ref, next_fwd_ref, inv_ref, q_out, k_out, v_out, mark_ref,
+    halo_ref, q_buf, k_buf, v_buf, sems, out_sems,
 ):
+    mark_ref[...] = jnp.zeros_like(mark_ref)
     first, before, after, last = (masks_ref[:, i : i + 1] for i in (0, 2, 3, 4))
     inv_first = masked_inverse(inv_ref[...], first)
     inv_last = masked_inverse(inv_ref[...], last)
     split = pair_ref.shape[1]
     spans = tiles(2 * split, 1)
     wait = fetch_halo(my_parity(), spans, cross_ref, pair_ref, halo_ref, sems)
-    q_out[:, :split] = q_half[...]
-    k_out[:, split:] = k_half[...]
-    v_out[:, split:] = v_half[...]
+    copies = []
+
+    def send(source, target):
+        copies.append(pltpu.make_async_copy(source, target, out_sems.at[len(copies)]))
+        copies[-1].start()
+
+    send(q_half, q_out.at[:, :split])
+    send(k_half, k_out.at[:, split:])
+    send(v_half, v_out.at[:, split:])
     for i, (start, stop, _) in enumerate(spans):
         at = slice(start, stop)
         taps = taps_ref[:, at]
@@ -296,19 +318,23 @@
         if start < split:
             later = dot(next_fwd_ref[...], doubled(masked(halo_ref[:, at], after)))
             back = back_ref[:, at] + invert(inv_last, times_conj(later, taps))
-            k_out[:, at] = (back * v_ref[:, at].astype(F32)).astype(k_out.dtype)
-            v_out[:, at] = (back * k_ref[:, at].astype(F32)).astype(v_out.dtype)
+            k_buf[:, at] = (back * v_ref[:, at].astype(F32)).astype(k_buf.dtype)
+            v_buf[:, at] = (back * k_ref[:, at].astype(F32)).astype(v_buf.dtype)
+            send(k_buf.at[:, at], k_out.at[:, at])
+            send(v_buf.at[:, at], v_out.at[:, at])
         else:
+            mine = slice(start - split, stop - split)
             prior = dot(prior_fwd_ref[...], doubled(masked(halo_ref[:, at], before)))
-            mixed = mixed_ref[:, start - split : stop - split] + invert(inv_first, times(prior, taps))
-            q_out[:, at] = (o_ref[:, at].astype(F32) * mixed).astype(q_out.dtype)
-
-
-def first_sum_kernel(keep_ref, swapped_ref, own_ref, *send_refs):
-    own_ref[...] = keep_ref[:2] + swapped_ref[:2].astype(F32)
-    for j, send_ref in enumerate(send_refs):
-        at = slice(2 * j + 2, 2 * j + 4)
-        send_ref[...] = (keep_ref[at] + swapped_ref[at].astype(F32)).astype(send_ref.dtype)
+            mixed = mixed_ref[:, mine] + invert(inv_first, times(prior, taps))
+            q_buf[:, mine] = (o_ref[:, at].astype(F32) * mixed).astype(q_buf.dtype)
+            send(q_buf.at[:, mine], q_out.at[:, at])
+    for copy in copies:
+        copy.wait()
+
+
+def first_sum_kernel(count, keep_ref, *refs):
+    for j, (swapped_ref, out_ref) in enumerate(zip(refs[:count], refs[count:])):
+        out_ref[...] = (keep_ref[2 * j : 2 * j + 2] + swapped_ref[...].astype(F32)).astype(out_ref.dtype)
 
 
 def second_sum_kernel(count, *refs):
@@ -359,8 +385,8 @@
 
 
 def gather_far_taps(near):
-    both = jnp.stack([near, swap(near, "dp", 2)])
-    return both, swap(both, "dp", 1)
+    far = swap(near, "dp", 2)
+    return near, far, swap(near, "dp", 1), swap(far, "dp", 1)
 
 
 def shards(query_act, key_act, value_act, out_grad, filter_taps, doc_ids):
@@ -382,7 +408,7 @@
     hbm = pl.BlockSpec(memory_space=pltpu.HBM)
     streamed = pl.BlockSpec()
 
-    def call(kernel, outs, *args, after=(), direct=0, out_specs=None, scratch=(), limit=8):
+    def call(kernel, outs, *args, after=(), direct=0, out_specs=None, scratch=(), limit=8, flops=1):
         read = len(args)
         return pl.pallas_call(
             lambda *refs: kernel(*refs[:read], *refs[read + len(after) :]),
@@ -391,7 +417,7 @@
             out_specs=jax.tree.map(lambda _: vmem, outs) if out_specs is None else out_specs,
             scratch_shapes=scratch,
             compiler_params=pltpu.CompilerParams(vmem_limit_bytes=limit * 1024 * 1024),
-            cost_estimate=pl.CostEstimate(flops=1, bytes_accessed=1, transcendentals=0),
+            cost_estimate=pl.CostEstimate(flops=flops, bytes_accessed=1, transcendentals=0),
         )(*args, *after)
 
     sds = jax.ShapeDtypeStruct
@@ -404,67 +430,72 @@
 
     share = chans // 4
     acts = (query_act, key_act, value_act, out_grad)
-    sent, held, taps_quarter = call(
+    sent, taps_quarter = call(
         prelude_kernel,
-        (half_act, half_act, sds((1, share, tap_count), BF16)),
+        (half_act, sds((1, share, tap_count), BF16)),
         *acts, filter_taps,
-        direct=5, out_specs=(streamed, vmem, streamed),
+        direct=5, out_specs=(vmem, vmem),
         scratch=[
-            pltpu.VMEM((4, rows, split), BF16),
+            pltpu.VMEM((rows, split), BF16),
+            pltpu.VMEM((rows, split), BF16),
             pltpu.VMEM((share, tap_count), F32),
-            pltpu.SemaphoreType.DMA((4, n_tiles)),
+            pltpu.SemaphoreType.DMA((2, n_tiles)),
             pltpu.SemaphoreType.DMA,
         ],
-        limit=60,
+        limit=56,
     )
     pair_early = lax.ppermute(sent, BOTH, pairs)
     taps_near = gather_near_taps(taps_quarter)
-    masks, sent = call(
-        masks_kernel,
-        (sds((rows, 8), F32), half_act),
-        held, doc_ids.reshape(-1, rows),
-        after=(taps_near, pair_early), out_specs=(vmem, streamed),
-    )
+    sent = call(cross_kernel, half_act, *acts, after=(taps_near, pair_early), out_specs=streamed)
     cross_early = lax.ppermute(sent, BOTH, crosses)
-    own_lags, xa, xb, ga, gb, held, sent, taps_near = call(
+    masks, pair_sent, cross_sent = call(
+        late_kernel,
+        (sds((rows, 8), F32), half_act, half_act),
+        *acts, doc_ids.reshape(-1, rows),
+        after=(sent,), out_specs=(vmem, streamed, streamed),
+    )
+    cross_late = lax.ppermute(cross_sent, BOTH, crosses)
+    pair_late = lax.ppermute(pair_sent, BOTH, pairs)
+    taps_all = gather_far_taps(taps_near)
+    own_lags, xa, xb, ga, gb = call(
         spectra_kernel,
-        (sds((rows, width), F32), full, full, full, full, half_act, half_act, sds(taps_near.shape, BF16)),
-        *acts, masks, fwd, inv, taps_near,
-        after=(pair_early,), out_specs=(vmem,) * 6 + (streamed,) * 2, limit=16,
-    )
-    cross_late = lax.ppermute(sent, BOTH, crosses)
-    taps_mine, taps_other = gather_far_taps(taps_near)
-    keep, halo, send, sent = call(
+        (sds((rows, width), F32), full, full, full, full),
+        *acts, masks, fwd, inv,
+        limit=16,
+    )
+    pair = (2, rows // 2, chans)
+    keep, halo, *sends = call(
         lags_kernel,
-        (sds((ctx, rows // 2, chans), F32), act, sds((ctx, rows // 2, chans), BF16), half_act),
-        pair_early, cross_early, held, own_lags, xa, xb, ga, masks, prior_fwd, next_fwd, inv,
-        direct=2, out_specs=(vmem, vmem, streamed, streamed),
+        (sds((ctx, rows // 2, chans), F32), act) + (sds(pair, BF16),) * (ctx // 2),
+        pair_early, cross_early, own_lags, xa, xb, ga, masks, prior_fwd, next_fwd, inv,
+        direct=2, out_specs=(vmem, vmem) + (streamed,) * (ctx // 2),
         scratch=[pltpu.SemaphoreType.DMA((n_tiles,))], limit=12,
     )
-    pair_late = lax.ppermute(sent, BOTH, pairs)
     spectrum, own_mixed, own_back, query_half, key_half, value_half = call(
         middle_kernel,
         (full, half_sum, half_sum, half_act, half_act, half_act),
-        halo, key_act, value_act, out_grad, xa, xb, ga, gb, taps_mine, taps_other,
+        halo, key_act, value_act, out_grad, xa, xb, ga, gb, *taps_all,
         masks, fwd, prior_fwd, next_fwd, inv,
-        after=(send,), limit=16,
+        after=(sends[0], cross_late), limit=16,
     )
 
     near = [j for j in range(2, ctx, 2)]
-    pair = (2, rows // 2, chans)
     own, *sends = call(
-        first_sum_kernel,
+        functools.partial(first_sum_kernel, ctx // 2),
         (sds(pair, F32),) + (sds(pair, BF16),) * len(near),
-        keep, swap(send, "dp", 1),
-        after=(cross_late,), out_specs=(vmem,) + (streamed,) * len(near),
+        keep, *(swap(value, "dp", 1) for value in sends),
+        out_specs=(vmem,) + (streamed,) * len(near),
     )
     got = [swap(value, "ctx", j) for value, j in zip(sends, near)]
-    query_grad, key_grad, value_grad = call(
+    query_grad, key_grad, value_grad, mark = call(
         last_kernel,
-        (act, act, act),
+        (act, act, act, sds((8, 128), F32)),
         pair_late, cross_late, key_act, value_act, out_grad, spectrum, own_mixed, own_back,
         query_half, key_half, value_half, masks, prior_fwd, next_fwd, inv,
-        direct=2, scratch=[buffer, pltpu.SemaphoreType.DMA((n_tiles,))], limit=12,
+        direct=2, out_specs=(hbm, hbm, hbm, vmem), limit=14,
+        scratch=[buffer]
+        + [pltpu.VMEM((rows, split), BF16)] * 3
+        + [pltpu.SemaphoreType.DMA((n_tiles,)), pltpu.SemaphoreType.DMA((3 + 2 * n_tiles,))],
     )
     piece = pair[1:]
     own, low, high = call(
@@ -474,13 +505,13 @@
         after=(query_half,), out_specs=(vmem, streamed, streamed),
     )
     got = [
-        cross(high if j else low, d, j) for d in range(0, dp, 2) for j in (0, 1) if d or j
+        cross(high if j else low, d, j) for d in reversed(range(0, dp, 2)) for j in (1, 0) if d or j
     ]
     total, total_sent = call(
         functools.partial(third_sum_kernel, 1 + len(got)),
         (sds(piece, F32), sds(piece, F32)),
         own, *got,
-        out_specs=(vmem, streamed),
+        after=(mark,), out_specs=(vmem, streamed),
     )
     filter_grad = call(
         functools.partial(finish_kernel, scale), sds((chans, tap_count), F32), total, swap(total_sent, "dp", 1),

time: 77.8 us -> 70 us (0.90)
  waiting for transfers between devices: 20.3 us -> 14.6 us
  local copies, waits for them, and re-layouts: 3.13 us -> 0.86 us
  starting transfers between devices: 29.3 us -> 31.3 us
  Pallas kernels: 23.7 us -> 21.9 us
    ppermute x3, waiting for transfers between devices: 5.16 us -> 0.01 us  [cross(): return lax.ppermute(value, BOTH, pairs)]
    unnamed x23 -> x21, local copies, waits for them, and re-layouts: 3.1 us -> 0.83 us
    ppermute x2, starting transfers between devices: 0.68 us -> 2.93 us  [the longest x1 2.24 us: shards(): pair_late = lax.ppermute(pair_sent, BOTH, pairs)]
    pallas_call x10 -> x11, Pallas kernels: 23.7 us -> 21.9 us  [call(): pl.pallas_call(lambda *refs: kernel(*refs[:read], *refs[read + len(after)...]
    ppermute x3, starting transfers between devices: 5.69 us -> 3.86 us  [cross(): return lax.ppermute(value, BOTH, pairs)]
    ppermute x11 -> x15, starting transfers between devices: 22.2 us -> 23.7 us  [swap(): return lax.ppermute(value, axis, [(i, i ^ bit) for i in range(count)])]
    ppermute x11 -> x15, waiting for transfers between devices: 14.8 us -> 14.2 us  [swap(): return lax.ppermute(value, axis, [(i, i ^ bit) for i in range(count)])]
  transfers between devices with their start and end apart: 18 -> 22, of which waited for: 9 -> 9; matrix products, arithmetic and copies ran while one was open for 1% -> 1% of each run, Pallas kernels for 25% -> 27%
where the time goes in v3:
time: 70 us; the launch traced here: 69.4 us
  starting transfers between devices  31.3 us (45%)
  Pallas kernels  21.9 us (31%)
  waiting for transfers between devices  14.6 us (21%)
  between operations  0.88 us (1%)
  local copies, waits for them, and re-layouts  0.86 us (1%)
    ppermute x15, starting transfers between devices, swap(): return lax.ppermute(value, axis, [(i, i ^ bit) for i in range(count)])  23.7 us
    pallas_call x11, Pallas kernels, call(): pl.pallas_call(lambda *refs: kernel(*refs[:read], *refs[read + len(after)...  21.9 us
    ppermute x15, waiting for transfers between devices, swap(): return lax.ppermute(value, axis, [(i, i ^ bit) for i in range(count)])  14.2 us
    ppermute x3, starting transfers between devices, cross(): return lax.ppermute(value, BOTH, pairs)  3.86 us
    ppermute x1, starting transfers between devices, shards(): pair_late = lax.ppermute(pair_sent, BOTH, pairs)  2.24 us
  transfers between devices with their start and end apart: 22, of which 9 were waited for; matrix products, arithmetic and copies ran while one was open for 1% of the time, Pallas kernels for 27%

profile of v3, /device:TPU:0, one launch (start us, length us, event | category | flops | bytes accessed | tf_op | source)
XLA Modules:
  0.0 69.4 jit_solution(4223247732277645514)
XLA Ops:
  0.7 2.3 %shard_map.129 = (bf16[128,2048]{1,0:T(8,128)(2,1)}, bf16[1,128,128]{2,1,0:T(8,128)(2,1)}) custom-call(bf16[128,4096]{1,0:T(8,128)(2,1)} %refs_0_.7, bf16[128,4096]{1,0:T(8,128)(2,1)} %refs_2_.11, bf16[128,4096]{1,0:T(8,128)(2,1)} %refs_3_.11, bf16[128,4096]{1,0:T(8,128)(2,1)} %refs_4_.3, f32[512,128]{1,0:T(8,128)} %refs_4_.2), custom_call_target="tpu_custom_call" | custom-call | flops 1 | bytes 1 | tf_op jit(solution)/shard_map/pallas_call | solution.py:413
  3.0 3.0 %collective-permute-start = (bf16[1,128,128]{2,1,0:T(8,128)(2,1)}, bf16[1,128,128]{2,1,0:T(8,128)(2,1)S(1)}, u32[]{:S(2)}, u32[]{:S(2)}) collective-permute-start(bf16[1,128,128]{2,1,0:T(8,128)(2,1)} %get-tuple-element.39), channel_id=1, source_target_pairs={{0,1},{1,0},{2,3},{3,2},{4,5},{5,4},{6,7},{7,6},{8,9},{9,8},{10,11... | collective-permute-start | bytes 98312 | tf_op jit(solution)/shard_map/ppermute | solution.py:368
  6.1 0.8 %constant_dynamic-update-slice_fusion.1 = (bf16[2,128,128]{2,1,0:T(8,128)(2,1)S(1)}, bf16[8,128,128]{2,1,0:T(8,128)(2,1)S(1)}) fusion(bf16[1,128,128]{2,1,0:T(8,128)(2,1)} %get-tuple-element.39), kind=kLoop, calls=%fused_computation.1 | loop fusion | bytes 98304
  6.8 1.3 %collective-permute-done = bf16[1,128,128]{2,1,0:T(8,128)(2,1)S(1)} collective-permute-done((bf16[1,128,128]{2,1,0:T(8,128)(2,1)}, bf16[1,128,128]{2,1,0:T(8,128)(2,1)S(1)}, u32[]{:S(2)}, u32[]{:S(2)}) %collective-permute-start) | collective-permute-done | bytes 32800 | tf_op jit(solution)/shard_map/ppermute | solution.py:368
  8.1 2.4 %collective-permute-start.1 = (bf16[2,128,128]{2,1,0:T(8,128)(2,1)S(1)}, bf16[2,128,128]{2,1,0:T(8,128)(2,1)S(1)}, u32[]{:S(2)}, u32[]{:S(2)}) collective-permute-start(bf16[2,128,128]{2,1,0:T(8,128)(2,1)S(1)} %get-tuple-element.74), channel_id=1, source_target_pairs={{0,2},{1,3},{2,0},{3,1},{4,6},{5,7},{6,4},{7,5},{8,10},{9,11},{10,... | collective-permute-start | bytes 196616 | tf_op jit(solution)/shard_map/ppermute | solution.py:368
  10.5 2.6 %collective-permute-start.2 = (bf16[2,128,128]{2,1,0:T(8,128)(2,1)S(1)}, bf16[2,128,128]{2,1,0:T(8,128)(2,1)S(1)}, u32[]{:S(2)}, u32[]{:S(2)}) collective-permute-start(bf16[2,128,128]{2,1,0:T(8,128)(2,1)S(1)} %get-tuple-element.74), channel_id=1, source_target_pairs={{0,4},{1,5},{2,6},{3,7},{4,0},{5,1},{6,2},{7,3},{8,12},{9,13},{10,... | collective-permute-start | bytes 196616 | tf_op jit(solution)/shard_map/ppermute | solution.py:368
  13.4 3.7 %collective-permute-done.2 = bf16[2,128,128]{2,1,0:T(8,128)(2,1)S(1)} collective-permute-done((bf16[2,128,128]{2,1,0:T(8,128)(2,1)S(1)}, bf16[2,128,128]{2,1,0:T(8,128)(2,1)S(1)}, u32[]{:S(2)}, u32[]{:S(2)}) %collective-permute-start.2) | collective-permute-done | bytes 65568 | tf_op jit(solution)/shard_map/ppermute | solution.py:368
  17.1 2.1 %collective-permute-done.3 = bf16[2,128,128]{2,1,0:T(8,128)(2,1)S(1)} collective-permute-done((bf16[2,128,128]{2,1,0:T(8,128)(2,1)S(1)}, bf16[2,128,128]{2,1,0:T(8,128)(2,1)S(1)}, u32[]{:S(2)}, u32[]{:S(2)}) %collective-permute-start.3) | collective-permute-done | bytes 65568 | tf_op jit(solution)/shard_map/ppermute | solution.py:368
  20.5 5.3 %collective-permute-start.8 = (bf16[8,128,128]{2,1,0:T(8,128)(2,1)S(1)}, bf16[8,128,128]{2,1,0:T(8,128)(2,1)S(1)}, u32[]{:S(2)}, u32[]{:S(2)}) collective-permute-start(bf16[8,128,128]{2,1,0:T(8,128)(2,1)S(1)} %constant_dynamic-update-slice_fusion.2.refs_4_.refs_8_), channel_id=1, source_target_pairs={{0,16},{8,24},{16,0},{24,8},{1,17},{9,25},{17,1},{25,9},{2,18},{10... | collective-permute-start | bytes 786440 | tf_op jit(solution)/shard_map/ppermute | solution.py:368
  27.2 4.7 %shard_map.132 = (f32[128,4096]{1,0:T(8,128)S(1)}, f32[256,4096]{1,0:T(8,128)S(1)}, f32[256,4096]{1,0:T(8,128)S(1)}, f32[256,4096]{1,0:T(8,128)S(1)}, f32[256,4096]{1,0:T(8,128)S(1)}) custom-call(bf16[128,4096]{1,0:T(8,128)(2,1)S(1)} %copy-done.3, bf16[128,4096]{1,0:T(8,128)(2,1)S(1)} %copy-done, bf16[128,4096]{1,0:T(8,128)(2,1)S(1)} %copy-done.1, ...), custom_call_target="tpu_custom_call" | custom-call | flops 1 | bytes 1 | tf_op jit(solution)/shard_map/pallas_call | solution.py:413
  31.9 3.2 %shard_map.133 = (f32[8,64,512]{2,1,0:T(8,128)S(1)}, bf16[128,4096]{1,0:T(8,128)(2,1)S(1)}, bf16[2,64,512]{2,1,0:T(8,128)(2,1)S(1)}, bf16[2,64,512]{2,1,0:T(8,12...) custom-call(bf16[128,2048]{1,0:T(8,128)(2,1)S(1)} %collective-permute-done.4.refs_5_.refs_0_, ...), custom_call_target="tpu_custom_call" | custom-call | flops 1 | bytes 1 | tf_op jit(solution)/shard_map/pallas_call | solution.py:413
  35.1 5.0 %collective-permute-start.11 = (bf16[2,64,512]{2,1,0:T(8,128)(2,1)S(1)}, bf16[2,64,512]{2,1,0:T(8,128)(2,1)S(1)}, u32[]{:S(2)}, u32[]{:S(2)}) collective-permute-start(bf16[2,64,512]{2,1,0:T(8,128)(2,1)S(1)} %get-tuple-element.50.refs_17_), channel_id=1, source_target_pairs={{0,8},{8,0},{16,24},{24,16},{1,9},{9,1},{17,25},{25,17},{2,10},{10... | collective-permute-start | bytes 393224 | tf_op jit(solution)/shard_map/ppermute | solution.py:368
  40.2 2.2 %collective-permute-start.5 = (bf16[128,2048]{1,0:T(8,128)(2,1)S(1)}, bf16[128,2048]{1,0:T(8,128)(2,1)S(1)}, u32[]{:S(2)}, u32[]{:S(2)}) collective-permute-start(bf16[128,2048]{1,0:T(8,128)(2,1)S(1)} %get-tuple-element.41), channel_id=1, source_target_pairs={{0,1},{1,0},{2,3},{3,2},{4,5},{5,4},{6,7},{7,6},{8,9},{9,8},{10,11... | collective-permute-start | bytes 1572872 | tf_op jit(solution)/shard_map/ppermute | solution.py:458
  43.9 1.2 %collective-permute-done.14.refs_4_ = bf16[2,64,512]{2,1,0:T(8,128)(2,1)S(1)} collective-permute-done((bf16[2,64,512]{2,1,0:T(8,128)(2,1)S(1)}, bf16[2,64,512]{2,1,0:T(8,128)(2,1)S(1)}, u32[]{:S(2)}, u32[]{:S(2)}) %collective-permute-start.14) | collective-permute-done | bytes 131104 | tf_op jit(solution)/shard_map/ppermute | solution.py:368
  45.2 1.3 %collective-permute-start.15 = (bf16[2,64,512]{2,1,0:T(8,128)(2,1)S(1)}, bf16[2,64,512]{2,1,0:T(8,128)(2,1)S(1)}, u32[]{:S(2)}, u32[]{:S(2)}) collective-permute-start(bf16[2,64,512]{2,1,0:T(8,128)(2,1)S(1)} %get-tuple-element.65), channel_id=1, source_target_pairs={{0,2},{1,3},{2,0},{3,1},{4,6},{5,7},{6,4},{7,5},{8,10},{9,11},{10,... | collective-permute-start | bytes 393224 | tf_op jit(solution)/shard_map/ppermute | solution.py:368
  46.6 2.3 %collective-permute-start.16 = (bf16[2,64,512]{2,1,0:T(8,128)(2,1)S(1)}, bf16[2,64,512]{2,1,0:T(8,128)(2,1)S(1)}, u32[]{:S(2)}, u32[]{:S(2)}) collective-permute-start(bf16[2,64,512]{2,1,0:T(8,128)(2,1)S(1)} %get-tuple-element.66), channel_id=1, source_target_pairs={{0,4},{1,5},{2,6},{3,7},{4,0},{5,1},{6,2},{7,3},{8,12},{9,13},{10,... | collective-permute-start | bytes 393224 | tf_op jit(solution)/shard_map/ppermute | solution.py:368
  48.9 0.8 %collective-permute-start.17 = (bf16[2,64,512]{2,1,0:T(8,128)(2,1)S(1)}, bf16[2,64,512]{2,1,0:T(8,128)(2,1)S(1)}, u32[]{:S(2)}, u32[]{:S(2)}) collective-permute-start(bf16[2,64,512]{2,1,0:T(8,128)(2,1)S(1)} %get-tuple-element.67), channel_id=1, source_target_pairs={{0,6},{1,7},{2,4},{3,5},{4,2},{5,3},{6,0},{7,1},{8,14},{9,15},{10,... | collective-permute-start | bytes 393224 | tf_op jit(solution)/shard_map/ppermute | solution.py:368
  49.7 6.2 %shard_map.134 = (f32[256,4096]{1,0:T(8,128)S(1)}, f32[128,2048]{1,0:T(8,128)S(1)}, f32[128,2048]{1,0:T(8,128)S(1)}, bf16[128,2048]{1,0:T(8,128)(2,1)S(1)}, bf16...) custom-call(bf16[128,4096]{1,0:T(8,128)(2,1)S(1)} %get-tuple-element.48.refs_0_, bf16[128,4096]{1,0:T(8,128)(2,1)S(1)} %copy-done, ...), custom_call_target="tpu_custom_call" | custom-call | flops 1 | bytes 1 | tf_op jit(solution)/shard_map/pallas_call | solution.py:413
  55.9 3.6 %collective-permute-done.16.refs_2_ = bf16[2,64,512]{2,1,0:T(8,128)(2,1)S(1)} collective-permute-done((bf16[2,64,512]{2,1,0:T(8,128)(2,1)S(1)}, bf16[2,64,512]{2,1,0:T(8,128)(2,1)S(1)}, u32[]{:S(2)}, u32[]{:S(2)}) %collective-permute-start.16) | collective-permute-done | bytes 131104 | tf_op jit(solution)/shard_map/ppermute | solution.py:368
  59.6 3.0 %collective-permute-start.18 = (bf16[64,512]{1,0:T(8,128)(2,1)S(1)}, bf16[64,512]{1,0:T(8,128)(2,1)S(1)}, u32[]{:S(2)}, u32[]{:S(2)}) collective-permute-start(bf16[64,512]{1,0:T(8,128)(2,1)S(1)} %get-tuple-element.69), channel_id=1, source_target_pairs={{0,17},{1,16},{2,19},{3,18},{4,21},{5,20},{6,23},{7,22},{8,25},{9,... | collective-permute-start | bytes 196616 | tf_op jit(solution)/shard_map/ppermute | solution.py:374
  62.5 0.9 %collective-permute-start.20 = (bf16[64,512]{1,0:T(8,128)(2,1)S(1)}, bf16[64,512]{1,0:T(8,128)(2,1)S(1)}, u32[]{:S(2)}, u32[]{:S(2)}) collective-permute-start(bf16[64,512]{1,0:T(8,128)(2,1)S(1)} %get-tuple-element.69), channel_id=1, source_target_pairs={{0,1},{1,0},{2,3},{3,2},{4,5},{5,4},{6,7},{7,6},{8,9},{9,8},{10,11... | collective-permute-start | bytes 196616 | tf_op jit(solution)/shard_map/ppermute | solution.py:374
  63.4 3.7 %shard_map.135 = (bf16[128,4096]{1,0:T(8,128)(2,1)}, bf16[128,4096]{1,0:T(8,128)(2,1)}, bf16[128,4096]{1,0:T(8,128)(2,1)}, f32[8,128]{1,0:T(8,128)S(1)}) custom-call(bf16[128,2048]{1,0:T(8,128)(2,1)S(1)} %collective-permute-done.5.refs_0_, bf16[128,2048]{1,0:T(8,128)(2,1)S(1)} %collective-permute-done.6.refs_18_.refs_1_, bf16[128,4096]{1,0:T(8,128)(2,1)S(1)} %copy-done, ...), custom_call_target="tpu_custom_call" | custom-call | flops 1 | bytes 1 | tf_op jit(solution)/shard_map/pallas_call | solution.py:413
  67.2 1.3 %collective-permute-done.21.refs_1_ = f32[64,512]{1,0:T(8,128)S(1)} collective-permute-done((f32[64,512]{1,0:T(8,128)S(1)}, f32[64,512]{1,0:T(8,128)S(1)}, u32[]{:S(2)}, u32[]{:S(2)}) %collective-permute-start.21) | collective-permute-done | bytes 131104 | tf_op jit(solution)/shard_map/ppermute | solution.py:368
  68.6 0.8 %shard_map.139 = f32[512,128]{1,0:T(8,128)} custom-call(f32[64,512]{1,0:T(8,128)S(1)} %get-tuple-element.72.refs_0_, f32[64,512]{1,0:T(8,128)S(1)} %collective-permute-done.21.refs_1_), custom_call_target="tpu_custom_call" | custom-call | flops 1 | bytes 1 | tf_op jit(solution)/shard_map/pallas_call | solution.py:413
  (54 shorter events, 4.8 us)
Async XLA Ops:
  0.6 18.9 %copy-start.3 = (bf16[128,4096]{1,0:T(8,128)(2,1)S(1)}, bf16[128,4096]{1,0:T(8,128)(2,1)}, u32[]{:S(2)}) copy-start(bf16[128,4096]{1,0:T(8,128)(2,1)} %refs_0_.7) | copy-start | bytes 3145732
  0.7 25.1 %copy-start.8 = (s32[4096]{0:T(1024)S(1)}, s32[4096]{0:T(1024)}, u32[]{:S(2)}) copy-start(s32[4096]{0:T(1024)} %param.15) | copy-start | bytes 49156
  3.0 5.1 %collective-permute-start = (bf16[1,128,128]{2,1,0:T(8,128)(2,1)}, bf16[1,128,128]{2,1,0:T(8,128)(2,1)S(1)}, u32[]{:S(2)}, u32[]{:S(2)}) collective-permute-start(bf16[1,128,128]{2,1,0:T(8,128)(2,1)} %get-tuple-element.39), channel_id=1, source_target_pairs={{0,1},{1,0},{2,3},{3,2},{4,5},{5,4},{6,7},{7,6},{8,9},{9,8},{10,11... | collective-permute-start | bytes 98312 | tf_op jit(solution)/shard_map/ppermute | solution.py:368
  6.0 13.6 %collective-permute-start.4 = (bf16[128,2048]{1,0:T(8,128)(2,1)}, bf16[128,2048]{1,0:T(8,128)(2,1)S(1)}, u32[]{:S(2)}, u32[]{:S(2)}) collective-permute-start(bf16[128,2048]{1,0:T(8,128)(2,1)} %get-tuple-element.40), channel_id=1, source_target_pairs={{0,1},{1,0},{2,3},{3,2},{4,5},{5,4},{6,7},{7,6},{8,9},{9,8},{10,11... | collective-permute-start | bytes 1572872 | tf_op jit(solution)/shard_map/ppermute | solution.py:447
  8.1 5.3 %collective-permute-start.1 = (bf16[2,128,128]{2,1,0:T(8,128)(2,1)S(1)}, bf16[2,128,128]{2,1,0:T(8,128)(2,1)S(1)}, u32[]{:S(2)}, u32[]{:S(2)}) collective-permute-start(bf16[2,128,128]{2,1,0:T(8,128)(2,1)S(1)} %get-tuple-element.74), channel_id=1, source_target_pairs={{0,2},{1,3},{2,0},{3,1},{4,6},{5,7},{6,4},{7,5},{8,10},{9,11},{10,... | collective-permute-start | bytes 196616 | tf_op jit(solution)/shard_map/ppermute | solution.py:368
  10.5 6.6 %collective-permute-start.2 = (bf16[2,128,128]{2,1,0:T(8,128)(2,1)S(1)}, bf16[2,128,128]{2,1,0:T(8,128)(2,1)S(1)}, u32[]{:S(2)}, u32[]{:S(2)}) collective-permute-start(bf16[2,128,128]{2,1,0:T(8,128)(2,1)S(1)} %get-tuple-element.74), channel_id=1, source_target_pairs={{0,4},{1,5},{2,6},{3,7},{4,0},{5,1},{6,2},{7,3},{8,12},{9,13},{10,... | collective-permute-start | bytes 196616 | tf_op jit(solution)/shard_map/ppermute | solution.py:368
  13.1 6.1 %collective-permute-start.3 = (bf16[2,128,128]{2,1,0:T(8,128)(2,1)S(1)}, bf16[2,128,128]{2,1,0:T(8,128)(2,1)S(1)}, u32[]{:S(2)}, u32[]{:S(2)}) collective-permute-start(bf16[2,128,128]{2,1,0:T(8,128)(2,1)S(1)} %get-tuple-element.74), channel_id=1, source_target_pairs={{0,6},{1,7},{2,4},{3,5},{4,2},{5,3},{6,0},{7,1},{8,14},{9,15},{10,... | collective-permute-start | bytes 196616 | tf_op jit(solution)/shard_map/ppermute | solution.py:368
  19.8 12.2 %collective-permute-start.7 = (bf16[128,2048]{1,0:T(8,128)(2,1)S(1)}, bf16[128,2048]{1,0:T(8,128)(2,1)S(1)}, u32[]{:S(2)}, u32[]{:S(2)}) collective-permute-start(bf16[128,2048]{1,0:T(8,128)(2,1)S(1)} %shard_map.130.refs_5_), channel_id=1, source_target_pairs={{1,2},{2,1},{3,4},{4,3},{5,6},{6,5},{7,8},{8,7},{9,10},{10,9},{11,... | collective-permute-start | bytes 1572872 | tf_op jit(solution)/shard_map/ppermute | solution.py:450
  20.5 22.0 %collective-permute-start.8 = (bf16[8,128,128]{2,1,0:T(8,128)(2,1)S(1)}, bf16[8,128,128]{2,1,0:T(8,128)(2,1)S(1)}, u32[]{:S(2)}, u32[]{:S(2)}) collective-permute-start(bf16[8,128,128]{2,1,0:T(8,128)(2,1)S(1)} %constant_dynamic-update-slice_fusion.2.refs_4_.refs_8_), channel_id=1, source_target_pairs={{0,16},{8,24},{16,0},{24,8},{1,17},{9,25},{17,1},{25,9},{2,18},{10... | collective-permute-start | bytes 786440 | tf_op jit(solution)/shard_map/ppermute | solution.py:368
  26.4 23.3 %collective-permute-start.6 = (bf16[128,2048]{1,0:T(8,128)(2,1)S(1)}, bf16[128,2048]{1,0:T(8,128)(2,1)S(1)}, u32[]{:S(2)}, u32[]{:S(2)}) collective-permute-start(bf16[128,2048]{1,0:T(8,128)(2,1)S(1)} %get-tuple-element.42), channel_id=1, source_target_pairs={{1,2},{2,1},{3,4},{4,3},{5,6},{6,5},{7,8},{8,7},{9,10},{10,9},{11,... | collective-permute-start | bytes 1572872 | tf_op jit(solution)/shard_map/ppermute | solution.py:457
  35.1 7.3 %collective-permute-start.11 = (bf16[2,64,512]{2,1,0:T(8,128)(2,1)S(1)}, bf16[2,64,512]{2,1,0:T(8,128)(2,1)S(1)}, u32[]{:S(2)}, u32[]{:S(2)}) collective-permute-start(bf16[2,64,512]{2,1,0:T(8,128)(2,1)S(1)} %get-tuple-element.50.refs_17_), channel_id=1, source_target_pairs={{0,8},{8,0},{16,24},{24,16},{1,9},{9,1},{17,25},{25,17},{2,10},{10... | collective-permute-start | bytes 393224 | tf_op jit(solution)/shard_map/ppermute | solution.py:368
  40.1 2.8 %collective-permute-start.12 = (bf16[2,64,512]{2,1,0:T(8,128)(2,1)S(1)}, bf16[2,64,512]{2,1,0:T(8,128)(2,1)S(1)}, u32[]{:S(2)}, u32[]{:S(2)}) collective-permute-start(bf16[2,64,512]{2,1,0:T(8,128)(2,1)S(1)} %get-tuple-element.61), channel_id=1, source_target_pairs={{0,8},{8,0},{16,24},{24,16},{1,9},{9,1},{17,25},{25,17},{2,10},{10... | collective-permute-start | bytes 393224 | tf_op jit(solution)/shard_map/ppermute | solution.py:368
  40.2 23.2 %collective-permute-start.5 = (bf16[128,2048]{1,0:T(8,128)(2,1)S(1)}, bf16[128,2048]{1,0:T(8,128)(2,1)S(1)}, u32[]{:S(2)}, u32[]{:S(2)}) collective-permute-start(bf16[128,2048]{1,0:T(8,128)(2,1)S(1)} %get-tuple-element.41), channel_id=1, source_target_pairs={{0,1},{1,0},{2,3},{3,2},{4,5},{5,4},{6,7},{7,6},{8,9},{9,8},{10,11... | collective-permute-start | bytes 1572872 | tf_op jit(solution)/shard_map/ppermute | solution.py:458
  42.4 1.3 %collective-permute-start.13 = (bf16[2,64,512]{2,1,0:T(8,128)(2,1)S(1)}, bf16[2,64,512]{2,1,0:T(8,128)(2,1)S(1)}, u32[]{:S(2)}, u32[]{:S(2)}) collective-permute-start(bf16[2,64,512]{2,1,0:T(8,128)(2,1)S(1)} %get-tuple-element.62), channel_id=1, source_target_pairs={{0,8},{8,0},{16,24},{24,16},{1,9},{9,1},{17,25},{25,17},{2,10},{10... | collective-permute-start | bytes 393224 | tf_op jit(solution)/shard_map/ppermute | solution.py:368
  42.5 4.1 %collective-permute-start.9 = (bf16[8,128,128]{2,1,0:T(8,128)(2,1)S(1)}, bf16[8,128,128]{2,1,0:T(8,128)(2,1)S(1)}, u32[]{:S(2)}, u32[]{:S(2)}) collective-permute-start(bf16[8,128,128]{2,1,0:T(8,128)(2,1)S(1)} %constant_dynamic-update-slice_fusion.2.refs_4_.refs_8_), channel_id=1, source_target_pairs={{0,8},{8,0},{16,24},{24,16},{1,9},{9,1},{17,25},{25,17},{2,10},{10... | collective-permute-start | bytes 786440 | tf_op jit(solution)/shard_map/ppermute | solution.py:368
  43.0 5.9 %collective-permute-start.10 = (bf16[8,128,128]{2,1,0:T(8,128)(2,1)S(1)}, bf16[8,128,128]{2,1,0:T(8,128)(2,1)S(1)}, u32[]{:S(2)}, u32[]{:S(2)}) collective-permute-start(bf16[8,128,128]{2,1,0:T(8,128)(2,1)S(1)} %collective-permute-done.8.refs_9_), channel_id=1, source_target_pairs={{0,8},{8,0},{16,24},{24,16},{1,9},{9,1},{17,25},{25,17},{2,10},{10... | collective-permute-start | bytes 786440 | tf_op jit(solution)/shard_map/ppermute | solution.py:368
  43.8 1.3 %collective-permute-start.14 = (bf16[2,64,512]{2,1,0:T(8,128)(2,1)S(1)}, bf16[2,64,512]{2,1,0:T(8,128)(2,1)S(1)}, u32[]{:S(2)}, u32[]{:S(2)}) collective-permute-start(bf16[2,64,512]{2,1,0:T(8,128)(2,1)S(1)} %get-tuple-element.63), channel_id=1, source_target_pairs={{0,8},{8,0},{16,24},{24,16},{1,9},{9,1},{17,25},{25,17},{2,10},{10... | collective-permute-start | bytes 393224 | tf_op jit(solution)/shard_map/ppermute | solution.py:368
  45.2 10.6 %collective-permute-start.15 = (bf16[2,64,512]{2,1,0:T(8,128)(2,1)S(1)}, bf16[2,64,512]{2,1,0:T(8,128)(2,1)S(1)}, u32[]{:S(2)}, u32[]{:S(2)}) collective-permute-start(bf16[2,64,512]{2,1,0:T(8,128)(2,1)S(1)} %get-tuple-element.65), channel_id=1, source_target_pairs={{0,2},{1,3},{2,0},{3,1},{4,6},{5,7},{6,4},{7,5},{8,10},{9,11},{10,... | collective-permute-start | bytes 393224 | tf_op jit(solution)/shard_map/ppermute | solution.py:368
  46.6 12.9 %collective-permute-start.16 = (bf16[2,64,512]{2,1,0:T(8,128)(2,1)S(1)}, bf16[2,64,512]{2,1,0:T(8,128)(2,1)S(1)}, u32[]{:S(2)}, u32[]{:S(2)}) collective-permute-start(bf16[2,64,512]{2,1,0:T(8,128)(2,1)S(1)} %get-tuple-element.66), channel_id=1, source_target_pairs={{0,4},{1,5},{2,6},{3,7},{4,0},{5,1},{6,2},{7,3},{8,12},{9,13},{10,... | collective-permute-start | bytes 393224 | tf_op jit(solution)/shard_map/ppermute | solution.py:368
  48.9 10.6 %collective-permute-start.17 = (bf16[2,64,512]{2,1,0:T(8,128)(2,1)S(1)}, bf16[2,64,512]{2,1,0:T(8,128)(2,1)S(1)}, u32[]{:S(2)}, u32[]{:S(2)}) collective-permute-start(bf16[2,64,512]{2,1,0:T(8,128)(2,1)S(1)} %get-tuple-element.67), channel_id=1, source_target_pairs={{0,6},{1,7},{2,4},{3,5},{4,2},{5,3},{6,0},{7,1},{8,14},{9,15},{10,... | collective-permute-start | bytes 393224 | tf_op jit(solution)/shard_map/ppermute | solution.py:368
  59.6 7.5 %collective-permute-start.18 = (bf16[64,512]{1,0:T(8,128)(2,1)S(1)}, bf16[64,512]{1,0:T(8,128)(2,1)S(1)}, u32[]{:S(2)}, u32[]{:S(2)}) collective-permute-start(bf16[64,512]{1,0:T(8,128)(2,1)S(1)} %get-tuple-element.69), channel_id=1, source_target_pairs={{0,17},{1,16},{2,19},{3,18},{4,21},{5,20},{6,23},{7,22},{8,25},{9,... | collective-permute-start | bytes 196616 | tf_op jit(solution)/shard_map/ppermute | solution.py:374
  62.5 4.6 %collective-permute-start.19 = (bf16[64,512]{1,0:T(8,128)(2,1)S(1)}, bf16[64,512]{1,0:T(8,128)(2,1)S(1)}, u32[]{:S(2)}, u32[]{:S(2)}) collective-permute-start(bf16[64,512]{1,0:T(8,128)(2,1)S(1)} %get-tuple-element.70), channel_id=1, source_target_pairs={{0,16},{1,17},{2,18},{3,19},{4,20},{5,21},{6,22},{7,23},{8,24},{9,... | collective-permute-start | bytes 196616 | tf_op jit(solution)/shard_map/ppermute | solution.py:374
  62.5 4.6 %collective-permute-start.20 = (bf16[64,512]{1,0:T(8,128)(2,1)S(1)}, bf16[64,512]{1,0:T(8,128)(2,1)S(1)}, u32[]{:S(2)}, u32[]{:S(2)}) collective-permute-start(bf16[64,512]{1,0:T(8,128)(2,1)S(1)} %get-tuple-element.69), channel_id=1, source_target_pairs={{0,1},{1,0},{2,3},{3,2},{4,5},{5,4},{6,7},{7,6},{8,9},{9,8},{10,11... | collective-permute-start | bytes 196616 | tf_op jit(solution)/shard_map/ppermute | solution.py:374
  67.2 1.4 %collective-permute-start.21 = (f32[64,512]{1,0:T(8,128)S(1)}, f32[64,512]{1,0:T(8,128)S(1)}, u32[]{:S(2)}, u32[]{:S(2)}) collective-permute-start(f32[64,512]{1,0:T(8,128)S(1)} %get-tuple-element.73), channel_id=1, source_target_pairs={{0,8},{8,0},{16,24},{24,16},{1,9},{9,1},{17,25},{25,17},{2,10},{10... | collective-permute-start | bytes 393224 | tf_op jit(solution)/shard_map/ppermute | solution.py:368
  (7 other events, 84.9 us)

commit v4 on v3

--- a/solution.py
+++ b/solution.py
@@ -200,28 +200,17 @@
         lags_ref[:, at] = invert(inv_ref[...], times_conj(ga, xa) + times_conj(gb, xb))
 
 
-def fetch_halo(odd, spans, low_if_odd, low_if_even, halo_ref, sems):
+def halo_of(low_if_odd, low_if_even, start, stop):
     split = low_if_odd.shape[1]
-    for i, (start, stop, _) in enumerate(spans):
-        target, sem = halo_ref.at[:, start:stop], sems.at[i]
-        if start < split:
-            start_copy(odd, low_if_odd.at[:, start:stop], low_if_even.at[:, start:stop], target, sem)
-        else:
-            high = slice(start - split, stop - split)
-            start_copy(odd, low_if_even.at[:, high], low_if_odd.at[:, high], target, sem)
-
-    def wait(i):
-        start, stop, _ = spans[i]
-        pltpu.make_async_copy(low_if_odd.at[:, 0 : stop - start], halo_ref.at[:, start:stop], sems.at[i]).wait()
-
-    return wait
+    at = slice(start % split, start % split + stop - start)
+    one, two = (low_if_odd, low_if_even) if start < split else (low_if_even, low_if_odd)
+    return pick(my_parity(), one[:, at], two[:, at])
 
 
 def lags_kernel(
     pair_ref, cross_ref, own_ref, xa_ref, xb_ref, ga_ref, masks_ref,
-    prior_fwd_ref, next_fwd_ref, inv_ref, keep_ref, halo_ref, *rest,
+    prior_fwd_ref, next_fwd_ref, inv_ref, keep_ref, halo_ref, *sends,
 ):
-    *sends, sems = rest
     rows = masks_ref.shape[0]
     before, after = masks_ref[:, 2:3], masks_ref[:, 3:4]
     single = masks_ref[rows - 1 : rows, 0:1] > 0.0
@@ -229,15 +218,15 @@
     me, core = my_ctx(), my_core()
     split = pair_ref.shape[1]
     spans = tiles(2 * split, chans)
-    wait = fetch_halo(my_parity(), spans, pair_ref, cross_ref, halo_ref, sems)
-    for i, (start, stop, groups) in enumerate(spans):
+    for start, stop, groups in spans:
         at = slice(start, stop)
-        wait(i)
+        halo = halo_of(pair_ref, cross_ref, start, stop)
+        halo_ref[:, at] = halo
         if start < split:
-            prior = dot(prior_fwd_ref[...], doubled(masked(halo_ref[:, at], before)))
+            prior = dot(prior_fwd_ref[...], doubled(masked(halo, before)))
             spectrum = times_conj(ga_ref[:, at], prior)
         else:
-            later = dot(next_fwd_ref[...], doubled(masked(halo_ref[:, at], after)))
+            later = dot(next_fwd_ref[...], doubled(masked(halo, after)))
             spectrum = times_conj(later, jnp.where(single, xa_ref[:, at], xb_ref[:, at]))
         lags = own_ref[:, at] + invert(inv_ref[...], spectrum)
         low, high = lags[:half], lags[half:]
@@ -293,7 +282,7 @@
 def last_kernel(
     pair_ref, cross_ref, k_ref, v_ref, o_ref, taps_ref, mixed_ref, back_ref, q_half, k_half, v_half,
     masks_ref, prior_fwd_ref, next_fwd_ref, inv_ref, q_out, k_out, v_out, mark_ref,
-    halo_ref, q_buf, k_buf, v_buf, sems, out_sems,
+    q_buf, k_buf, v_buf, out_sems,
 ):
     mark_ref[...] = jnp.zeros_like(mark_ref)
     first, before, after, last = (masks_ref[:, i : i + 1] for i in (0, 2, 3, 4))
@@ -301,7 +290,6 @@
     inv_last = masked_inverse(inv_ref[...], last)
     split = pair_ref.shape[1]
     spans = tiles(2 * split, 1)
-    wait = fetch_halo(my_parity(), spans, cross_ref, pair_ref, halo_ref, sems)
     copies = []
 
     def send(source, target):
@@ -311,12 +299,12 @@
     send(q_half, q_out.at[:, :split])
     send(k_half, k_out.at[:, split:])
     send(v_half, v_out.at[:, split:])
-    for i, (start, stop, _) in enumerate(spans):
+    for start, stop, _ in spans:
         at = slice(start, stop)
         taps = taps_ref[:, at]
-        wait(i)
+        halo = halo_of(cross_ref, pair_ref, start, stop)
         if start < split:
-            later = dot(next_fwd_ref[...], doubled(masked(halo_ref[:, at], after)))
+            later = dot(next_fwd_ref[...], doubled(masked(halo, after)))
             back = back_ref[:, at] + invert(inv_last, times_conj(later, taps))
             k_buf[:, at] = (back * v_ref[:, at].astype(F32)).astype(k_buf.dtype)
             v_buf[:, at] = (back * k_ref[:, at].astype(F32)).astype(v_buf.dtype)
@@ -324,7 +312,7 @@
             send(v_buf.at[:, at], v_out.at[:, at])
         else:
             mine = slice(start - split, stop - split)
-            prior = dot(prior_fwd_ref[...], doubled(masked(halo_ref[:, at], before)))
+            prior = dot(prior_fwd_ref[...], doubled(masked(halo, before)))
             mixed = mixed_ref[:, mine] + invert(inv_first, times(prior, taps))
             q_buf[:, mine] = (o_ref[:, at].astype(F32) * mixed).astype(q_buf.dtype)
             send(q_buf.at[:, mine], q_out.at[:, at])
@@ -426,7 +414,6 @@
     half_act = sds((rows, split), BF16)
     half_sum = sds((rows, split), F32)
     n_tiles = len(tiles(width, chans))
-    buffer = pltpu.VMEM((rows, width), BF16)
 
     share = chans // 4
     acts = (query_act, key_act, value_act, out_grad)
@@ -468,8 +455,7 @@
         lags_kernel,
         (sds((ctx, rows // 2, chans), F32), act) + (sds(pair, BF16),) * (ctx // 2),
         pair_early, cross_early, own_lags, xa, xb, ga, masks, prior_fwd, next_fwd, inv,
-        direct=2, out_specs=(vmem, vmem) + (streamed,) * (ctx // 2),
-        scratch=[pltpu.SemaphoreType.DMA((n_tiles,))], limit=12,
+        out_specs=(vmem, vmem) + (streamed,) * (ctx // 2), limit=12,
     )
     spectrum, own_mixed, own_back, query_half, key_half, value_half = call(
         middle_kernel,
@@ -492,10 +478,8 @@
         (act, act, act, sds((8, 128), F32)),
         pair_late, cross_late, key_act, value_act, out_grad, spectrum, own_mixed, own_back,
         query_half, key_half, value_half, masks, prior_fwd, next_fwd, inv,
-        direct=2, out_specs=(hbm, hbm, hbm, vmem), limit=14,
-        scratch=[buffer]
-        + [pltpu.VMEM((rows, split), BF16)] * 3
-        + [pltpu.SemaphoreType.DMA((n_tiles,)), pltpu.SemaphoreType.DMA((3 + 2 * n_tiles,))],
+        out_specs=(hbm, hbm, hbm, vmem), limit=14,
+        scratch=[pltpu.VMEM((rows, split), BF16)] * 3 + [pltpu.SemaphoreType.DMA((3 + 2 * n_tiles,))],
     )
     piece = pair[1:]
     own, low, high = call(

time: 70 us -> 69.5 us (level)
  Pallas kernels: 21.9 us -> 20.9 us
    pallas_call x11, Pallas kernels: 21.9 us -> 20.9 us  [call(): pl.pallas_call(lambda *refs: kernel(*refs[:read], *refs[read + len(after)...]
  transfers between devices with their start and end apart: 22 -> 22, of which waited for: 9 -> 10; matrix products, arithmetic and copies ran while one was open for 1% -> 1% of each run, Pallas kernels for 27% -> 26%
where the time goes in v4:
time: 69.5 us; the launch traced here: 68.9 us
  starting transfers between devices  31.2 us (45%)
  Pallas kernels  20.9 us (30%)
  waiting for transfers between devices  15 us (22%)
  between operations  0.87 us (1%)
  local copies, waits for them, and re-layouts  0.86 us (1%)
    ppermute x15, starting transfers between devices, swap(): return lax.ppermute(value, axis, [(i, i ^ bit) for i in range(count)])  23.7 us
    pallas_call x11, Pallas kernels, call(): pl.pallas_call(lambda *refs: kernel(*refs[:read], *refs[read + len(after)...  20.9 us
    ppermute x15, waiting for transfers between devices, swap(): return lax.ppermute(value, axis, [(i, i ^ bit) for i in range(count)])  14.2 us
    ppermute x3, starting transfers between devices, cross(): return lax.ppermute(value, BOTH, pairs)  3.85 us
    ppermute x1, starting transfers between devices, shards(): pair_late = lax.ppermute(pair_sent, BOTH, pairs)  2.24 us
  transfers between devices with their start and end apart: 22, of which 10 were waited for; matrix products, arithmetic and copies ran while one was open for 1% of the time, Pallas kernels for 26%

profile of v4, /device:TPU:0, one launch (start us, length us, event | category | flops | bytes accessed | tf_op | source)
XLA Modules:
  0.0 68.9 jit_solution(12339003362718839173)
XLA Ops:
  0.7 2.3 %shard_map.129 = (bf16[128,2048]{1,0:T(8,128)(2,1)}, bf16[1,128,128]{2,1,0:T(8,128)(2,1)}) custom-call(bf16[128,4096]{1,0:T(8,128)(2,1)} %refs_0_.7, bf16[128,4096]{1,0:T(8,128)(2,1)} %refs_2_.11, bf16[128,4096]{1,0:T(8,128)(2,1)} %refs_3_.11, bf16[128,4096]{1,0:T(8,128)(2,1)} %refs_4_.3, f32[512,128]{1,0:T(8,128)} %refs_4_.2), custom_call_target="tpu_custom_call" | custom-call | flops 1 | bytes 1 | tf_op jit(solution)/shard_map/pallas_call | solution.py:401
  3.0 3.0 %collective-permute-start = (bf16[1,128,128]{2,1,0:T(8,128)(2,1)}, bf16[1,128,128]{2,1,0:T(8,128)(2,1)S(1)}, u32[]{:S(2)}, u32[]{:S(2)}) collective-permute-start(bf16[1,128,128]{2,1,0:T(8,128)(2,1)} %get-tuple-element.39), channel_id=1, source_target_pairs={{0,1},{1,0},{2,3},{3,2},{4,5},{5,4},{6,7},{7,6},{8,9},{9,8},{10,11... | collective-permute-start | bytes 98312 | tf_op jit(solution)/shard_map/ppermute | solution.py:356
  6.1 0.8 %constant_dynamic-update-slice_fusion.1 = (bf16[2,128,128]{2,1,0:T(8,128)(2,1)S(1)}, bf16[8,128,128]{2,1,0:T(8,128)(2,1)S(1)}) fusion(bf16[1,128,128]{2,1,0:T(8,128)(2,1)} %get-tuple-element.39), kind=kLoop, calls=%fused_computation.1 | loop fusion | bytes 98304
  6.8 1.3 %collective-permute-done = bf16[1,128,128]{2,1,0:T(8,128)(2,1)S(1)} collective-permute-done((bf16[1,128,128]{2,1,0:T(8,128)(2,1)}, bf16[1,128,128]{2,1,0:T(8,128)(2,1)S(1)}, u32[]{:S(2)}, u32[]{:S(2)}) %collective-permute-start) | collective-permute-done | bytes 32800 | tf_op jit(solution)/shard_map/ppermute | solution.py:356
  8.1 2.4 %collective-permute-start.1 = (bf16[2,128,128]{2,1,0:T(8,128)(2,1)S(1)}, bf16[2,128,128]{2,1,0:T(8,128)(2,1)S(1)}, u32[]{:S(2)}, u32[]{:S(2)}) collective-permute-start(bf16[2,128,128]{2,1,0:T(8,128)(2,1)S(1)} %get-tuple-element.74), channel_id=1, source_target_pairs={{0,2},{1,3},{2,0},{3,1},{4,6},{5,7},{6,4},{7,5},{8,10},{9,11},{10,... | collective-permute-start | bytes 196616 | tf_op jit(solution)/shard_map/ppermute | solution.py:356
  10.5 2.6 %collective-permute-start.2 = (bf16[2,128,128]{2,1,0:T(8,128)(2,1)S(1)}, bf16[2,128,128]{2,1,0:T(8,128)(2,1)S(1)}, u32[]{:S(2)}, u32[]{:S(2)}) collective-permute-start(bf16[2,128,128]{2,1,0:T(8,128)(2,1)S(1)} %get-tuple-element.74), channel_id=1, source_target_pairs={{0,4},{1,5},{2,6},{3,7},{4,0},{5,1},{6,2},{7,3},{8,12},{9,13},{10,... | collective-permute-start | bytes 196616 | tf_op jit(solution)/shard_map/ppermute | solution.py:356
  13.4 3.7 %collective-permute-done.2 = bf16[2,128,128]{2,1,0:T(8,128)(2,1)S(1)} collective-permute-done((bf16[2,128,128]{2,1,0:T(8,128)(2,1)S(1)}, bf16[2,128,128]{2,1,0:T(8,128)(2,1)S(1)}, u32[]{:S(2)}, u32[]{:S(2)}) %collective-permute-start.2) | collective-permute-done | bytes 65568 | tf_op jit(solution)/shard_map/ppermute | solution.py:356
  17.1 2.1 %collective-permute-done.3 = bf16[2,128,128]{2,1,0:T(8,128)(2,1)S(1)} collective-permute-done((bf16[2,128,128]{2,1,0:T(8,128)(2,1)S(1)}, bf16[2,128,128]{2,1,0:T(8,128)(2,1)S(1)}, u32[]{:S(2)}, u32[]{:S(2)}) %collective-permute-start.3) | collective-permute-done | bytes 65568 | tf_op jit(solution)/shard_map/ppermute | solution.py:356
  20.5 5.3 %collective-permute-start.8 = (bf16[8,128,128]{2,1,0:T(8,128)(2,1)S(1)}, bf16[8,128,128]{2,1,0:T(8,128)(2,1)S(1)}, u32[]{:S(2)}, u32[]{:S(2)}) collective-permute-start(bf16[8,128,128]{2,1,0:T(8,128)(2,1)S(1)} %constant_dynamic-update-slice_fusion.2.refs_4_.refs_8_), channel_id=1, source_target_pairs={{0,16},{8,24},{16,0},{24,8},{1,17},{9,25},{17,1},{25,9},{2,18},{10... | collective-permute-start | bytes 786440 | tf_op jit(solution)/shard_map/ppermute | solution.py:356
  27.2 4.7 %shard_map.132 = (f32[128,4096]{1,0:T(8,128)S(1)}, f32[256,4096]{1,0:T(8,128)S(1)}, f32[256,4096]{1,0:T(8,128)S(1)}, f32[256,4096]{1,0:T(8,128)S(1)}, f32[256,4096]{1,0:T(8,128)S(1)}) custom-call(bf16[128,4096]{1,0:T(8,128)(2,1)S(1)} %copy-done.3, bf16[128,4096]{1,0:T(8,128)(2,1)S(1)} %copy-done, bf16[128,4096]{1,0:T(8,128)(2,1)S(1)} %copy-done.1, ...), custom_call_target="tpu_custom_call" | custom-call | flops 1 | bytes 1 | tf_op jit(solution)/shard_map/pallas_call | solution.py:401
  31.9 3.0 %shard_map.133 = (f32[8,64,512]{2,1,0:T(8,128)S(1)}, bf16[128,4096]{1,0:T(8,128)(2,1)S(1)}, bf16[2,64,512]{2,1,0:T(8,128)(2,1)S(1)}, bf16[2,64,512]{2,1,0:T(8,12...) custom-call(bf16[128,2048]{1,0:T(8,128)(2,1)S(1)} %collective-permute-done.4.refs_5_.refs_0_, ...), custom_call_target="tpu_custom_call" | custom-call | flops 1 | bytes 1 | tf_op jit(solution)/shard_map/pallas_call | solution.py:401
  35.0 5.0 %collective-permute-start.11 = (bf16[2,64,512]{2,1,0:T(8,128)(2,1)S(1)}, bf16[2,64,512]{2,1,0:T(8,128)(2,1)S(1)}, u32[]{:S(2)}, u32[]{:S(2)}) collective-permute-start(bf16[2,64,512]{2,1,0:T(8,128)(2,1)S(1)} %get-tuple-element.50.refs_17_), channel_id=1, source_target_pairs={{0,8},{8,0},{16,24},{24,16},{1,9},{9,1},{17,25},{25,17},{2,10},{10... | collective-permute-start | bytes 393224 | tf_op jit(solution)/shard_map/ppermute | solution.py:356
  40.0 2.2 %collective-permute-start.5 = (bf16[128,2048]{1,0:T(8,128)(2,1)S(1)}, bf16[128,2048]{1,0:T(8,128)(2,1)S(1)}, u32[]{:S(2)}, u32[]{:S(2)}) collective-permute-start(bf16[128,2048]{1,0:T(8,128)(2,1)S(1)} %get-tuple-element.41), channel_id=1, source_target_pairs={{0,1},{1,0},{2,3},{3,2},{4,5},{5,4},{6,7},{7,6},{8,9},{9,8},{10,11... | collective-permute-start | bytes 1572872 | tf_op jit(solution)/shard_map/ppermute | solution.py:445
  43.8 1.2 %collective-permute-done.14.refs_4_ = bf16[2,64,512]{2,1,0:T(8,128)(2,1)S(1)} collective-permute-done((bf16[2,64,512]{2,1,0:T(8,128)(2,1)S(1)}, bf16[2,64,512]{2,1,0:T(8,128)(2,1)S(1)}, u32[]{:S(2)}, u32[]{:S(2)}) %collective-permute-start.14) | collective-permute-done | bytes 131104 | tf_op jit(solution)/shard_map/ppermute | solution.py:356
  45.1 1.4 %collective-permute-start.15 = (bf16[2,64,512]{2,1,0:T(8,128)(2,1)S(1)}, bf16[2,64,512]{2,1,0:T(8,128)(2,1)S(1)}, u32[]{:S(2)}, u32[]{:S(2)}) collective-permute-start(bf16[2,64,512]{2,1,0:T(8,128)(2,1)S(1)} %get-tuple-element.65), channel_id=1, source_target_pairs={{0,2},{1,3},{2,0},{3,1},{4,6},{5,7},{6,4},{7,5},{8,10},{9,11},{10,... | collective-permute-start | bytes 393224 | tf_op jit(solution)/shard_map/ppermute | solution.py:356
  46.4 2.3 %collective-permute-start.16 = (bf16[2,64,512]{2,1,0:T(8,128)(2,1)S(1)}, bf16[2,64,512]{2,1,0:T(8,128)(2,1)S(1)}, u32[]{:S(2)}, u32[]{:S(2)}) collective-permute-start(bf16[2,64,512]{2,1,0:T(8,128)(2,1)S(1)} %get-tuple-element.66), channel_id=1, source_target_pairs={{0,4},{1,5},{2,6},{3,7},{4,0},{5,1},{6,2},{7,3},{8,12},{9,13},{10,... | collective-permute-start | bytes 393224 | tf_op jit(solution)/shard_map/ppermute | solution.py:356
  48.7 0.8 %collective-permute-start.17 = (bf16[2,64,512]{2,1,0:T(8,128)(2,1)S(1)}, bf16[2,64,512]{2,1,0:T(8,128)(2,1)S(1)}, u32[]{:S(2)}, u32[]{:S(2)}) collective-permute-start(bf16[2,64,512]{2,1,0:T(8,128)(2,1)S(1)} %get-tuple-element.67), channel_id=1, source_target_pairs={{0,6},{1,7},{2,4},{3,5},{4,2},{5,3},{6,0},{7,1},{8,14},{9,15},{10,... | collective-permute-start | bytes 393224 | tf_op jit(solution)/shard_map/ppermute | solution.py:356
  49.5 6.2 %shard_map.134 = (f32[256,4096]{1,0:T(8,128)S(1)}, f32[128,2048]{1,0:T(8,128)S(1)}, f32[128,2048]{1,0:T(8,128)S(1)}, bf16[128,2048]{1,0:T(8,128)(2,1)S(1)}, bf16...) custom-call(bf16[128,4096]{1,0:T(8,128)(2,1)S(1)} %get-tuple-element.48.refs_0_, bf16[128,4096]{1,0:T(8,128)(2,1)S(1)} %copy-done, ...), custom_call_target="tpu_custom_call" | custom-call | flops 1 | bytes 1 | tf_op jit(solution)/shard_map/pallas_call | solution.py:401
  55.7 3.6 %collective-permute-done.16.refs_2_ = bf16[2,64,512]{2,1,0:T(8,128)(2,1)S(1)} collective-permute-done((bf16[2,64,512]{2,1,0:T(8,128)(2,1)S(1)}, bf16[2,64,512]{2,1,0:T(8,128)(2,1)S(1)}, u32[]{:S(2)}, u32[]{:S(2)}) %collective-permute-start.16) | collective-permute-done | bytes 131104 | tf_op jit(solution)/shard_map/ppermute | solution.py:356
  59.4 3.0 %collective-permute-start.18 = (bf16[64,512]{1,0:T(8,128)(2,1)S(1)}, bf16[64,512]{1,0:T(8,128)(2,1)S(1)}, u32[]{:S(2)}, u32[]{:S(2)}) collective-permute-start(bf16[64,512]{1,0:T(8,128)(2,1)S(1)} %get-tuple-element.69), channel_id=1, source_target_pairs={{0,17},{1,16},{2,19},{3,18},{4,21},{5,20},{6,23},{7,22},{8,25},{9,... | collective-permute-start | bytes 196616 | tf_op jit(solution)/shard_map/ppermute | solution.py:362
  62.4 0.9 %collective-permute-start.20 = (bf16[64,512]{1,0:T(8,128)(2,1)S(1)}, bf16[64,512]{1,0:T(8,128)(2,1)S(1)}, u32[]{:S(2)}, u32[]{:S(2)}) collective-permute-start(bf16[64,512]{1,0:T(8,128)(2,1)S(1)} %get-tuple-element.69), channel_id=1, source_target_pairs={{0,1},{1,0},{2,3},{3,2},{4,5},{5,4},{6,7},{7,6},{8,9},{9,8},{10,11... | collective-permute-start | bytes 196616 | tf_op jit(solution)/shard_map/ppermute | solution.py:362
  63.3 2.9 %shard_map.135 = (bf16[128,4096]{1,0:T(8,128)(2,1)}, bf16[128,4096]{1,0:T(8,128)(2,1)}, bf16[128,4096]{1,0:T(8,128)(2,1)}, f32[8,128]{1,0:T(8,128)S(1)}) custom-call(bf16[128,2048]{1,0:T(8,128)(2,1)S(1)} %collective-permute-done.5.refs_0_, bf16[128,2048]{1,0:T(8,128)(2,1)S(1)} %collective-permute-done.6.refs_18_.refs_1_, bf16[128,4096]{1,0:T(8,128)(2,1)S(1)} %copy-done, ...), custom_call_target="tpu_custom_call" | custom-call | flops 1 | bytes 1 | tf_op jit(solution)/shard_map/pallas_call | solution.py:401
  66.7 1.3 %collective-permute-done.21.refs_1_ = f32[64,512]{1,0:T(8,128)S(1)} collective-permute-done((f32[64,512]{1,0:T(8,128)S(1)}, f32[64,512]{1,0:T(8,128)S(1)}, u32[]{:S(2)}, u32[]{:S(2)}) %collective-permute-start.21) | collective-permute-done | bytes 131104 | tf_op jit(solution)/shard_map/ppermute | solution.py:356
  68.1 0.8 %shard_map.139 = f32[512,128]{1,0:T(8,128)} custom-call(f32[64,512]{1,0:T(8,128)S(1)} %get-tuple-element.72.refs_0_, f32[64,512]{1,0:T(8,128)S(1)} %collective-permute-done.21.refs_1_), custom_call_target="tpu_custom_call" | custom-call | flops 1 | bytes 1 | tf_op jit(solution)/shard_map/pallas_call | solution.py:401
  (54 shorter events, 5.3 us)
Async XLA Ops:
  0.6 18.9 %copy-start.3 = (bf16[128,4096]{1,0:T(8,128)(2,1)S(1)}, bf16[128,4096]{1,0:T(8,128)(2,1)}, u32[]{:S(2)}) copy-start(bf16[128,4096]{1,0:T(8,128)(2,1)} %refs_0_.7) | copy-start | bytes 3145732
  0.7 25.1 %copy-start.8 = (s32[4096]{0:T(1024)S(1)}, s32[4096]{0:T(1024)}, u32[]{:S(2)}) copy-start(s32[4096]{0:T(1024)} %param.15) | copy-start | bytes 49156
  3.0 5.1 %collective-permute-start = (bf16[1,128,128]{2,1,0:T(8,128)(2,1)}, bf16[1,128,128]{2,1,0:T(8,128)(2,1)S(1)}, u32[]{:S(2)}, u32[]{:S(2)}) collective-permute-start(bf16[1,128,128]{2,1,0:T(8,128)(2,1)} %get-tuple-element.39), channel_id=1, source_target_pairs={{0,1},{1,0},{2,3},{3,2},{4,5},{5,4},{6,7},{7,6},{8,9},{9,8},{10,11... | collective-permute-start | bytes 98312 | tf_op jit(solution)/shard_map/ppermute | solution.py:356
  6.0 13.6 %collective-permute-start.4 = (bf16[128,2048]{1,0:T(8,128)(2,1)}, bf16[128,2048]{1,0:T(8,128)(2,1)S(1)}, u32[]{:S(2)}, u32[]{:S(2)}) collective-permute-start(bf16[128,2048]{1,0:T(8,128)(2,1)} %get-tuple-element.40), channel_id=1, source_target_pairs={{0,1},{1,0},{2,3},{3,2},{4,5},{5,4},{6,7},{7,6},{8,9},{9,8},{10,11... | collective-permute-start | bytes 1572872 | tf_op jit(solution)/shard_map/ppermute | solution.py:434
  8.1 5.3 %collective-permute-start.1 = (bf16[2,128,128]{2,1,0:T(8,128)(2,1)S(1)}, bf16[2,128,128]{2,1,0:T(8,128)(2,1)S(1)}, u32[]{:S(2)}, u32[]{:S(2)}) collective-permute-start(bf16[2,128,128]{2,1,0:T(8,128)(2,1)S(1)} %get-tuple-element.74), channel_id=1, source_target_pairs={{0,2},{1,3},{2,0},{3,1},{4,6},{5,7},{6,4},{7,5},{8,10},{9,11},{10,... | collective-permute-start | bytes 196616 | tf_op jit(solution)/shard_map/ppermute | solution.py:356
  10.5 6.6 %collective-permute-start.2 = (bf16[2,128,128]{2,1,0:T(8,128)(2,1)S(1)}, bf16[2,128,128]{2,1,0:T(8,128)(2,1)S(1)}, u32[]{:S(2)}, u32[]{:S(2)}) collective-permute-start(bf16[2,128,128]{2,1,0:T(8,128)(2,1)S(1)} %get-tuple-element.74), channel_id=1, source_target_pairs={{0,4},{1,5},{2,6},{3,7},{4,0},{5,1},{6,2},{7,3},{8,12},{9,13},{10,... | collective-permute-start | bytes 196616 | tf_op jit(solution)/shard_map/ppermute | solution.py:356
  13.1 6.1 %collective-permute-start.3 = (bf16[2,128,128]{2,1,0:T(8,128)(2,1)S(1)}, bf16[2,128,128]{2,1,0:T(8,128)(2,1)S(1)}, u32[]{:S(2)}, u32[]{:S(2)}) collective-permute-start(bf16[2,128,128]{2,1,0:T(8,128)(2,1)S(1)} %get-tuple-element.74), channel_id=1, source_target_pairs={{0,6},{1,7},{2,4},{3,5},{4,2},{5,3},{6,0},{7,1},{8,14},{9,15},{10,... | collective-permute-start | bytes 196616 | tf_op jit(solution)/shard_map/ppermute | solution.py:356
  19.8 12.2 %collective-permute-start.7 = (bf16[128,2048]{1,0:T(8,128)(2,1)S(1)}, bf16[128,2048]{1,0:T(8,128)(2,1)S(1)}, u32[]{:S(2)}, u32[]{:S(2)}) collective-permute-start(bf16[128,2048]{1,0:T(8,128)(2,1)S(1)} %shard_map.130.refs_5_), channel_id=1, source_target_pairs={{1,2},{2,1},{3,4},{4,3},{5,6},{6,5},{7,8},{8,7},{9,10},{10,9},{11,... | collective-permute-start | bytes 1572872 | tf_op jit(solution)/shard_map/ppermute | solution.py:437
  20.5 21.8 %collective-permute-start.8 = (bf16[8,128,128]{2,1,0:T(8,128)(2,1)S(1)}, bf16[8,128,128]{2,1,0:T(8,128)(2,1)S(1)}, u32[]{:S(2)}, u32[]{:S(2)}) collective-permute-start(bf16[8,128,128]{2,1,0:T(8,128)(2,1)S(1)} %constant_dynamic-update-slice_fusion.2.refs_4_.refs_8_), channel_id=1, source_target_pairs={{0,16},{8,24},{16,0},{24,8},{1,17},{9,25},{17,1},{25,9},{2,18},{10... | collective-permute-start | bytes 786440 | tf_op jit(solution)/shard_map/ppermute | solution.py:356
  26.4 23.1 %collective-permute-start.6 = (bf16[128,2048]{1,0:T(8,128)(2,1)S(1)}, bf16[128,2048]{1,0:T(8,128)(2,1)S(1)}, u32[]{:S(2)}, u32[]{:S(2)}) collective-permute-start(bf16[128,2048]{1,0:T(8,128)(2,1)S(1)} %get-tuple-element.42), channel_id=1, source_target_pairs={{1,2},{2,1},{3,4},{4,3},{5,6},{6,5},{7,8},{8,7},{9,10},{10,9},{11,... | collective-permute-start | bytes 1572872 | tf_op jit(solution)/shard_map/ppermute | solution.py:444
  35.0 7.3 %collective-permute-start.11 = (bf16[2,64,512]{2,1,0:T(8,128)(2,1)S(1)}, bf16[2,64,512]{2,1,0:T(8,128)(2,1)S(1)}, u32[]{:S(2)}, u32[]{:S(2)}) collective-permute-start(bf16[2,64,512]{2,1,0:T(8,128)(2,1)S(1)} %get-tuple-element.50.refs_17_), channel_id=1, source_target_pairs={{0,8},{8,0},{16,24},{24,16},{1,9},{9,1},{17,25},{25,17},{2,10},{10... | collective-permute-start | bytes 393224 | tf_op jit(solution)/shard_map/ppermute | solution.py:356
  40.0 2.8 %collective-permute-start.12 = (bf16[2,64,512]{2,1,0:T(8,128)(2,1)S(1)}, bf16[2,64,512]{2,1,0:T(8,128)(2,1)S(1)}, u32[]{:S(2)}, u32[]{:S(2)}) collective-permute-start(bf16[2,64,512]{2,1,0:T(8,128)(2,1)S(1)} %get-tuple-element.61), channel_id=1, source_target_pairs={{0,8},{8,0},{16,24},{24,16},{1,9},{9,1},{17,25},{25,17},{2,10},{10... | collective-permute-start | bytes 393224 | tf_op jit(solution)/shard_map/ppermute | solution.py:356
  40.0 23.2 %collective-permute-start.5 = (bf16[128,2048]{1,0:T(8,128)(2,1)S(1)}, bf16[128,2048]{1,0:T(8,128)(2,1)S(1)}, u32[]{:S(2)}, u32[]{:S(2)}) collective-permute-start(bf16[128,2048]{1,0:T(8,128)(2,1)S(1)} %get-tuple-element.41), channel_id=1, source_target_pairs={{0,1},{1,0},{2,3},{3,2},{4,5},{5,4},{6,7},{7,6},{8,9},{9,8},{10,11... | collective-permute-start | bytes 1572872 | tf_op jit(solution)/shard_map/ppermute | solution.py:445
  42.3 1.3 %collective-permute-start.13 = (bf16[2,64,512]{2,1,0:T(8,128)(2,1)S(1)}, bf16[2,64,512]{2,1,0:T(8,128)(2,1)S(1)}, u32[]{:S(2)}, u32[]{:S(2)}) collective-permute-start(bf16[2,64,512]{2,1,0:T(8,128)(2,1)S(1)} %get-tuple-element.62), channel_id=1, source_target_pairs={{0,8},{8,0},{16,24},{24,16},{1,9},{9,1},{17,25},{25,17},{2,10},{10... | collective-permute-start | bytes 393224 | tf_op jit(solution)/shard_map/ppermute | solution.py:356
  42.3 4.1 %collective-permute-start.9 = (bf16[8,128,128]{2,1,0:T(8,128)(2,1)S(1)}, bf16[8,128,128]{2,1,0:T(8,128)(2,1)S(1)}, u32[]{:S(2)}, u32[]{:S(2)}) collective-permute-start(bf16[8,128,128]{2,1,0:T(8,128)(2,1)S(1)} %constant_dynamic-update-slice_fusion.2.refs_4_.refs_8_), channel_id=1, source_target_pairs={{0,8},{8,0},{16,24},{24,16},{1,9},{9,1},{17,25},{25,17},{2,10},{10... | collective-permute-start | bytes 786440 | tf_op jit(solution)/shard_map/ppermute | solution.py:356
  42.8 5.9 %collective-permute-start.10 = (bf16[8,128,128]{2,1,0:T(8,128)(2,1)S(1)}, bf16[8,128,128]{2,1,0:T(8,128)(2,1)S(1)}, u32[]{:S(2)}, u32[]{:S(2)}) collective-permute-start(bf16[8,128,128]{2,1,0:T(8,128)(2,1)S(1)} %collective-permute-done.8.refs_9_), channel_id=1, source_target_pairs={{0,8},{8,0},{16,24},{24,16},{1,9},{9,1},{17,25},{25,17},{2,10},{10... | collective-permute-start | bytes 786440 | tf_op jit(solution)/shard_map/ppermute | solution.py:356
  43.6 1.3 %collective-permute-start.14 = (bf16[2,64,512]{2,1,0:T(8,128)(2,1)S(1)}, bf16[2,64,512]{2,1,0:T(8,128)(2,1)S(1)}, u32[]{:S(2)}, u32[]{:S(2)}) collective-permute-start(bf16[2,64,512]{2,1,0:T(8,128)(2,1)S(1)} %get-tuple-element.63), channel_id=1, source_target_pairs={{0,8},{8,0},{16,24},{24,16},{1,9},{9,1},{17,25},{25,17},{2,10},{10... | collective-permute-start | bytes 393224 | tf_op jit(solution)/shard_map/ppermute | solution.py:356
  45.1 10.7 %collective-permute-start.15 = (bf16[2,64,512]{2,1,0:T(8,128)(2,1)S(1)}, bf16[2,64,512]{2,1,0:T(8,128)(2,1)S(1)}, u32[]{:S(2)}, u32[]{:S(2)}) collective-permute-start(bf16[2,64,512]{2,1,0:T(8,128)(2,1)S(1)} %get-tuple-element.65), channel_id=1, source_target_pairs={{0,2},{1,3},{2,0},{3,1},{4,6},{5,7},{6,4},{7,5},{8,10},{9,11},{10,... | collective-permute-start | bytes 393224 | tf_op jit(solution)/shard_map/ppermute | solution.py:356
  46.4 12.9 %collective-permute-start.16 = (bf16[2,64,512]{2,1,0:T(8,128)(2,1)S(1)}, bf16[2,64,512]{2,1,0:T(8,128)(2,1)S(1)}, u32[]{:S(2)}, u32[]{:S(2)}) collective-permute-start(bf16[2,64,512]{2,1,0:T(8,128)(2,1)S(1)} %get-tuple-element.66), channel_id=1, source_target_pairs={{0,4},{1,5},{2,6},{3,7},{4,0},{5,1},{6,2},{7,3},{8,12},{9,13},{10,... | collective-permute-start | bytes 393224 | tf_op jit(solution)/shard_map/ppermute | solution.py:356
  48.7 10.6 %collective-permute-start.17 = (bf16[2,64,512]{2,1,0:T(8,128)(2,1)S(1)}, bf16[2,64,512]{2,1,0:T(8,128)(2,1)S(1)}, u32[]{:S(2)}, u32[]{:S(2)}) collective-permute-start(bf16[2,64,512]{2,1,0:T(8,128)(2,1)S(1)} %get-tuple-element.67), channel_id=1, source_target_pairs={{0,6},{1,7},{2,4},{3,5},{4,2},{5,3},{6,0},{7,1},{8,14},{9,15},{10,... | collective-permute-start | bytes 393224 | tf_op jit(solution)/shard_map/ppermute | solution.py:356
  59.4 6.7 %collective-permute-start.18 = (bf16[64,512]{1,0:T(8,128)(2,1)S(1)}, bf16[64,512]{1,0:T(8,128)(2,1)S(1)}, u32[]{:S(2)}, u32[]{:S(2)}) collective-permute-start(bf16[64,512]{1,0:T(8,128)(2,1)S(1)} %get-tuple-element.69), channel_id=1, source_target_pairs={{0,17},{1,16},{2,19},{3,18},{4,21},{5,20},{6,23},{7,22},{8,25},{9,... | collective-permute-start | bytes 196616 | tf_op jit(solution)/shard_map/ppermute | solution.py:362
  62.4 4.3 %collective-permute-start.19 = (bf16[64,512]{1,0:T(8,128)(2,1)S(1)}, bf16[64,512]{1,0:T(8,128)(2,1)S(1)}, u32[]{:S(2)}, u32[]{:S(2)}) collective-permute-start(bf16[64,512]{1,0:T(8,128)(2,1)S(1)} %get-tuple-element.70), channel_id=1, source_target_pairs={{0,16},{1,17},{2,18},{3,19},{4,20},{5,21},{6,22},{7,23},{8,24},{9,... | collective-permute-start | bytes 196616 | tf_op jit(solution)/shard_map/ppermute | solution.py:362
  62.4 4.3 %collective-permute-start.20 = (bf16[64,512]{1,0:T(8,128)(2,1)S(1)}, bf16[64,512]{1,0:T(8,128)(2,1)S(1)}, u32[]{:S(2)}, u32[]{:S(2)}) collective-permute-start(bf16[64,512]{1,0:T(8,128)(2,1)S(1)} %get-tuple-element.69), channel_id=1, source_target_pairs={{0,1},{1,0},{2,3},{3,2},{4,5},{5,4},{6,7},{7,6},{8,9},{9,8},{10,11... | collective-permute-start | bytes 196616 | tf_op jit(solution)/shard_map/ppermute | solution.py:362
  66.7 1.4 %collective-permute-start.21 = (f32[64,512]{1,0:T(8,128)S(1)}, f32[64,512]{1,0:T(8,128)S(1)}, u32[]{:S(2)}, u32[]{:S(2)}) collective-permute-start(f32[64,512]{1,0:T(8,128)S(1)} %get-tuple-element.73), channel_id=1, source_target_pairs={{0,8},{8,0},{16,24},{24,16},{1,9},{9,1},{17,25},{25,17},{2,10},{10... | collective-permute-start | bytes 393224 | tf_op jit(solution)/shard_map/ppermute | solution.py:356
  (7 other events, 84.9 us)

commit v5 on v4

--- a/solution.py
+++ b/solution.py
@@ -472,7 +472,8 @@
         keep, *(swap(value, "dp", 1) for value in sends),
         out_specs=(vmem,) + (streamed,) * len(near),
     )
-    got = [swap(value, "ctx", j) for value, j in zip(sends, near)]
+    routes = list(zip(sends, near))
+    got = [swap(value, "ctx", j) for value, j in routes[1:] + routes[:1]]
     query_grad, key_grad, value_grad, mark = call(
         last_kernel,
         (act, act, act, sds((8, 128), F32)),

time: 69.5 us -> 68.6 us (0.987)
    ppermute x15, starting transfers between devices: 23.7 us -> 23 us  [swap(): return lax.ppermute(value, axis, [(i, i ^ bit) for i in range(count)])]
  transfers between devices with their start and end apart: 22 -> 22, of which waited for: 10 -> 11; matrix products, arithmetic and copies ran while one was open for 1% -> 1% of each run, Pallas kernels for 26% -> 26%
where the time goes in v5:
time: 68.6 us; the launch traced here: 68.4 us
  starting transfers between devices  31.1 us (45%)
  Pallas kernels  20.9 us (30%)
  waiting for transfers between devices  14.6 us (21%)
  local copies, waits for them, and re-layouts  0.86 us (1%)
  between operations  0.86 us (1%)
    ppermute x15, starting transfers between devices, swap(): return lax.ppermute(value, axis, [(i, i ^ bit) for i in range(count)])  23 us
    pallas_call x11, Pallas kernels, call(): pl.pallas_call(lambda *refs: kernel(*refs[:read], *refs[read + len(after)...  20.9 us
    ppermute x15, waiting for transfers between devices, swap(): return lax.ppermute(value, axis, [(i, i ^ bit) for i in range(count)])  14.2 us
    ppermute x3, starting transfers between devices, cross(): return lax.ppermute(value, BOTH, pairs)  4.47 us
    ppermute x1, starting transfers between devices, shards(): pair_late = lax.ppermute(pair_sent, BOTH, pairs)  2.24 us
  transfers between devices with their start and end apart: 22, of which 11 were waited for; matrix products, arithmetic and copies ran while one was open for 1% of the time, Pallas kernels for 26%

profile of v5, /device:TPU:0, one launch (start us, length us, event | category | flops | bytes accessed | tf_op | source)
XLA Modules:
  0.0 68.4 jit_solution(478719833120334697)
XLA Ops:
  0.7 2.3 %shard_map.129 = (bf16[128,2048]{1,0:T(8,128)(2,1)}, bf16[1,128,128]{2,1,0:T(8,128)(2,1)}) custom-call(bf16[128,4096]{1,0:T(8,128)(2,1)} %refs_0_.7, bf16[128,4096]{1,0:T(8,128)(2,1)} %refs_2_.11, bf16[128,4096]{1,0:T(8,128)(2,1)} %refs_3_.11, bf16[128,4096]{1,0:T(8,128)(2,1)} %refs_4_.3, f32[512,128]{1,0:T(8,128)} %refs_4_.2), custom_call_target="tpu_custom_call" | custom-call | flops 1 | bytes 1 | tf_op jit(solution)/shard_map/pallas_call | solution.py:401
  3.0 3.0 %collective-permute-start = (bf16[1,128,128]{2,1,0:T(8,128)(2,1)}, bf16[1,128,128]{2,1,0:T(8,128)(2,1)S(1)}, u32[]{:S(2)}, u32[]{:S(2)}) collective-permute-start(bf16[1,128,128]{2,1,0:T(8,128)(2,1)} %get-tuple-element.39), channel_id=1, source_target_pairs={{0,1},{1,0},{2,3},{3,2},{4,5},{5,4},{6,7},{7,6},{8,9},{9,8},{10,11... | collective-permute-start | bytes 98312 | tf_op jit(solution)/shard_map/ppermute | solution.py:356
  6.1 0.8 %constant_dynamic-update-slice_fusion.1 = (bf16[2,128,128]{2,1,0:T(8,128)(2,1)S(1)}, bf16[8,128,128]{2,1,0:T(8,128)(2,1)S(1)}) fusion(bf16[1,128,128]{2,1,0:T(8,128)(2,1)} %get-tuple-element.39), kind=kLoop, calls=%fused_computation.1 | loop fusion | bytes 98304
  6.8 1.3 %collective-permute-done = bf16[1,128,128]{2,1,0:T(8,128)(2,1)S(1)} collective-permute-done((bf16[1,128,128]{2,1,0:T(8,128)(2,1)}, bf16[1,128,128]{2,1,0:T(8,128)(2,1)S(1)}, u32[]{:S(2)}, u32[]{:S(2)}) %collective-permute-start) | collective-permute-done | bytes 32800 | tf_op jit(solution)/shard_map/ppermute | solution.py:356
  8.1 2.4 %collective-permute-start.1 = (bf16[2,128,128]{2,1,0:T(8,128)(2,1)S(1)}, bf16[2,128,128]{2,1,0:T(8,128)(2,1)S(1)}, u32[]{:S(2)}, u32[]{:S(2)}) collective-permute-start(bf16[2,128,128]{2,1,0:T(8,128)(2,1)S(1)} %get-tuple-element.74), channel_id=1, source_target_pairs={{0,2},{1,3},{2,0},{3,1},{4,6},{5,7},{6,4},{7,5},{8,10},{9,11},{10,... | collective-permute-start | bytes 196616 | tf_op jit(solution)/shard_map/ppermute | solution.py:356
  10.5 2.6 %collective-permute-start.2 = (bf16[2,128,128]{2,1,0:T(8,128)(2,1)S(1)}, bf16[2,128,128]{2,1,0:T(8,128)(2,1)S(1)}, u32[]{:S(2)}, u32[]{:S(2)}) collective-permute-start(bf16[2,128,128]{2,1,0:T(8,128)(2,1)S(1)} %get-tuple-element.74), channel_id=1, source_target_pairs={{0,4},{1,5},{2,6},{3,7},{4,0},{5,1},{6,2},{7,3},{8,12},{9,13},{10,... | collective-permute-start | bytes 196616 | tf_op jit(solution)/shard_map/ppermute | solution.py:356
  13.4 3.7 %collective-permute-done.2 = bf16[2,128,128]{2,1,0:T(8,128)(2,1)S(1)} collective-permute-done((bf16[2,128,128]{2,1,0:T(8,128)(2,1)S(1)}, bf16[2,128,128]{2,1,0:T(8,128)(2,1)S(1)}, u32[]{:S(2)}, u32[]{:S(2)}) %collective-permute-start.2) | collective-permute-done | bytes 65568 | tf_op jit(solution)/shard_map/ppermute | solution.py:356
  17.1 2.1 %collective-permute-done.3 = bf16[2,128,128]{2,1,0:T(8,128)(2,1)S(1)} collective-permute-done((bf16[2,128,128]{2,1,0:T(8,128)(2,1)S(1)}, bf16[2,128,128]{2,1,0:T(8,128)(2,1)S(1)}, u32[]{:S(2)}, u32[]{:S(2)}) %collective-permute-start.3) | collective-permute-done | bytes 65568 | tf_op jit(solution)/shard_map/ppermute | solution.py:356
  20.5 5.3 %collective-permute-start.8 = (bf16[8,128,128]{2,1,0:T(8,128)(2,1)S(1)}, bf16[8,128,128]{2,1,0:T(8,128)(2,1)S(1)}, u32[]{:S(2)}, u32[]{:S(2)}) collective-permute-start(bf16[8,128,128]{2,1,0:T(8,128)(2,1)S(1)} %constant_dynamic-update-slice_fusion.2.refs_4_.refs_8_), channel_id=1, source_target_pairs={{0,16},{8,24},{16,0},{24,8},{1,17},{9,25},{17,1},{25,9},{2,18},{10... | collective-permute-start | bytes 786440 | tf_op jit(solution)/shard_map/ppermute | solution.py:356
  27.2 4.7 %shard_map.132 = (f32[128,4096]{1,0:T(8,128)S(1)}, f32[256,4096]{1,0:T(8,128)S(1)}, f32[256,4096]{1,0:T(8,128)S(1)}, f32[256,4096]{1,0:T(8,128)S(1)}, f32[256,4096]{1,0:T(8,128)S(1)}) custom-call(bf16[128,4096]{1,0:T(8,128)(2,1)S(1)} %copy-done.3, bf16[128,4096]{1,0:T(8,128)(2,1)S(1)} %copy-done, bf16[128,4096]{1,0:T(8,128)(2,1)S(1)} %copy-done.1, ...), custom_call_target="tpu_custom_call" | custom-call | flops 1 | bytes 1 | tf_op jit(solution)/shard_map/pallas_call | solution.py:401
  31.9 3.0 %shard_map.133 = (f32[8,64,512]{2,1,0:T(8,128)S(1)}, bf16[128,4096]{1,0:T(8,128)(2,1)S(1)}, bf16[2,64,512]{2,1,0:T(8,128)(2,1)S(1)}, bf16[2,64,512]{2,1,0:T(8,12...) custom-call(bf16[128,2048]{1,0:T(8,128)(2,1)S(1)} %collective-permute-done.4.refs_5_.refs_0_, ...), custom_call_target="tpu_custom_call" | custom-call | flops 1 | bytes 1 | tf_op jit(solution)/shard_map/pallas_call | solution.py:401
  35.0 5.0 %collective-permute-start.11 = (bf16[2,64,512]{2,1,0:T(8,128)(2,1)S(1)}, bf16[2,64,512]{2,1,0:T(8,128)(2,1)S(1)}, u32[]{:S(2)}, u32[]{:S(2)}) collective-permute-start(bf16[2,64,512]{2,1,0:T(8,128)(2,1)S(1)} %get-tuple-element.50.refs_17_), channel_id=1, source_target_pairs={{0,8},{8,0},{16,24},{24,16},{1,9},{9,1},{17,25},{25,17},{2,10},{10... | collective-permute-start | bytes 393224 | tf_op jit(solution)/shard_map/ppermute | solution.py:356
  40.0 2.2 %collective-permute-start.5 = (bf16[128,2048]{1,0:T(8,128)(2,1)S(1)}, bf16[128,2048]{1,0:T(8,128)(2,1)S(1)}, u32[]{:S(2)}, u32[]{:S(2)}) collective-permute-start(bf16[128,2048]{1,0:T(8,128)(2,1)S(1)} %get-tuple-element.41), channel_id=1, source_target_pairs={{0,1},{1,0},{2,3},{3,2},{4,5},{5,4},{6,7},{7,6},{8,9},{9,8},{10,11... | collective-permute-start | bytes 1572872 | tf_op jit(solution)/shard_map/ppermute | solution.py:445
  42.9 0.8 %collective-permute-done.13.refs_3_ = bf16[2,64,512]{2,1,0:T(8,128)(2,1)S(1)} collective-permute-done((bf16[2,64,512]{2,1,0:T(8,128)(2,1)S(1)}, bf16[2,64,512]{2,1,0:T(8,128)(2,1)S(1)}, u32[]{:S(2)}, u32[]{:S(2)}) %collective-permute-start.13) | collective-permute-done | bytes 131104 | tf_op jit(solution)/shard_map/ppermute | solution.py:356
  43.8 1.2 %collective-permute-done.14.refs_4_ = bf16[2,64,512]{2,1,0:T(8,128)(2,1)S(1)} collective-permute-done((bf16[2,64,512]{2,1,0:T(8,128)(2,1)S(1)}, bf16[2,64,512]{2,1,0:T(8,128)(2,1)S(1)}, u32[]{:S(2)}, u32[]{:S(2)}) %collective-permute-start.14) | collective-permute-done | bytes 131104 | tf_op jit(solution)/shard_map/ppermute | solution.py:356
  45.1 2.4 %collective-permute-start.15 = (bf16[2,64,512]{2,1,0:T(8,128)(2,1)S(1)}, bf16[2,64,512]{2,1,0:T(8,128)(2,1)S(1)}, u32[]{:S(2)}, u32[]{:S(2)}) collective-permute-start(bf16[2,64,512]{2,1,0:T(8,128)(2,1)S(1)} %get-tuple-element.65), channel_id=1, source_target_pairs={{0,4},{1,5},{2,6},{3,7},{4,0},{5,1},{6,2},{7,3},{8,12},{9,13},{10,... | collective-permute-start | bytes 393224 | tf_op jit(solution)/shard_map/ppermute | solution.py:356
  47.4 1.4 %collective-permute-start.16 = (bf16[2,64,512]{2,1,0:T(8,128)(2,1)S(1)}, bf16[2,64,512]{2,1,0:T(8,128)(2,1)S(1)}, u32[]{:S(2)}, u32[]{:S(2)}) collective-permute-start(bf16[2,64,512]{2,1,0:T(8,128)(2,1)S(1)} %get-tuple-element.66), channel_id=1, source_target_pairs={{0,6},{1,7},{2,4},{3,5},{4,2},{5,3},{6,0},{7,1},{8,14},{9,15},{10,... | collective-permute-start | bytes 393224 | tf_op jit(solution)/shard_map/ppermute | solution.py:356
  48.8 6.2 %shard_map.134 = (f32[256,4096]{1,0:T(8,128)S(1)}, f32[128,2048]{1,0:T(8,128)S(1)}, f32[128,2048]{1,0:T(8,128)S(1)}, bf16[128,2048]{1,0:T(8,128)(2,1)S(1)}, bf16...) custom-call(bf16[128,4096]{1,0:T(8,128)(2,1)S(1)} %get-tuple-element.48.refs_0_, bf16[128,4096]{1,0:T(8,128)(2,1)S(1)} %copy-done, ...), custom_call_target="tpu_custom_call" | custom-call | flops 1 | bytes 1 | tf_op jit(solution)/shard_map/pallas_call | solution.py:401
  55.0 3.0 %collective-permute-done.15.refs_1_ = bf16[2,64,512]{2,1,0:T(8,128)(2,1)S(1)} collective-permute-done((bf16[2,64,512]{2,1,0:T(8,128)(2,1)S(1)}, bf16[2,64,512]{2,1,0:T(8,128)(2,1)S(1)}, u32[]{:S(2)}, u32[]{:S(2)}) %collective-permute-start.15) | collective-permute-done | bytes 131104 | tf_op jit(solution)/shard_map/ppermute | solution.py:356
  58.6 3.2 %collective-permute-start.18 = (bf16[64,512]{1,0:T(8,128)(2,1)S(1)}, bf16[64,512]{1,0:T(8,128)(2,1)S(1)}, u32[]{:S(2)}, u32[]{:S(2)}) collective-permute-start(bf16[64,512]{1,0:T(8,128)(2,1)S(1)} %get-tuple-element.69), channel_id=1, source_target_pairs={{0,17},{1,16},{2,19},{3,18},{4,21},{5,20},{6,23},{7,22},{8,25},{9,... | collective-permute-start | bytes 196616 | tf_op jit(solution)/shard_map/ppermute | solution.py:362
  61.8 1.3 %collective-permute-start.20 = (bf16[64,512]{1,0:T(8,128)(2,1)S(1)}, bf16[64,512]{1,0:T(8,128)(2,1)S(1)}, u32[]{:S(2)}, u32[]{:S(2)}) collective-permute-start(bf16[64,512]{1,0:T(8,128)(2,1)S(1)} %get-tuple-element.69), channel_id=1, source_target_pairs={{0,1},{1,0},{2,3},{3,2},{4,5},{5,4},{6,7},{7,6},{8,9},{9,8},{10,11... | collective-permute-start | bytes 196616 | tf_op jit(solution)/shard_map/ppermute | solution.py:362
  63.1 2.9 %shard_map.135 = (bf16[128,4096]{1,0:T(8,128)(2,1)}, bf16[128,4096]{1,0:T(8,128)(2,1)}, bf16[128,4096]{1,0:T(8,128)(2,1)}, f32[8,128]{1,0:T(8,128)S(1)}) custom-call(bf16[128,2048]{1,0:T(8,128)(2,1)S(1)} %collective-permute-done.5.refs_0_, bf16[128,2048]{1,0:T(8,128)(2,1)S(1)} %collective-permute-done.6.refs_18_.refs_1_, bf16[128,4096]{1,0:T(8,128)(2,1)S(1)} %copy-done, ...), custom_call_target="tpu_custom_call" | custom-call | flops 1 | bytes 1 | tf_op jit(solution)/shard_map/pallas_call | solution.py:401
  66.2 1.3 %collective-permute-done.21.refs_1_ = f32[64,512]{1,0:T(8,128)S(1)} collective-permute-done((f32[64,512]{1,0:T(8,128)S(1)}, f32[64,512]{1,0:T(8,128)S(1)}, u32[]{:S(2)}, u32[]{:S(2)}) %collective-permute-start.21) | collective-permute-done | bytes 131104 | tf_op jit(solution)/shard_map/ppermute | solution.py:356
  67.6 0.8 %shard_map.139 = f32[512,128]{1,0:T(8,128)} custom-call(f32[64,512]{1,0:T(8,128)S(1)} %get-tuple-element.72.refs_0_, f32[64,512]{1,0:T(8,128)S(1)} %collective-permute-done.21.refs_1_), custom_call_target="tpu_custom_call" | custom-call | flops 1 | bytes 1 | tf_op jit(solution)/shard_map/pallas_call | solution.py:401
  (54 shorter events, 4.7 us)
Async XLA Ops:
  0.6 18.9 %copy-start.3 = (bf16[128,4096]{1,0:T(8,128)(2,1)S(1)}, bf16[128,4096]{1,0:T(8,128)(2,1)}, u32[]{:S(2)}) copy-start(bf16[128,4096]{1,0:T(8,128)(2,1)} %refs_0_.7) | copy-start | bytes 3145732
  0.7 25.1 %copy-start.8 = (s32[4096]{0:T(1024)S(1)}, s32[4096]{0:T(1024)}, u32[]{:S(2)}) copy-start(s32[4096]{0:T(1024)} %param.15) | copy-start | bytes 49156
  3.0 5.1 %collective-permute-start = (bf16[1,128,128]{2,1,0:T(8,128)(2,1)}, bf16[1,128,128]{2,1,0:T(8,128)(2,1)S(1)}, u32[]{:S(2)}, u32[]{:S(2)}) collective-permute-start(bf16[1,128,128]{2,1,0:T(8,128)(2,1)} %get-tuple-element.39), channel_id=1, source_target_pairs={{0,1},{1,0},{2,3},{3,2},{4,5},{5,4},{6,7},{7,6},{8,9},{9,8},{10,11... | collective-permute-start | bytes 98312 | tf_op jit(solution)/shard_map/ppermute | solution.py:356
  6.0 13.6 %collective-permute-start.4 = (bf16[128,2048]{1,0:T(8,128)(2,1)}, bf16[128,2048]{1,0:T(8,128)(2,1)S(1)}, u32[]{:S(2)}, u32[]{:S(2)}) collective-permute-start(bf16[128,2048]{1,0:T(8,128)(2,1)} %get-tuple-element.40), channel_id=1, source_target_pairs={{0,1},{1,0},{2,3},{3,2},{4,5},{5,4},{6,7},{7,6},{8,9},{9,8},{10,11... | collective-permute-start | bytes 1572872 | tf_op jit(solution)/shard_map/ppermute | solution.py:434
  8.1 5.3 %collective-permute-start.1 = (bf16[2,128,128]{2,1,0:T(8,128)(2,1)S(1)}, bf16[2,128,128]{2,1,0:T(8,128)(2,1)S(1)}, u32[]{:S(2)}, u32[]{:S(2)}) collective-permute-start(bf16[2,128,128]{2,1,0:T(8,128)(2,1)S(1)} %get-tuple-element.74), channel_id=1, source_target_pairs={{0,2},{1,3},{2,0},{3,1},{4,6},{5,7},{6,4},{7,5},{8,10},{9,11},{10,... | collective-permute-start | bytes 196616 | tf_op jit(solution)/shard_map/ppermute | solution.py:356
  10.5 6.6 %collective-permute-start.2 = (bf16[2,128,128]{2,1,0:T(8,128)(2,1)S(1)}, bf16[2,128,128]{2,1,0:T(8,128)(2,1)S(1)}, u32[]{:S(2)}, u32[]{:S(2)}) collective-permute-start(bf16[2,128,128]{2,1,0:T(8,128)(2,1)S(1)} %get-tuple-element.74), channel_id=1, source_target_pairs={{0,4},{1,5},{2,6},{3,7},{4,0},{5,1},{6,2},{7,3},{8,12},{9,13},{10,... | collective-permute-start | bytes 196616 | tf_op jit(solution)/shard_map/ppermute | solution.py:356
  13.1 6.1 %collective-permute-start.3 = (bf16[2,128,128]{2,1,0:T(8,128)(2,1)S(1)}, bf16[2,128,128]{2,1,0:T(8,128)(2,1)S(1)}, u32[]{:S(2)}, u32[]{:S(2)}) collective-permute-start(bf16[2,128,128]{2,1,0:T(8,128)(2,1)S(1)} %get-tuple-element.74), channel_id=1, source_target_pairs={{0,6},{1,7},{2,4},{3,5},{4,2},{5,3},{6,0},{7,1},{8,14},{9,15},{10,... | collective-permute-start | bytes 196616 | tf_op jit(solution)/shard_map/ppermute | solution.py:356
  19.8 12.2 %collective-permute-start.7 = (bf16[128,2048]{1,0:T(8,128)(2,1)S(1)}, bf16[128,2048]{1,0:T(8,128)(2,1)S(1)}, u32[]{:S(2)}, u32[]{:S(2)}) collective-permute-start(bf16[128,2048]{1,0:T(8,128)(2,1)S(1)} %shard_map.130.refs_5_), channel_id=1, source_target_pairs={{1,2},{2,1},{3,4},{4,3},{5,6},{6,5},{7,8},{8,7},{9,10},{10,9},{11,... | collective-permute-start | bytes 1572872 | tf_op jit(solution)/shard_map/ppermute | solution.py:437
  20.5 21.8 %collective-permute-start.8 = (bf16[8,128,128]{2,1,0:T(8,128)(2,1)S(1)}, bf16[8,128,128]{2,1,0:T(8,128)(2,1)S(1)}, u32[]{:S(2)}, u32[]{:S(2)}) collective-permute-start(bf16[8,128,128]{2,1,0:T(8,128)(2,1)S(1)} %constant_dynamic-update-slice_fusion.2.refs_4_.refs_8_), channel_id=1, source_target_pairs={{0,16},{8,24},{16,0},{24,8},{1,17},{9,25},{17,1},{25,9},{2,18},{10... | collective-permute-start | bytes 786440 | tf_op jit(solution)/shard_map/ppermute | solution.py:356
  26.4 22.4 %collective-permute-start.6 = (bf16[128,2048]{1,0:T(8,128)(2,1)S(1)}, bf16[128,2048]{1,0:T(8,128)(2,1)S(1)}, u32[]{:S(2)}, u32[]{:S(2)}) collective-permute-start(bf16[128,2048]{1,0:T(8,128)(2,1)S(1)} %get-tuple-element.42), channel_id=1, source_target_pairs={{1,2},{2,1},{3,4},{4,3},{5,6},{6,5},{7,8},{8,7},{9,10},{10,9},{11,... | collective-permute-start | bytes 1572872 | tf_op jit(solution)/shard_map/ppermute | solution.py:444
  35.0 7.3 %collective-permute-start.11 = (bf16[2,64,512]{2,1,0:T(8,128)(2,1)S(1)}, bf16[2,64,512]{2,1,0:T(8,128)(2,1)S(1)}, u32[]{:S(2)}, u32[]{:S(2)}) collective-permute-start(bf16[2,64,512]{2,1,0:T(8,128)(2,1)S(1)} %get-tuple-element.50.refs_17_), channel_id=1, source_target_pairs={{0,8},{8,0},{16,24},{24,16},{1,9},{9,1},{17,25},{25,17},{2,10},{10... | collective-permute-start | bytes 393224 | tf_op jit(solution)/shard_map/ppermute | solution.py:356
  40.0 2.8 %collective-permute-start.12 = (bf16[2,64,512]{2,1,0:T(8,128)(2,1)S(1)}, bf16[2,64,512]{2,1,0:T(8,128)(2,1)S(1)}, u32[]{:S(2)}, u32[]{:S(2)}) collective-permute-start(bf16[2,64,512]{2,1,0:T(8,128)(2,1)S(1)} %get-tuple-element.61), channel_id=1, source_target_pairs={{0,8},{8,0},{16,24},{24,16},{1,9},{9,1},{17,25},{25,17},{2,10},{10... | collective-permute-start | bytes 393224 | tf_op jit(solution)/shard_map/ppermute | solution.py:356
  40.0 23.1 %collective-permute-start.5 = (bf16[128,2048]{1,0:T(8,128)(2,1)S(1)}, bf16[128,2048]{1,0:T(8,128)(2,1)S(1)}, u32[]{:S(2)}, u32[]{:S(2)}) collective-permute-start(bf16[128,2048]{1,0:T(8,128)(2,1)S(1)} %get-tuple-element.41), channel_id=1, source_target_pairs={{0,1},{1,0},{2,3},{3,2},{4,5},{5,4},{6,7},{7,6},{8,9},{9,8},{10,11... | collective-permute-start | bytes 1572872 | tf_op jit(solution)/shard_map/ppermute | solution.py:445
  42.3 1.3 %collective-permute-start.13 = (bf16[2,64,512]{2,1,0:T(8,128)(2,1)S(1)}, bf16[2,64,512]{2,1,0:T(8,128)(2,1)S(1)}, u32[]{:S(2)}, u32[]{:S(2)}) collective-permute-start(bf16[2,64,512]{2,1,0:T(8,128)(2,1)S(1)} %get-tuple-element.62), channel_id=1, source_target_pairs={{0,8},{8,0},{16,24},{24,16},{1,9},{9,1},{17,25},{25,17},{2,10},{10... | collective-permute-start | bytes 393224 | tf_op jit(solution)/shard_map/ppermute | solution.py:356
  42.3 5.1 %collective-permute-start.9 = (bf16[8,128,128]{2,1,0:T(8,128)(2,1)S(1)}, bf16[8,128,128]{2,1,0:T(8,128)(2,1)S(1)}, u32[]{:S(2)}, u32[]{:S(2)}) collective-permute-start(bf16[8,128,128]{2,1,0:T(8,128)(2,1)S(1)} %constant_dynamic-update-slice_fusion.2.refs_4_.refs_8_), channel_id=1, source_target_pairs={{0,8},{8,0},{16,24},{24,16},{1,9},{9,1},{17,25},{25,17},{2,10},{10... | collective-permute-start | bytes 786440 | tf_op jit(solution)/shard_map/ppermute | solution.py:356
  42.8 6.0 %collective-permute-start.10 = (bf16[8,128,128]{2,1,0:T(8,128)(2,1)S(1)}, bf16[8,128,128]{2,1,0:T(8,128)(2,1)S(1)}, u32[]{:S(2)}, u32[]{:S(2)}) collective-permute-start(bf16[8,128,128]{2,1,0:T(8,128)(2,1)S(1)} %collective-permute-done.8.refs_9_), channel_id=1, source_target_pairs={{0,8},{8,0},{16,24},{24,16},{1,9},{9,1},{17,25},{25,17},{2,10},{10... | collective-permute-start | bytes 786440 | tf_op jit(solution)/shard_map/ppermute | solution.py:356
  43.6 1.3 %collective-permute-start.14 = (bf16[2,64,512]{2,1,0:T(8,128)(2,1)S(1)}, bf16[2,64,512]{2,1,0:T(8,128)(2,1)S(1)}, u32[]{:S(2)}, u32[]{:S(2)}) collective-permute-start(bf16[2,64,512]{2,1,0:T(8,128)(2,1)S(1)} %get-tuple-element.63), channel_id=1, source_target_pairs={{0,8},{8,0},{16,24},{24,16},{1,9},{9,1},{17,25},{25,17},{2,10},{10... | collective-permute-start | bytes 393224 | tf_op jit(solution)/shard_map/ppermute | solution.py:356
  45.1 13.0 %collective-permute-start.15 = (bf16[2,64,512]{2,1,0:T(8,128)(2,1)S(1)}, bf16[2,64,512]{2,1,0:T(8,128)(2,1)S(1)}, u32[]{:S(2)}, u32[]{:S(2)}) collective-permute-start(bf16[2,64,512]{2,1,0:T(8,128)(2,1)S(1)} %get-tuple-element.65), channel_id=1, source_target_pairs={{0,4},{1,5},{2,6},{3,7},{4,0},{5,1},{6,2},{7,3},{8,12},{9,13},{10,... | collective-permute-start | bytes 393224 | tf_op jit(solution)/shard_map/ppermute | solution.py:356
  47.4 10.6 %collective-permute-start.16 = (bf16[2,64,512]{2,1,0:T(8,128)(2,1)S(1)}, bf16[2,64,512]{2,1,0:T(8,128)(2,1)S(1)}, u32[]{:S(2)}, u32[]{:S(2)}) collective-permute-start(bf16[2,64,512]{2,1,0:T(8,128)(2,1)S(1)} %get-tuple-element.66), channel_id=1, source_target_pairs={{0,6},{1,7},{2,4},{3,5},{4,2},{5,3},{6,0},{7,1},{8,14},{9,15},{10,... | collective-permute-start | bytes 393224 | tf_op jit(solution)/shard_map/ppermute | solution.py:356
  48.8 9.8 %collective-permute-start.17 = (bf16[2,64,512]{2,1,0:T(8,128)(2,1)S(1)}, bf16[2,64,512]{2,1,0:T(8,128)(2,1)S(1)}, u32[]{:S(2)}, u32[]{:S(2)}) collective-permute-start(bf16[2,64,512]{2,1,0:T(8,128)(2,1)S(1)} %get-tuple-element.67), channel_id=1, source_target_pairs={{0,2},{1,3},{2,0},{3,1},{4,6},{5,7},{6,4},{7,5},{8,10},{9,11},{10,... | collective-permute-start | bytes 393224 | tf_op jit(solution)/shard_map/ppermute | solution.py:356
  58.6 7.4 %collective-permute-start.18 = (bf16[64,512]{1,0:T(8,128)(2,1)S(1)}, bf16[64,512]{1,0:T(8,128)(2,1)S(1)}, u32[]{:S(2)}, u32[]{:S(2)}) collective-permute-start(bf16[64,512]{1,0:T(8,128)(2,1)S(1)} %get-tuple-element.69), channel_id=1, source_target_pairs={{0,17},{1,16},{2,19},{3,18},{4,21},{5,20},{6,23},{7,22},{8,25},{9,... | collective-permute-start | bytes 196616 | tf_op jit(solution)/shard_map/ppermute | solution.py:362
  61.8 4.3 %collective-permute-start.19 = (bf16[64,512]{1,0:T(8,128)(2,1)S(1)}, bf16[64,512]{1,0:T(8,128)(2,1)S(1)}, u32[]{:S(2)}, u32[]{:S(2)}) collective-permute-start(bf16[64,512]{1,0:T(8,128)(2,1)S(1)} %get-tuple-element.70), channel_id=1, source_target_pairs={{0,16},{1,17},{2,18},{3,19},{4,20},{5,21},{6,22},{7,23},{8,24},{9,... | collective-permute-start | bytes 196616 | tf_op jit(solution)/shard_map/ppermute | solution.py:362
  61.8 4.3 %collective-permute-start.20 = (bf16[64,512]{1,0:T(8,128)(2,1)S(1)}, bf16[64,512]{1,0:T(8,128)(2,1)S(1)}, u32[]{:S(2)}, u32[]{:S(2)}) collective-permute-start(bf16[64,512]{1,0:T(8,128)(2,1)S(1)} %get-tuple-element.69), channel_id=1, source_target_pairs={{0,1},{1,0},{2,3},{3,2},{4,5},{5,4},{6,7},{7,6},{8,9},{9,8},{10,11... | collective-permute-start | bytes 196616 | tf_op jit(solution)/shard_map/ppermute | solution.py:362
  66.1 1.4 %collective-permute-start.21 = (f32[64,512]{1,0:T(8,128)S(1)}, f32[64,512]{1,0:T(8,128)S(1)}, u32[]{:S(2)}, u32[]{:S(2)}) collective-permute-start(f32[64,512]{1,0:T(8,128)S(1)} %get-tuple-element.73), channel_id=1, source_target_pairs={{0,8},{8,0},{16,24},{24,16},{1,9},{9,1},{17,25},{25,17},{2,10},{10... | collective-permute-start | bytes 393224 | tf_op jit(solution)/shard_map/ppermute | solution.py:356
  (7 other events, 84.9 us)

commit v6 on v5

--- a/solution.py
+++ b/solution.py
@@ -490,7 +490,7 @@
         after=(query_half,), out_specs=(vmem, streamed, streamed),
     )
     got = [
-        cross(high if j else low, d, j) for d in reversed(range(0, dp, 2)) for j in (1, 0) if d or j
+        cross(high if j else low, d, j) for j in (1, 0) for d in reversed(range(0, dp, 2)) if d or j
     ]
     total, total_sent = call(
         functools.partial(third_sum_kernel, 1 + len(got)),

time: 68.6 us -> 69.9 us (1.019)
  waiting for transfers between devices: 14.6 us -> 15.9 us
    ppermute x3, waiting for transfers between devices: 0.1 us -> 1.36 us  [cross(): return lax.ppermute(value, BOTH, pairs)]
  transfers between devices with their start and end apart: 22 -> 22, of which waited for: 11 -> 12; matrix products, arithmetic and copies ran while one was open for 1% -> 1% of each run, Pallas kernels for 26% -> 25%
where the time goes in v6:
time: 69.9 us; the launch traced here: 69.7 us
  starting transfers between devices  31.1 us (44%)
  Pallas kernels  20.9 us (30%)
  waiting for transfers between devices  15.9 us (23%)
  local copies, waits for them, and re-layouts  0.86 us (1%)
  between operations  0.86 us (1%)
    ppermute x15, starting transfers between devices, swap(): return lax.ppermute(value, axis, [(i, i ^ bit) for i in range(count)])  23 us
    pallas_call x11, Pallas kernels, call(): pl.pallas_call(lambda *refs: kernel(*refs[:read], *refs[read + len(after)...  20.9 us
    ppermute x15, waiting for transfers between devices, swap(): return lax.ppermute(value, axis, [(i, i ^ bit) for i in range(count)])  14.2 us
    ppermute x3, starting transfers between devices, cross(): return lax.ppermute(value, BOTH, pairs)  4.47 us
    ppermute x1, starting transfers between devices, shards(): pair_late = lax.ppermute(pair_sent, BOTH, pairs)  2.24 us
  transfers between devices with their start and end apart: 22, of which 12 were waited for; matrix products, arithmetic and copies ran while one was open for 1% of the time, Pallas kernels for 25%

profile of v6, /device:TPU:0, one launch (start us, length us, event | category | flops | bytes accessed | tf_op | source)
XLA Modules:
  0.0 69.7 jit_solution(2943081110671985317)
XLA Ops:
  0.7 2.3 %shard_map.129 = (bf16[128,2048]{1,0:T(8,128)(2,1)}, bf16[1,128,128]{2,1,0:T(8,128)(2,1)}) custom-call(bf16[128,4096]{1,0:T(8,128)(2,1)} %refs_0_.7, bf16[128,4096]{1,0:T(8,128)(2,1)} %refs_2_.11, bf16[128,4096]{1,0:T(8,128)(2,1)} %refs_3_.11, bf16[128,4096]{1,0:T(8,128)(2,1)} %refs_4_.3, f32[512,128]{1,0:T(8,128)} %refs_4_.2), custom_call_target="tpu_custom_call" | custom-call | flops 1 | bytes 1 | tf_op jit(solution)/shard_map/pallas_call | solution.py:401
  3.0 3.0 %collective-permute-start = (bf16[1,128,128]{2,1,0:T(8,128)(2,1)}, bf16[1,128,128]{2,1,0:T(8,128)(2,1)S(1)}, u32[]{:S(2)}, u32[]{:S(2)}) collective-permute-start(bf16[1,128,128]{2,1,0:T(8,128)(2,1)} %get-tuple-element.39), channel_id=1, source_target_pairs={{0,1},{1,0},{2,3},{3,2},{4,5},{5,4},{6,7},{7,6},{8,9},{9,8},{10,11... | collective-permute-start | bytes 98312 | tf_op jit(solution)/shard_map/ppermute | solution.py:356
  6.1 0.8 %constant_dynamic-update-slice_fusion.1 = (bf16[2,128,128]{2,1,0:T(8,128)(2,1)S(1)}, bf16[8,128,128]{2,1,0:T(8,128)(2,1)S(1)}) fusion(bf16[1,128,128]{2,1,0:T(8,128)(2,1)} %get-tuple-element.39), kind=kLoop, calls=%fused_computation.1 | loop fusion | bytes 98304
  6.8 1.3 %collective-permute-done = bf16[1,128,128]{2,1,0:T(8,128)(2,1)S(1)} collective-permute-done((bf16[1,128,128]{2,1,0:T(8,128)(2,1)}, bf16[1,128,128]{2,1,0:T(8,128)(2,1)S(1)}, u32[]{:S(2)}, u32[]{:S(2)}) %collective-permute-start) | collective-permute-done | bytes 32800 | tf_op jit(solution)/shard_map/ppermute | solution.py:356
  8.1 2.4 %collective-permute-start.1 = (bf16[2,128,128]{2,1,0:T(8,128)(2,1)S(1)}, bf16[2,128,128]{2,1,0:T(8,128)(2,1)S(1)}, u32[]{:S(2)}, u32[]{:S(2)}) collective-permute-start(bf16[2,128,128]{2,1,0:T(8,128)(2,1)S(1)} %get-tuple-element.74), channel_id=1, source_target_pairs={{0,2},{1,3},{2,0},{3,1},{4,6},{5,7},{6,4},{7,5},{8,10},{9,11},{10,... | collective-permute-start | bytes 196616 | tf_op jit(solution)/shard_map/ppermute | solution.py:356
  10.5 2.6 %collective-permute-start.2 = (bf16[2,128,128]{2,1,0:T(8,128)(2,1)S(1)}, bf16[2,128,128]{2,1,0:T(8,128)(2,1)S(1)}, u32[]{:S(2)}, u32[]{:S(2)}) collective-permute-start(bf16[2,128,128]{2,1,0:T(8,128)(2,1)S(1)} %get-tuple-element.74), channel_id=1, source_target_pairs={{0,4},{1,5},{2,6},{3,7},{4,0},{5,1},{6,2},{7,3},{8,12},{9,13},{10,... | collective-permute-start | bytes 196616 | tf_op jit(solution)/shard_map/ppermute | solution.py:356
  13.4 3.7 %collective-permute-done.2 = bf16[2,128,128]{2,1,0:T(8,128)(2,1)S(1)} collective-permute-done((bf16[2,128,128]{2,1,0:T(8,128)(2,1)S(1)}, bf16[2,128,128]{2,1,0:T(8,128)(2,1)S(1)}, u32[]{:S(2)}, u32[]{:S(2)}) %collective-permute-start.2) | collective-permute-done | bytes 65568 | tf_op jit(solution)/shard_map/ppermute | solution.py:356
  17.1 2.1 %collective-permute-done.3 = bf16[2,128,128]{2,1,0:T(8,128)(2,1)S(1)} collective-permute-done((bf16[2,128,128]{2,1,0:T(8,128)(2,1)S(1)}, bf16[2,128,128]{2,1,0:T(8,128)(2,1)S(1)}, u32[]{:S(2)}, u32[]{:S(2)}) %collective-permute-start.3) | collective-permute-done | bytes 65568 | tf_op jit(solution)/shard_map/ppermute | solution.py:356
  20.5 5.3 %collective-permute-start.8 = (bf16[8,128,128]{2,1,0:T(8,128)(2,1)S(1)}, bf16[8,128,128]{2,1,0:T(8,128)(2,1)S(1)}, u32[]{:S(2)}, u32[]{:S(2)}) collective-permute-start(bf16[8,128,128]{2,1,0:T(8,128)(2,1)S(1)} %constant_dynamic-update-slice_fusion.2.refs_4_.refs_8_), channel_id=1, source_target_pairs={{0,16},{8,24},{16,0},{24,8},{1,17},{9,25},{17,1},{25,9},{2,18},{10... | collective-permute-start | bytes 786440 | tf_op jit(solution)/shard_map/ppermute | solution.py:356
  27.2 4.7 %shard_map.132 = (f32[128,4096]{1,0:T(8,128)S(1)}, f32[256,4096]{1,0:T(8,128)S(1)}, f32[256,4096]{1,0:T(8,128)S(1)}, f32[256,4096]{1,0:T(8,128)S(1)}, f32[256,4096]{1,0:T(8,128)S(1)}) custom-call(bf16[128,4096]{1,0:T(8,128)(2,1)S(1)} %copy-done.3, bf16[128,4096]{1,0:T(8,128)(2,1)S(1)} %copy-done, bf16[128,4096]{1,0:T(8,128)(2,1)S(1)} %copy-done.1, ...), custom_call_target="tpu_custom_call" | custom-call | flops 1 | bytes 1 | tf_op jit(solution)/shard_map/pallas_call | solution.py:401
  31.9 3.0 %shard_map.133 = (f32[8,64,512]{2,1,0:T(8,128)S(1)}, bf16[128,4096]{1,0:T(8,128)(2,1)S(1)}, bf16[2,64,512]{2,1,0:T(8,128)(2,1)S(1)}, bf16[2,64,512]{2,1,0:T(8,12...) custom-call(bf16[128,2048]{1,0:T(8,128)(2,1)S(1)} %collective-permute-done.4.refs_5_.refs_0_, ...), custom_call_target="tpu_custom_call" | custom-call | flops 1 | bytes 1 | tf_op jit(solution)/shard_map/pallas_call | solution.py:401
  35.0 5.0 %collective-permute-start.11 = (bf16[2,64,512]{2,1,0:T(8,128)(2,1)S(1)}, bf16[2,64,512]{2,1,0:T(8,128)(2,1)S(1)}, u32[]{:S(2)}, u32[]{:S(2)}) collective-permute-start(bf16[2,64,512]{2,1,0:T(8,128)(2,1)S(1)} %get-tuple-element.50.refs_17_), channel_id=1, source_target_pairs={{0,8},{8,0},{16,24},{24,16},{1,9},{9,1},{17,25},{25,17},{2,10},{10... | collective-permute-start | bytes 393224 | tf_op jit(solution)/shard_map/ppermute | solution.py:356
  40.0 2.2 %collective-permute-start.5 = (bf16[128,2048]{1,0:T(8,128)(2,1)S(1)}, bf16[128,2048]{1,0:T(8,128)(2,1)S(1)}, u32[]{:S(2)}, u32[]{:S(2)}) collective-permute-start(bf16[128,2048]{1,0:T(8,128)(2,1)S(1)} %get-tuple-element.41), channel_id=1, source_target_pairs={{0,1},{1,0},{2,3},{3,2},{4,5},{5,4},{6,7},{7,6},{8,9},{9,8},{10,11... | collective-permute-start | bytes 1572872 | tf_op jit(solution)/shard_map/ppermute | solution.py:445
  43.8 1.2 %collective-permute-done.14.refs_4_ = bf16[2,64,512]{2,1,0:T(8,128)(2,1)S(1)} collective-permute-done((bf16[2,64,512]{2,1,0:T(8,128)(2,1)S(1)}, bf16[2,64,512]{2,1,0:T(8,128)(2,1)S(1)}, u32[]{:S(2)}, u32[]{:S(2)}) %collective-permute-start.14) | collective-permute-done | bytes 131104 | tf_op jit(solution)/shard_map/ppermute | solution.py:356
  45.1 2.4 %collective-permute-start.15 = (bf16[2,64,512]{2,1,0:T(8,128)(2,1)S(1)}, bf16[2,64,512]{2,1,0:T(8,128)(2,1)S(1)}, u32[]{:S(2)}, u32[]{:S(2)}) collective-permute-start(bf16[2,64,512]{2,1,0:T(8,128)(2,1)S(1)} %get-tuple-element.65), channel_id=1, source_target_pairs={{0,4},{1,5},{2,6},{3,7},{4,0},{5,1},{6,2},{7,3},{8,12},{9,13},{10,... | collective-permute-start | bytes 393224 | tf_op jit(solution)/shard_map/ppermute | solution.py:356
  47.4 1.4 %collective-permute-start.16 = (bf16[2,64,512]{2,1,0:T(8,128)(2,1)S(1)}, bf16[2,64,512]{2,1,0:T(8,128)(2,1)S(1)}, u32[]{:S(2)}, u32[]{:S(2)}) collective-permute-start(bf16[2,64,512]{2,1,0:T(8,128)(2,1)S(1)} %get-tuple-element.66), channel_id=1, source_target_pairs={{0,6},{1,7},{2,4},{3,5},{4,2},{5,3},{6,0},{7,1},{8,14},{9,15},{10,... | collective-permute-start | bytes 393224 | tf_op jit(solution)/shard_map/ppermute | solution.py:356
  48.8 6.2 %shard_map.134 = (f32[256,4096]{1,0:T(8,128)S(1)}, f32[128,2048]{1,0:T(8,128)S(1)}, f32[128,2048]{1,0:T(8,128)S(1)}, bf16[128,2048]{1,0:T(8,128)(2,1)S(1)}, bf16...) custom-call(bf16[128,4096]{1,0:T(8,128)(2,1)S(1)} %get-tuple-element.48.refs_0_, bf16[128,4096]{1,0:T(8,128)(2,1)S(1)} %copy-done, ...), custom_call_target="tpu_custom_call" | custom-call | flops 1 | bytes 1 | tf_op jit(solution)/shard_map/pallas_call | solution.py:401
  55.0 3.0 %collective-permute-done.15.refs_1_ = bf16[2,64,512]{2,1,0:T(8,128)(2,1)S(1)} collective-permute-done((bf16[2,64,512]{2,1,0:T(8,128)(2,1)S(1)}, bf16[2,64,512]{2,1,0:T(8,128)(2,1)S(1)}, u32[]{:S(2)}, u32[]{:S(2)}) %collective-permute-start.15) | collective-permute-done | bytes 131104 | tf_op jit(solution)/shard_map/ppermute | solution.py:356
  58.6 3.2 %collective-permute-start.18 = (bf16[64,512]{1,0:T(8,128)(2,1)S(1)}, bf16[64,512]{1,0:T(8,128)(2,1)S(1)}, u32[]{:S(2)}, u32[]{:S(2)}) collective-permute-start(bf16[64,512]{1,0:T(8,128)(2,1)S(1)} %get-tuple-element.69), channel_id=1, source_target_pairs={{0,17},{1,16},{2,19},{3,18},{4,21},{5,20},{6,23},{7,22},{8,25},{9,... | collective-permute-start | bytes 196616 | tf_op jit(solution)/shard_map/ppermute | solution.py:362
  61.8 1.3 %collective-permute-start.19 = (bf16[64,512]{1,0:T(8,128)(2,1)S(1)}, bf16[64,512]{1,0:T(8,128)(2,1)S(1)}, u32[]{:S(2)}, u32[]{:S(2)}) collective-permute-start(bf16[64,512]{1,0:T(8,128)(2,1)S(1)} %get-tuple-element.69), channel_id=1, source_target_pairs={{0,1},{1,0},{2,3},{3,2},{4,5},{5,4},{6,7},{7,6},{8,9},{9,8},{10,11... | collective-permute-start | bytes 196616 | tf_op jit(solution)/shard_map/ppermute | solution.py:362
  63.1 2.9 %shard_map.135 = (bf16[128,4096]{1,0:T(8,128)(2,1)}, bf16[128,4096]{1,0:T(8,128)(2,1)}, bf16[128,4096]{1,0:T(8,128)(2,1)}, f32[8,128]{1,0:T(8,128)S(1)}) custom-call(bf16[128,2048]{1,0:T(8,128)(2,1)S(1)} %collective-permute-done.5.refs_0_, bf16[128,2048]{1,0:T(8,128)(2,1)S(1)} %collective-permute-done.6.refs_18_.refs_1_, bf16[128,4096]{1,0:T(8,128)(2,1)S(1)} %copy-done, ...), custom_call_target="tpu_custom_call" | custom-call | flops 1 | bytes 1 | tf_op jit(solution)/shard_map/pallas_call | solution.py:401
  66.1 1.3 %collective-permute-done.20.refs_3_ = bf16[64,512]{1,0:T(8,128)(2,1)S(1)} collective-permute-done((bf16[64,512]{1,0:T(8,128)(2,1)S(1)}, bf16[64,512]{1,0:T(8,128)(2,1)S(1)}, u32[]{:S(2)}, u32[]{:S(2)}) %collective-permute-start.20) | collective-permute-done | bytes 65568 | tf_op jit(solution)/shard_map/ppermute | solution.py:362
  67.5 1.3 %collective-permute-done.21.refs_1_ = f32[64,512]{1,0:T(8,128)S(1)} collective-permute-done((f32[64,512]{1,0:T(8,128)S(1)}, f32[64,512]{1,0:T(8,128)S(1)}, u32[]{:S(2)}, u32[]{:S(2)}) %collective-permute-start.21) | collective-permute-done | bytes 131104 | tf_op jit(solution)/shard_map/ppermute | solution.py:356
  68.8 0.8 %shard_map.139 = f32[512,128]{1,0:T(8,128)} custom-call(f32[64,512]{1,0:T(8,128)S(1)} %get-tuple-element.72.refs_0_, f32[64,512]{1,0:T(8,128)S(1)} %collective-permute-done.21.refs_1_), custom_call_target="tpu_custom_call" | custom-call | flops 1 | bytes 1 | tf_op jit(solution)/shard_map/pallas_call | solution.py:401
  (54 shorter events, 5.4 us)
Async XLA Ops:
  0.6 18.9 %copy-start.3 = (bf16[128,4096]{1,0:T(8,128)(2,1)S(1)}, bf16[128,4096]{1,0:T(8,128)(2,1)}, u32[]{:S(2)}) copy-start(bf16[128,4096]{1,0:T(8,128)(2,1)} %refs_0_.7) | copy-start | bytes 3145732
  0.7 25.1 %copy-start.8 = (s32[4096]{0:T(1024)S(1)}, s32[4096]{0:T(1024)}, u32[]{:S(2)}) copy-start(s32[4096]{0:T(1024)} %param.15) | copy-start | bytes 49156
  3.0 5.1 %collective-permute-start = (bf16[1,128,128]{2,1,0:T(8,128)(2,1)}, bf16[1,128,128]{2,1,0:T(8,128)(2,1)S(1)}, u32[]{:S(2)}, u32[]{:S(2)}) collective-permute-start(bf16[1,128,128]{2,1,0:T(8,128)(2,1)} %get-tuple-element.39), channel_id=1, source_target_pairs={{0,1},{1,0},{2,3},{3,2},{4,5},{5,4},{6,7},{7,6},{8,9},{9,8},{10,11... | collective-permute-start | bytes 98312 | tf_op jit(solution)/shard_map/ppermute | solution.py:356
  6.0 13.6 %collective-permute-start.4 = (bf16[128,2048]{1,0:T(8,128)(2,1)}, bf16[128,2048]{1,0:T(8,128)(2,1)S(1)}, u32[]{:S(2)}, u32[]{:S(2)}) collective-permute-start(bf16[128,2048]{1,0:T(8,128)(2,1)} %get-tuple-element.40), channel_id=1, source_target_pairs={{0,1},{1,0},{2,3},{3,2},{4,5},{5,4},{6,7},{7,6},{8,9},{9,8},{10,11... | collective-permute-start | bytes 1572872 | tf_op jit(solution)/shard_map/ppermute | solution.py:434
  8.1 5.3 %collective-permute-start.1 = (bf16[2,128,128]{2,1,0:T(8,128)(2,1)S(1)}, bf16[2,128,128]{2,1,0:T(8,128)(2,1)S(1)}, u32[]{:S(2)}, u32[]{:S(2)}) collective-permute-start(bf16[2,128,128]{2,1,0:T(8,128)(2,1)S(1)} %get-tuple-element.74), channel_id=1, source_target_pairs={{0,2},{1,3},{2,0},{3,1},{4,6},{5,7},{6,4},{7,5},{8,10},{9,11},{10,... | collective-permute-start | bytes 196616 | tf_op jit(solution)/shard_map/ppermute | solution.py:356
  10.5 6.6 %collective-permute-start.2 = (bf16[2,128,128]{2,1,0:T(8,128)(2,1)S(1)}, bf16[2,128,128]{2,1,0:T(8,128)(2,1)S(1)}, u32[]{:S(2)}, u32[]{:S(2)}) collective-permute-start(bf16[2,128,128]{2,1,0:T(8,128)(2,1)S(1)} %get-tuple-element.74), channel_id=1, source_target_pairs={{0,4},{1,5},{2,6},{3,7},{4,0},{5,1},{6,2},{7,3},{8,12},{9,13},{10,... | collective-permute-start | bytes 196616 | tf_op jit(solution)/shard_map/ppermute | solution.py:356
  13.1 6.1 %collective-permute-start.3 = (bf16[2,128,128]{2,1,0:T(8,128)(2,1)S(1)}, bf16[2,128,128]{2,1,0:T(8,128)(2,1)S(1)}, u32[]{:S(2)}, u32[]{:S(2)}) collective-permute-start(bf16[2,128,128]{2,1,0:T(8,128)(2,1)S(1)} %get-tuple-element.74), channel_id=1, source_target_pairs={{0,6},{1,7},{2,4},{3,5},{4,2},{5,3},{6,0},{7,1},{8,14},{9,15},{10,... | collective-permute-start | bytes 196616 | tf_op jit(solution)/shard_map/ppermute | solution.py:356
  19.8 12.2 %collective-permute-start.7 = (bf16[128,2048]{1,0:T(8,128)(2,1)S(1)}, bf16[128,2048]{1,0:T(8,128)(2,1)S(1)}, u32[]{:S(2)}, u32[]{:S(2)}) collective-permute-start(bf16[128,2048]{1,0:T(8,128)(2,1)S(1)} %shard_map.130.refs_5_), channel_id=1, source_target_pairs={{1,2},{2,1},{3,4},{4,3},{5,6},{6,5},{7,8},{8,7},{9,10},{10,9},{11,... | collective-permute-start | bytes 1572872 | tf_op jit(solution)/shard_map/ppermute | solution.py:437
  20.5 21.8 %collective-permute-start.8 = (bf16[8,128,128]{2,1,0:T(8,128)(2,1)S(1)}, bf16[8,128,128]{2,1,0:T(8,128)(2,1)S(1)}, u32[]{:S(2)}, u32[]{:S(2)}) collective-permute-start(bf16[8,128,128]{2,1,0:T(8,128)(2,1)S(1)} %constant_dynamic-update-slice_fusion.2.refs_4_.refs_8_), channel_id=1, source_target_pairs={{0,16},{8,24},{16,0},{24,8},{1,17},{9,25},{17,1},{25,9},{2,18},{10... | collective-permute-start | bytes 786440 | tf_op jit(solution)/shard_map/ppermute | solution.py:356
  26.4 22.4 %collective-permute-start.6 = (bf16[128,2048]{1,0:T(8,128)(2,1)S(1)}, bf16[128,2048]{1,0:T(8,128)(2,1)S(1)}, u32[]{:S(2)}, u32[]{:S(2)}) collective-permute-start(bf16[128,2048]{1,0:T(8,128)(2,1)S(1)} %get-tuple-element.42), channel_id=1, source_target_pairs={{1,2},{2,1},{3,4},{4,3},{5,6},{6,5},{7,8},{8,7},{9,10},{10,9},{11,... | collective-permute-start | bytes 1572872 | tf_op jit(solution)/shard_map/ppermute | solution.py:444
  35.0 7.3 %collective-permute-start.11 = (bf16[2,64,512]{2,1,0:T(8,128)(2,1)S(1)}, bf16[2,64,512]{2,1,0:T(8,128)(2,1)S(1)}, u32[]{:S(2)}, u32[]{:S(2)}) collective-permute-start(bf16[2,64,512]{2,1,0:T(8,128)(2,1)S(1)} %get-tuple-element.50.refs_17_), channel_id=1, source_target_pairs={{0,8},{8,0},{16,24},{24,16},{1,9},{9,1},{17,25},{25,17},{2,10},{10... | collective-permute-start | bytes 393224 | tf_op jit(solution)/shard_map/ppermute | solution.py:356
  40.0 2.8 %collective-permute-start.12 = (bf16[2,64,512]{2,1,0:T(8,128)(2,1)S(1)}, bf16[2,64,512]{2,1,0:T(8,128)(2,1)S(1)}, u32[]{:S(2)}, u32[]{:S(2)}) collective-permute-start(bf16[2,64,512]{2,1,0:T(8,128)(2,1)S(1)} %get-tuple-element.61), channel_id=1, source_target_pairs={{0,8},{8,0},{16,24},{24,16},{1,9},{9,1},{17,25},{25,17},{2,10},{10... | collective-permute-start | bytes 393224 | tf_op jit(solution)/shard_map/ppermute | solution.py:356
  40.0 23.1 %collective-permute-start.5 = (bf16[128,2048]{1,0:T(8,128)(2,1)S(1)}, bf16[128,2048]{1,0:T(8,128)(2,1)S(1)}, u32[]{:S(2)}, u32[]{:S(2)}) collective-permute-start(bf16[128,2048]{1,0:T(8,128)(2,1)S(1)} %get-tuple-element.41), channel_id=1, source_target_pairs={{0,1},{1,0},{2,3},{3,2},{4,5},{5,4},{6,7},{7,6},{8,9},{9,8},{10,11... | collective-permute-start | bytes 1572872 | tf_op jit(solution)/shard_map/ppermute | solution.py:445
  42.3 1.3 %collective-permute-start.13 = (bf16[2,64,512]{2,1,0:T(8,128)(2,1)S(1)}, bf16[2,64,512]{2,1,0:T(8,128)(2,1)S(1)}, u32[]{:S(2)}, u32[]{:S(2)}) collective-permute-start(bf16[2,64,512]{2,1,0:T(8,128)(2,1)S(1)} %get-tuple-element.62), channel_id=1, source_target_pairs={{0,8},{8,0},{16,24},{24,16},{1,9},{9,1},{17,25},{25,17},{2,10},{10... | collective-permute-start | bytes 393224 | tf_op jit(solution)/shard_map/ppermute | solution.py:356
  42.3 5.1 %collective-permute-start.9 = (bf16[8,128,128]{2,1,0:T(8,128)(2,1)S(1)}, bf16[8,128,128]{2,1,0:T(8,128)(2,1)S(1)}, u32[]{:S(2)}, u32[]{:S(2)}) collective-permute-start(bf16[8,128,128]{2,1,0:T(8,128)(2,1)S(1)} %constant_dynamic-update-slice_fusion.2.refs_4_.refs_8_), channel_id=1, source_target_pairs={{0,8},{8,0},{16,24},{24,16},{1,9},{9,1},{17,25},{25,17},{2,10},{10... | collective-permute-start | bytes 786440 | tf_op jit(solution)/shard_map/ppermute | solution.py:356
  42.8 6.0 %collective-permute-start.10 = (bf16[8,128,128]{2,1,0:T(8,128)(2,1)S(1)}, bf16[8,128,128]{2,1,0:T(8,128)(2,1)S(1)}, u32[]{:S(2)}, u32[]{:S(2)}) collective-permute-start(bf16[8,128,128]{2,1,0:T(8,128)(2,1)S(1)} %collective-permute-done.8.refs_9_), channel_id=1, source_target_pairs={{0,8},{8,0},{16,24},{24,16},{1,9},{9,1},{17,25},{25,17},{2,10},{10... | collective-permute-start | bytes 786440 | tf_op jit(solution)/shard_map/ppermute | solution.py:356
  43.6 1.3 %collective-permute-start.14 = (bf16[2,64,512]{2,1,0:T(8,128)(2,1)S(1)}, bf16[2,64,512]{2,1,0:T(8,128)(2,1)S(1)}, u32[]{:S(2)}, u32[]{:S(2)}) collective-permute-start(bf16[2,64,512]{2,1,0:T(8,128)(2,1)S(1)} %get-tuple-element.63), channel_id=1, source_target_pairs={{0,8},{8,0},{16,24},{24,16},{1,9},{9,1},{17,25},{25,17},{2,10},{10... | collective-permute-start | bytes 393224 | tf_op jit(solution)/shard_map/ppermute | solution.py:356
  45.1 13.0 %collective-permute-start.15 = (bf16[2,64,512]{2,1,0:T(8,128)(2,1)S(1)}, bf16[2,64,512]{2,1,0:T(8,128)(2,1)S(1)}, u32[]{:S(2)}, u32[]{:S(2)}) collective-permute-start(bf16[2,64,512]{2,1,0:T(8,128)(2,1)S(1)} %get-tuple-element.65), channel_id=1, source_target_pairs={{0,4},{1,5},{2,6},{3,7},{4,0},{5,1},{6,2},{7,3},{8,12},{9,13},{10,... | collective-permute-start | bytes 393224 | tf_op jit(solution)/shard_map/ppermute | solution.py:356
  47.4 10.6 %collective-permute-start.16 = (bf16[2,64,512]{2,1,0:T(8,128)(2,1)S(1)}, bf16[2,64,512]{2,1,0:T(8,128)(2,1)S(1)}, u32[]{:S(2)}, u32[]{:S(2)}) collective-permute-start(bf16[2,64,512]{2,1,0:T(8,128)(2,1)S(1)} %get-tuple-element.66), channel_id=1, source_target_pairs={{0,6},{1,7},{2,4},{3,5},{4,2},{5,3},{6,0},{7,1},{8,14},{9,15},{10,... | collective-permute-start | bytes 393224 | tf_op jit(solution)/shard_map/ppermute | solution.py:356
  48.8 9.8 %collective-permute-start.17 = (bf16[2,64,512]{2,1,0:T(8,128)(2,1)S(1)}, bf16[2,64,512]{2,1,0:T(8,128)(2,1)S(1)}, u32[]{:S(2)}, u32[]{:S(2)}) collective-permute-start(bf16[2,64,512]{2,1,0:T(8,128)(2,1)S(1)} %get-tuple-element.67), channel_id=1, source_target_pairs={{0,2},{1,3},{2,0},{3,1},{4,6},{5,7},{6,4},{7,5},{8,10},{9,11},{10,... | collective-permute-start | bytes 393224 | tf_op jit(solution)/shard_map/ppermute | solution.py:356
  58.6 7.4 %collective-permute-start.18 = (bf16[64,512]{1,0:T(8,128)(2,1)S(1)}, bf16[64,512]{1,0:T(8,128)(2,1)S(1)}, u32[]{:S(2)}, u32[]{:S(2)}) collective-permute-start(bf16[64,512]{1,0:T(8,128)(2,1)S(1)} %get-tuple-element.69), channel_id=1, source_target_pairs={{0,17},{1,16},{2,19},{3,18},{4,21},{5,20},{6,23},{7,22},{8,25},{9,... | collective-permute-start | bytes 196616 | tf_op jit(solution)/shard_map/ppermute | solution.py:362
  61.8 4.3 %collective-permute-start.19 = (bf16[64,512]{1,0:T(8,128)(2,1)S(1)}, bf16[64,512]{1,0:T(8,128)(2,1)S(1)}, u32[]{:S(2)}, u32[]{:S(2)}) collective-permute-start(bf16[64,512]{1,0:T(8,128)(2,1)S(1)} %get-tuple-element.69), channel_id=1, source_target_pairs={{0,1},{1,0},{2,3},{3,2},{4,5},{5,4},{6,7},{7,6},{8,9},{9,8},{10,11... | collective-permute-start | bytes 196616 | tf_op jit(solution)/shard_map/ppermute | solution.py:362
  63.1 4.3 %collective-permute-start.20 = (bf16[64,512]{1,0:T(8,128)(2,1)S(1)}, bf16[64,512]{1,0:T(8,128)(2,1)S(1)}, u32[]{:S(2)}, u32[]{:S(2)}) collective-permute-start(bf16[64,512]{1,0:T(8,128)(2,1)S(1)} %get-tuple-element.70), channel_id=1, source_target_pairs={{0,16},{1,17},{2,18},{3,19},{4,20},{5,21},{6,22},{7,23},{8,24},{9,... | collective-permute-start | bytes 196616 | tf_op jit(solution)/shard_map/ppermute | solution.py:362
  67.4 1.4 %collective-permute-start.21 = (f32[64,512]{1,0:T(8,128)S(1)}, f32[64,512]{1,0:T(8,128)S(1)}, u32[]{:S(2)}, u32[]{:S(2)}) collective-permute-start(f32[64,512]{1,0:T(8,128)S(1)} %get-tuple-element.73), channel_id=1, source_target_pairs={{0,8},{8,0},{16,24},{24,16},{1,9},{9,1},{17,25},{25,17},{2,10},{10... | collective-permute-start | bytes 393224 | tf_op jit(solution)/shard_map/ppermute | solution.py:356
  (7 other events, 84.9 us)
